TPU v7x, 256 devices: a whole 4x4x8 slice. The times are simulated.
256 devices in a mesh: fsdp: 8 (over y, core), tp: 16 (over x_lo, z), rollout: 2 (over x_hi).
Axes of the slice: x: 4 (x_hi: 2, x_lo: 2; x = x_hi * 2 + x_lo), y: 4, z: 8, core: 2. Of those that a mesh axis runs over, the one named last changes fastest.
Arguments:
- weights: bfloat16 [2, 4096, 14336], P('rollout', 'fsdp', 'tp'), may hold values from -6 to 6
- gradient: bfloat16 [2, 4096, 14336], P('rollout', 'fsdp', 'tp'), may hold values from -6 to 6
- momentum: float32 [2, 4096, 14336], P('rollout', 'fsdp', 'tp'), may hold values from -90 to 90
- basis: float32 [2, 14336, 512], P('rollout', 'tp'), may hold values from -6 to 6
Outputs:
- weights_next: bfloat16 [2, 4096, 14336], P('rollout', 'fsdp', 'tp')
- momentum_next: float32 [2, 4096, 14336], P('rollout', 'fsdp', 'tp')
- basis_next: float32 [2, 14336, 512], P('rollout', 'tp')
- rollout_weights: bfloat16 [2, 4096, 14336], P(None, 'fsdp', 'tp')
All inputs are finite; a program needn't handle non-finite values.
Results may differ from a plain program's by a relative error of at most 0.013.
Values may be sent and summed in bfloat16 or wider, within the bound.
No kernel may reach another device: no remote copies, remote signals or barrier semaphores. Data moves between devices by JAX's collectives and lax.ppermute only.
A program may use at most 64 MiB of HBM per device.

v0:
```python
import jax
import jax.numpy as jnp
from jax import lax
from jax.sharding import Mesh
from jax.sharding import PartitionSpec as P

COLS = 14336
TP = ("tp_0", "tp_1")
FSDP = ("fsdp_0", "fsdp_1")


def in_blocks(x, dim, count):
    before, after = (x.shape[:dim], x.shape[dim + 1 :])
    return jnp.moveaxis(x.reshape(*before, count, -1, *after), dim, 0)


def sum_at_owner(x, axis, dim):
    count = lax.axis_size(axis)
    pieces = lax.all_to_all(in_blocks(x, dim, count), axis, 0, 0, tiled=True)
    return jnp.sum(pieces, axis=0)


def padded_to(lines, count):
    spare = -lines.shape[0] % count
    if not spare:
        return lines
    return jnp.concatenate([lines, jnp.zeros((spare, *lines.shape[1:]), lines.dtype)])


def copy_for_each(x, axis):
    count = lax.axis_size(axis)
    return lax.all_to_all(jnp.broadcast_to(x[None], (count, *x.shape)), axis, 0, 0, tiled=True)


def joined_along(pieces, dim):
    lengths = list(pieces.shape[1:])
    lengths[dim] *= pieces.shape[0]
    return jnp.moveaxis(pieces, 0, dim).reshape(lengths)


def gathered_by_axis(x, axes, dim):
    far, near = axes
    pieces = copy_for_each(copy_for_each(x, far), near)
    return joined_along(pieces.swapaxes(0, 1).reshape(-1, *x.shape), dim)


def sum_by_axis(x, axes, dim):
    far, near = axes
    own = sum_at_owner(in_blocks(x, dim, lax.axis_size(far)), near, dim + 1)
    return jnp.sum(lax.all_to_all(own, far, 0, 0, tiled=True), axis=0)


def sum_by_parts(x, axes):
    lines = x.reshape(-1, x.shape[-1])
    padded = padded_to(lines, lax.axis_size(axes[0]) * lax.axis_size(axes[1]))
    whole = gathered_by_axis(sum_by_axis(padded, axes, 0), axes, 0)
    return lax.slice_in_dim(whole, 0, len(lines)).reshape(x.shape)


def gather_directly(x, axis, dim):
    return joined_along(copy_for_each(x, axis), dim)


def sent_and_summed(x, axis, dim):
    pieces = in_blocks(x, dim, lax.axis_size(axis))
    arrived = lax.all_to_all(pieces, axis, split_axis=0, concat_axis=0, tiled=True)
    return arrived.astype(jnp.float32).sum(axis=0)


def taken_together(x, axis):
    return copy_for_each(x, axis).sum(axis=0)


def by_axis(x, axes):
    far, near = axes
    return taken_together(taken_together(x, near), far)


def body(weights, gradient, momentum, basis):
    blend = momentum[0] + gradient[0].astype(jnp.float32)
    prior = basis[0]
    block = blend
    share = sum_at_owner(jnp.dot(block, prior, preferred_element_type=jnp.float32), TP, 0)
    gram = sum_by_parts(
        jnp.dot(share.T, share, preferred_element_type=jnp.float32),
        (("fsdp_0", "fsdp_1"), ("tp_0", "tp_1")),
    )
    left = gather_directly(share, TP, 0)
    lower = jnp.linalg.cholesky(gram)
    ortho = lax.linalg.triangular_solve(lower, left, left_side=False, lower=True, transpose_a=True)
    block = blend
    right_share = sent_and_summed(
        jnp.dot(block.T, ortho, preferred_element_type=jnp.float32).astype(jnp.bfloat16), FSDP, 0
    )
    squares = by_axis(
        jnp.sum(right_share * right_share, axis=0), (("fsdp_0", "fsdp_1"), ("tp_0", "tp_1"))
    )
    meansq = squares / COLS
    basis_share = right_share * lax.rsqrt(meansq + 1e-06)
    basis_new = gathered_by_axis(basis_share, ("fsdp_0", "fsdp_1"), 0)
    norms = jnp.sqrt(meansq + 1e-06)
    moment_new = blend - 0.05 * jnp.dot(
        ortho * norms, basis_new.T, preferred_element_type=jnp.float32
    )
    update = jnp.dot(ortho, basis_new.T, preferred_element_type=jnp.float32)
    weight_new = (weights[0].astype(jnp.float32) - 0.3 * update).astype(jnp.bfloat16)[None]
    rollout_copy = gather_directly(weight_new, "rollout", 0)
    return (weight_new, moment_new[None], basis_new[None], rollout_copy)


def solution(mesh):
    finer = Mesh(
        mesh.devices.reshape(4, 2, 2, 8, mesh.shape["rollout"]),
        ("fsdp_0", "fsdp_1", "tp_0", "tp_1", "rollout"),
    )
    in_specs = (
        P("rollout", FSDP, TP),
        P("rollout", FSDP, TP),
        P("rollout", FSDP, TP),
        P("rollout", TP, None),
    )
    out_specs = (
        P("rollout", FSDP, TP),
        P("rollout", FSDP, TP),
        P("rollout", TP, None),
        P(None, FSDP, TP),
    )
    return jax.shard_map(body, mesh=finer, in_specs=in_specs, out_specs=out_specs, check_vma=False)
```

profile of v0, /device:TPU:1, one launch (start us, length us, event | category | flops | bytes accessed | tf_op | source)
XLA Modules:
  0.0 384.1 jit_solution(9065410563920115615)
XLA Ops:
  0.6 2.0 convert_add_fusion
  3.9 34.8 %all_to_all.62 = f32[16,32,512]{2,1,0:T(8,128)S(1)} all-to-all(f32[16,32,512]{2,1,0:T(8,128)S(1)} %fusion.53), channel_id=1, replica_groups=mesh['fsdp_0'=4,'fsdp_1'=2,'tp_0'=2,'tp_1'=8,'rollout'=2] {'tp_0','tp_1'}, dimensions={0} | all-to-all | bytes 2097152 | tf_op jit(solution)/shard_map/all_to_all | solution.py:19
  39.8 29.9 %all_to_all.63 = f32[16,8,4,512]{3,2,1,0:T(4,128)S(1)} all-to-all(f32[16,8,4,512]{3,2,1,0:T(4,128)S(1)} %copy.32), channel_id=1, replica_groups=mesh['fsdp_0'=4,'fsdp_1'=2,'tp_0'=2,'tp_1'=8,'rollout'=2] {'tp_0','tp_1'}, dimensions={0} | all-to-all | bytes 2097152 | tf_op jit(solution)/shard_map/all_to_all | solution.py:19
  69.9 12.3 %all_to_all.64 = f32[8,4,512]{2,1,0:T(4,128)S(1)} all-to-all(f32[8,4,512]{2,1,0:T(4,128)S(1)} %reduce_sum.64), channel_id=1, replica_groups=mesh['fsdp_0'=4,'fsdp_1'=2,'tp_0'=2,'tp_1'=8,'rollout'=2] {'fsdp_0','fsd..., dimensions={0} | all-to-all | bytes 131072 | tf_op jit(solution)/shard_map/all_to_all | solution.py:50
  82.2 8.0 %all_to_all.65 = f32[8,4,512]{2,1,0:T(4,128)S(1)} all-to-all(f32[8,4,512]{2,1,0:T(4,128)S(1)} %broadcast_in_dim.23), channel_id=1, replica_groups=mesh['fsdp_0'=4,'fsdp_1'=2,'tp_0'=2,'tp_1'=8,'rollout'=2] {'fsdp_0','fsd..., dimensions={0} | all-to-all | bytes 131072 | tf_op jit(solution)/shard_map/all_to_all | solution.py:32
  91.4 4.9 %all-to-all-start.5 = ((f32[16,8,4,512]{3,2,1,0:T(4,128)}), f32[16,8,4,512]{3,2,1,0:T(4,128)S(1)}, u32[]{:S(2)}, u32[]{:S(2)}) async-start(f32[16,8,4,512]{3,2,1,0:T(4,128)} %broadcast_in_dim.24), calls=%async_computation.5 | async-start | bytes 2097152 | tf_op jit(solution)/shard_map/all_to_all | solution.py:32
  96.3 25.6 %all-to-all-done.5 = f32[16,8,4,512]{3,2,1,0:T(4,128)S(1)} async-done(((f32[16,8,4,512]{3,2,1,0:T(4,128)}), f32[16,8,4,512]{3,2,1,0:T(4,128)S(1)}, u32[]{:S(2)}, u32[]{:S(2)}) %all-to-all-start.5) | async-done | bytes 1048608 | tf_op jit(solution)/shard_map/all_to_all | solution.py:32
  123.0 6.3 %all-to-all-start.1 = ((f32[16,32,512]{2,1,0:T(8,128)}), f32[16,32,512]{2,1,0:T(8,128)}, u32[]{:S(2)}, u32[]{:S(2)}) async-start(f32[16,32,512]{2,1,0:T(8,128)} %broadcast_in_dim.22), calls=%async_computation.1 | async-start | bytes 2097152 | tf_op jit(solution)/shard_map/all_to_all | solution.py:32
  135.7 11.7 %cholesky.104 = f32[128,128]{1,0:T(8,128)S(1)} custom-call(f32[128,128]{1,0:T(8,128)S(1)} %cholesky.266), custom_call_target="Cholesky" | custom-call | tf_op jit(solution)/shard_map/jit(cholesky)/cholesky | solution.py:89
  147.5 9.8 %custom-call.30 = f32[1,128,128]{1,2,0:T(8,128)S(1)} custom-call(f32[1,128,128]{2,1,0:T(8,128)S(1)} %get-tuple-element.31), custom_call_target="InvertDiagBlocksLowerTriangular" | custom-call | tf_op jit(solution)/shard_map/jit(cholesky)/cholesky | solution.py:89
  159.9 11.7 %cholesky.217 = f32[128,128]{1,0:T(8,128)S(1)} custom-call(f32[128,128]{1,0:T(8,128)S(1)} %cholesky.270), custom_call_target="Cholesky" | custom-call | tf_op jit(solution)/shard_map/jit(cholesky)/cholesky | solution.py:89
  171.6 10.0 %custom-call.31 = f32[1,128,128]{1,2,0:T(8,128)S(1)} custom-call(f32[1,128,128]{2,1,0:T(8,128)S(1)} %get-tuple-element.28), custom_call_target="InvertDiagBlocksLowerTriangular" | custom-call | tf_op jit(solution)/shard_map/jit(cholesky)/cholesky | solution.py:89
  183.2 11.7 %cholesky.238 = f32[128,128]{1,0:T(8,128)S(1)} custom-call(f32[128,128]{1,0:T(8,128)S(1)} %cholesky.275), custom_call_target="Cholesky" | custom-call | tf_op jit(solution)/shard_map/jit(cholesky)/cholesky | solution.py:89
  195.7 9.8 %custom-call.32 = f32[1,128,128]{1,2,0:T(8,128)S(1)} custom-call(f32[1,128,128]{2,1,0:T(8,128)S(1)} %get-tuple-element.25), custom_call_target="InvertDiagBlocksLowerTriangular" | custom-call | tf_op jit(solution)/shard_map/jit(cholesky)/cholesky | solution.py:89
  206.9 11.9 %cholesky.255 = f32[128,128]{1,0:T(8,128)S(1)} custom-call(f32[128,128]{1,0:T(8,128)S(1)} %convolution_subtract_fusion.5), custom_call_target="Cholesky" | custom-call | tf_op jit(solution)/shard_map/jit(cholesky)/cholesky | solution.py:89
  223.8 11.7 %while.1 = (s32[]{:T(128)}, f32[512,512]{1,0:T(8,128)}, s32[4,2]{0,1:T(2,128)S(1)}, f32[4,128,128]{2,1,0:T(8,128)S(1)}, s32[]{:T(128)}) while((s32[]{:T(128)}, f32[512,512]{1,0:T(8,128)}, s32[4,2]{0,1:T(2,128)S(1)}, f32[4,128,128]{2,1,0:T(8,128)S(1)}, s32[]{:T(128)}) %tuple.32), condition=%wide.while_cond, body=%wide.while_body.sunk | while | flops 2 | bytes 131189 | solution.py:90
  224.5 2.3 bitcast_dynamic-update-slice_fusion.2
  227.4 2.3 bitcast_dynamic-update-slice_fusion.2
  230.4 2.3 bitcast_dynamic-update-slice_fusion.2
  233.3 2.2 bitcast_dynamic-update-slice_fusion.2
  235.5 39.3 %custom-call.33 = f32[4,128,128]{1,2,0:T(8,128)S(1)} custom-call(f32[4,128,128]{2,1,0:T(8,128)S(1)} %get-tuple-element.11), custom_call_target="InvertDiagBlocksLowerTriangular" | custom-call | tf_op jit(solution)/shard_map/triangular_solve | solution.py:90
  278.3 2.1 convolution_subtract_fusion
  280.8 2.5 convolution_subtract_fusion.2
  284.5 17.0 %all_to_all.66 = bf16[8,112,512]{2,1,0:T(8,128)(2,1)S(1)} all-to-all(bf16[8,112,512]{2,1,0:T(8,128)(2,1)S(1)} %bitcast.121), channel_id=1, replica_groups=mesh['fsdp_0'=4,'fsdp_1'=2,'tp_0'=2,'tp_1'=8,'rollout'=2] {'fsdp_0','fsd..., dimensions={0} | all-to-all | bytes 1835008 | tf_op jit(solution)/shard_map/all_to_all | solution.py:66
  301.7 14.9 %all_to_all.67 = f32[16,1,512]{2,1,0:T(1,128)S(1)} all-to-all(f32[16,1,512]{2,1,0:T(1,128)S(1)} %broadcast_in_dim.25), channel_id=1, replica_groups=mesh['fsdp_0'=4,'fsdp_1'=2,'tp_0'=2,'tp_1'=8,'rollout'=2] {'tp_0','tp_1'}, dimensions={0} | all-to-all | bytes 65536 | tf_op jit(solution)/shard_map/all_to_all | solution.py:32
  316.6 9.3 %all_to_all.68 = f32[8,1,512]{2,1,0:T(1,128)S(1)} all-to-all(f32[8,1,512]{2,1,0:T(1,128)S(1)} %broadcast_in_dim.26), channel_id=1, replica_groups=mesh['fsdp_0'=4,'fsdp_1'=2,'tp_0'=2,'tp_1'=8,'rollout'=2] {'fsdp_0','fsd..., dimensions={0} | all-to-all | bytes 32768 | tf_op jit(solution)/shard_map/all_to_all | solution.py:32
  326.1 15.2 %all_to_all.69 = f32[4,112,512]{2,1,0:T(8,128)S(1)} all-to-all(f32[4,112,512]{2,1,0:T(8,128)S(1)} %broadcast_in_dim.27), channel_id=1, replica_groups=mesh['fsdp_0'=4,'fsdp_1'=2,'tp_0'=2,'tp_1'=8,'rollout'=2] {'fsdp_0'}, dimensions={0} | all-to-all | bytes 1835008 | tf_op jit(solution)/shard_map/all_to_all | solution.py:32
  341.5 6.7 %all_to_all.70 = f32[2,4,112,512]{3,2,1,0:T(8,128)S(1)} all-to-all(f32[2,4,112,512]{3,2,1,0:T(8,128)S(1)} %broadcast_in_dim.28), channel_id=1, replica_groups=mesh['fsdp_0'=4,'fsdp_1'=2,'tp_0'=2,'tp_1'=8,'rollout'=2] {'fsdp_1'}, dimensions={0} | all-to-all | bytes 3670016 | tf_op jit(solution)/shard_map/all_to_all | solution.py:32
  352.7 4.7 %all-to-all-start.11 = ((bf16[2,1,512,896]{3,2,1,0:T(8,128)(2,1)}), bf16[2,1,512,896]{3,2,1,0:T(8,128)(2,1)}, u32[]{:S(2)}, u32[]{:S(2)}) async-start(bf16[2,1,512,896]{3,2,1,0:T(8,128)(2,1)} %broadcast_in_dim.31), calls=%async_computation.11 | async-start | bytes 3670016 | tf_op jit(solution)/shard_map/all_to_all | solution.py:32
  357.5 4.2 %fusion.3 = f32[1,512,896]{2,1,0:T(8,128)} fusion(f32[1,512,896]{2,1,0:T(8,128)} %copy-done.1, f32[896,512]{1,0:T(8,128)} %bitcast.117, f32[512]{0:T(512)S(1)} %get-tuple-element.32, f32[512,128]{0,1:T(8,128)S(1)} %fusion.31, f32[512,128]{0,1:T(8,128)S(1)} %fusion.32, f32[512,128]{0,1:T(8,128)S(1)} %fusion.33, f32[512,128]{0,1:T(8,128)S(1)} %fusion.21), kind=kOutput, calls=%fused_computation.7 | convolution fusion | flops 471728128 | bytes 6555648 | tf_op jit(solution)/shard_map/dot_general | solution.py:102
  361.7 19.2 %all-to-all-done.11 = bf16[2,1,512,896]{3,2,1,0:T(8,128)(2,1)} async-done(((bf16[2,1,512,896]{3,2,1,0:T(8,128)(2,1)}), bf16[2,1,512,896]{3,2,1,0:T(8,128)(2,1)}, u32[]{:S(2)}, u32[]{:S(2)}) %all-to-all-start.11) | async-done | bytes 1835040 | tf_op jit(solution)/shard_map/all_to_all | solution.py:32
  380.8 2.9 copy.61
  (77 shorter events, 32.7 us)
Async XLA Ops:
  0.6 2.3 copy-start
  2.7 1.2 copy-start.1
  91.4 30.5 %all-to-all-start.5 = ((f32[16,8,4,512]{3,2,1,0:T(4,128)}), f32[16,8,4,512]{3,2,1,0:T(4,128)S(1)}, u32[]{:S(2)}, u32[]{:S(2)}) async-start(f32[16,8,4,512]{3,2,1,0:T(4,128)} %broadcast_in_dim.24), calls=%async_computation.5 | async-start | bytes 2097152 | tf_op jit(solution)/shard_map/all_to_all | solution.py:32
  123.0 151.9 %all-to-all-start.1 = ((f32[16,32,512]{2,1,0:T(8,128)}), f32[16,32,512]{2,1,0:T(8,128)}, u32[]{:S(2)}, u32[]{:S(2)}) async-start(f32[16,32,512]{2,1,0:T(8,128)} %broadcast_in_dim.22), calls=%async_computation.1 | async-start | bytes 2097152 | tf_op jit(solution)/shard_map/all_to_all | solution.py:32
  134.7 1.0 copy-start.5
  278.2 5.5 %copy-start.2 = (f32[1,512,896]{2,1,0:T(8,128)S(1)}, f32[1,512,896]{2,1,0:T(8,128)}, u32[]{:S(2)}) copy-start(f32[1,512,896]{2,1,0:T(8,128)} %copy-done.1) | copy-start | bytes 5505028
  348.3 1.4 copy-start.6
  348.4 2.0 copy-start.3
  350.5 0.9 copy-start.4
  352.7 28.1 %all-to-all-start.11 = ((bf16[2,1,512,896]{3,2,1,0:T(8,128)(2,1)}), bf16[2,1,512,896]{3,2,1,0:T(8,128)(2,1)}, u32[]{:S(2)}, u32[]{:S(2)}) async-start(bf16[2,1,512,896]{3,2,1,0:T(8,128)(2,1)} %broadcast_in_dim.31), calls=%async_computation.11 | async-start | bytes 3670016 | tf_op jit(solution)/shard_map/all_to_all | solution.py:32
where the time goes:
time: 388 us; the launch traced here: 384 us
  blocking collectives  148 us (38%)
  other arithmetic  123 us (32%)
  waiting for transfers between devices  44.8 us (12%)
  local copies, waits for them, and re-layouts  27.2 us (7%)
  matrix products  21 us (5%)
  starting transfers between devices  15.8 us (4%)
  between operations  4 us (1%)
    another operation x14, other arithmetic, body(): lower = jnp.linalg.cholesky(gram)  78.8 us
    all_to_all x2, blocking collectives, sum_at_owner(): pieces = lax.all_to_all(in_blocks(x, dim, count), axis, 0, 0, tiled=True)  64.7 us
    all_to_all x5, blocking collectives, copy_for_each(): lax.all_to_all(jnp.broadcast_to(x[None], (count, *x.shape)), axis, 0, 0,...  54.1 us
    all_to_all x3, waiting for transfers between devices, copy_for_each(): lax.all_to_all(jnp.broadcast_to(x[None], (count, *x.shape)), axis, 0, 0,...  44.8 us
    another operation x3, other arithmetic, body(): lax.linalg.triangular_solve(lower, left, left_side=False, lower=True, tra...  40.4 us
    all_to_all x1, blocking collectives, sent_and_summed(): lax.all_to_all(pieces, axis, split_axis=0, concat_axis=0, tiled=True)  17 us
    all_to_all x3, starting transfers between devices, copy_for_each(): lax.all_to_all(jnp.broadcast_to(x[None], (count, *x.shape)), axis, 0, 0,...  15.8 us
    all_to_all x1, blocking collectives, sum_by_axis(): return jnp.sum(lax.all_to_all(own, far, 0, 0, tiled=True), axis=0)  12.3 us
  transfers between devices with their start and end apart: 3, of which 2 were waited for; matrix products, arithmetic and copies ran while one was open for 38% of the time, Pallas kernels for 0%

commit v1 on v0

v1 whole, which is shorter than its diff:
```python
import jax
import jax.numpy as jnp
from jax import lax
from jax.experimental import pallas as pl
from jax.experimental.pallas import tpu as pltpu
from jax.sharding import Mesh
from jax.sharding import PartitionSpec as P

COLS = 14336
TP = ("x", "z")
FSDP = ("y", "c")
F = jnp.float32
B = jnp.bfloat16

N = 512
NB = 128


def split(x):
    hi=x.astype(B); return hi,(x-hi.astype(F)).astype(B)
def dot3(a,b,dims):
    ah,al=split(a); bh,bl=split(b)
    d=lambda p,q: lax.dot_general(p,q,(dims,((),())),preferred_element_type=F)
    return d(ah,bh)+(d(ah,bl)+d(al,bh))

def factor(rows, inv_rows):
    n=len(rows)
    sub=lax.broadcasted_iota(jnp.int32,(8,NB),0)
    for p in range(n):
        for k in range(8):
            j=8*p+k
            col=jnp.broadcast_to(rows[p][:,j:j+1],(8,NB))
            rt=lax.rsqrt(col[k:k+1,:])
            row=rows[p][k:k+1,:]*rt
            erow=inv_rows[p][k:k+1,:]*rt
            row=jnp.broadcast_to(row,(8,NB)); erow=jnp.broadcast_to(erow,(8,NB))
            rtb=jnp.broadcast_to(rt,(8,NB))
            for q in range(p,n):
                c=col if q==p else jnp.broadcast_to(rows[q][:,j:j+1],(8,NB))
                l=c*rtb
                if q==p:
                    l=jnp.where(sub>k,l,0.0)
                    inv_rows[q]=jnp.where(sub==k,erow,inv_rows[q]-l*erow)
                else:
                    inv_rows[q]=inv_rows[q]-l*erow
                rows[q]=rows[q]-l*row
    return inv_rows

def chol_kernel(g_ref, left_ref, ortho_ref, w_ref, a_ref):
    a_ref[...]=g_ref[...]
    ri=lax.broadcasted_iota(jnp.int32,(8,NB),0); ci=lax.broadcasted_iota(jnp.int32,(8,NB),1)
    nblk=N//NB
    for k in range(nblk):
        lo=k*NB; hi=lo+NB
        rows=[a_ref[lo+8*p:lo+8*p+8,lo:hi] for p in range(NB//8)]
        inv=[(ci==ri+8*p).astype(F) for p in range(NB//8)]
        inv=factor(rows,inv)
        wkk=jnp.concatenate(inv,axis=0)
        w_ref[lo:hi,lo:hi]=wkk
        if hi<N: w_ref[lo:hi,hi:]=jnp.zeros((NB,N-hi),F)
        if k>0:
            w_ref[lo:hi,:lo]=dot3(wkk,w_ref[lo:hi,:lo],((1,),(0,)))
        if hi<N:
            r=dot3(wkk,a_ref[lo:hi,hi:],((1,),(0,)))
            a_ref[hi:,hi:]=a_ref[hi:,hi:]-dot3(r,r,((0,),(0,)))
            upd=dot3(r,w_ref[lo:hi,:hi],((0,),(0,)))
            if k==0: w_ref[hi:,:hi]=-upd
            else:
                w_ref[hi:,:lo]=w_ref[hi:,:lo]-upd[:,:lo]
                w_ref[hi:,lo:hi]=-upd[:,lo:]
    wh, wl = split(w_ref[...])
    left = left_ref[...]
    nt = lambda p, q: lax.dot_general(p, q, (((1,), (1,)), ((), ())), preferred_element_type=F)
    ortho_ref[...] = nt(left, wh) + nt(left, wl)


def orthonormal(gram, left):
    return pl.pallas_call(
        chol_kernel,
        out_shape=jax.ShapeDtypeStruct(left.shape, F),
        in_specs=[pl.BlockSpec(memory_space=pltpu.VMEM)] * 2,
        out_specs=pl.BlockSpec(memory_space=pltpu.VMEM),
        scratch_shapes=[pltpu.VMEM((N, N), F), pltpu.VMEM((N, N), F)],
        compiler_params=pltpu.CompilerParams(vmem_limit_bytes=32 * 2**20),
        name="orthonormal",
    )(gram, left)


def exchange(x, axis):
    return lax.all_to_all(x, axis, 0, 0, tiled=True)


def scatter_sum(x, axis, dtype):
    count = lax.axis_size(axis)
    pieces = exchange(x.astype(dtype).reshape(count, -1, x.shape[-1]), axis)
    return jnp.sum(pieces.astype(F), axis=0)


def gather(x, axis):
    count = lax.axis_size(axis)
    return exchange(jnp.broadcast_to(x[None], (count, *x.shape)), axis).reshape(-1, x.shape[-1])


def body(weights, gradient, momentum, basis):
    blend = momentum[0] + gradient[0].astype(F)
    blend16 = blend.astype(B)
    share = scatter_sum(jnp.dot(blend16, basis[0].astype(B), preferred_element_type=F), TP, B)
    left = gather(share.astype(B), TP)
    nn = lambda p, q, dims: lax.dot_general(p, q, (dims, ((), ())), preferred_element_type=F)
    gram = gather(scatter_sum(nn(left, left, ((0,), (0,))), FSDP, F), FSDP)
    ortho = orthonormal(gram, left)
    ortho16 = ortho.astype(B)
    right_share = scatter_sum(nn(blend16, ortho16, ((0,), (0,))), FSDP, B)
    right = lax.all_gather(right_share.astype(B), FSDP, axis=0, tiled=True)
    right32 = right.astype(F)
    squares = gather(jnp.sum(right32 * right32, axis=0, keepdims=True), TP)
    scale = lax.rsqrt(jnp.sum(squares, axis=0) / COLS + 1e-06)
    moment_new = blend - 0.05 * nn(ortho16, right, ((1,), (1,)))
    basis_new = right32 * scale
    update = nn((ortho * scale).astype(B), right, ((1,), (1,)))
    weight_new = (weights[0].astype(F) - 0.3 * update).astype(B)
    other = lax.ppermute(weight_new, "r", [(0, 1), (1, 0)])
    first = lax.axis_index("r") == 0
    both = jnp.where(first, jnp.stack([weight_new, other]), jnp.stack([other, weight_new]))
    return weight_new[None], moment_new[None], basis_new[None], both


def solution(mesh):
    finer = Mesh(mesh.devices.reshape(4, 2, 2, 8, 2), ("y", "c", "x", "z", "r"))
    split_specs = P("r", FSDP, TP)
    basis_spec = P("r", TP, None)
    return jax.shard_map(
        body,
        mesh=finer,
        in_specs=(split_specs, split_specs, split_specs, basis_spec),
        out_specs=(split_specs, split_specs, basis_spec, P(None, FSDP, TP)),
        check_vma=False,
    )
```

time: 388 us -> 208 us (0.54)
  other arithmetic: 123 us -> 5.64 us
  Pallas kernels: 0 us -> 45.3 us
  waiting for transfers between devices: 44.8 us -> 14.6 us
  local copies, waits for them, and re-layouts: 27.2 us -> 0.4 us
  blocking collectives: 148 us -> 127 us
  starting transfers between devices: 15.8 us -> 2.46 us
  matrix products: 21 us -> 10.5 us
    another operation x17 -> x0, other arithmetic: 119 us -> none  [the longest x14 78.8 us: body(): lower = jnp.linalg.cholesky(gram)]
    pallas_call x0 -> x1, Pallas kernels: none -> 45.3 us  [orthonormal(): pl.pallas_call(chol_kernel, out_shape=jax.ShapeDtypeStruct(left.shape, F)...]
    all_to_all x3 -> x0, waiting for transfers between devices: 44.8 us -> none  [copy_for_each(): lax.all_to_all(jnp.broadcast_to(x[None], (count, *x.shape)), axis, 0, 0,...]
    all_to_all x9 -> x6, blocking collectives: 148 us -> 113 us  [exchange(): return lax.all_to_all(x, axis, 0, 0, tiled=True)]
    all_to_all x3 -> x0, starting transfers between devices: 15.8 us -> none  [copy_for_each(): lax.all_to_all(jnp.broadcast_to(x[None], (count, *x.shape)), axis, 0, 0,...]
    another operation x19 -> x0, local copies, waits for them, and re-layouts: 14.7 us -> none
    ppermute x0 -> x1, waiting for transfers between devices: none -> 14.6 us  [body(): other = lax.ppermute(weight_new, 'r', [(0, 1), (1, 0)])]
    all_gather x0 -> x1, blocking collectives: none -> 14.3 us  [body(): right = lax.all_gather(right_share.astype(B), FSDP, axis=0, tiled=True)]
  transfers between devices with their start and end apart: 3 -> 1, of which waited for: 2 -> 1; matrix products, arithmetic and copies ran while one was open for 38% -> 2% of each run, Pallas kernels for 0% -> 0%
where the time goes in v1:
time: 208 us; the launch traced here: 207 us
  blocking collectives  127 us (61%)
  Pallas kernels  45.3 us (22%)
  waiting for transfers between devices  14.6 us (7%)
  matrix products  10.5 us (5%)
  other arithmetic  5.64 us (3%)
  starting transfers between devices  2.46 us (1%)
    all_to_all x6, blocking collectives, exchange(): return lax.all_to_all(x, axis, 0, 0, tiled=True)  113 us
    pallas_call x1, Pallas kernels, orthonormal(): pl.pallas_call(chol_kernel, out_shape=jax.ShapeDtypeStruct(left.shape, F)...  45.3 us
    ppermute x1, waiting for transfers between devices, body(): other = lax.ppermute(weight_new, 'r', [(0, 1), (1, 0)])  14.6 us
    all_gather x1, blocking collectives, body(): right = lax.all_gather(right_share.astype(B), FSDP, axis=0, tiled=True)  14.3 us
    dot_general x4, matrix products, body(): lax.dot_general(p, q, (dims, ((), ())), preferred_element_type=F)  7.44 us
  transfers between devices with their start and end apart: 1, of which 1 were waited for; matrix products, arithmetic and copies ran while one was open for 2% of the time, Pallas kernels for 0%

profile of v1, /device:TPU:1, one launch (start us, length us, event | category | flops | bytes accessed | tf_op | source)
XLA Modules:
  0.0 206.6 jit_solution(12481254822844575718)
XLA Ops:
  0.6 3.1 %convolution_convert_fusion.1 = bf16[512,512]{1,0:T(8,128)(2,1)S(1)} fusion(f32[1,896,512]{2,1,0:T(8,128)} %param.7, f32[1,512,896]{2,1,0:T(8,128)} %param.6, bf16[1,512,896]{2,1,0:T(8,128)(2,1)} %param.5), kind=kOutput, calls=%fused_computation.12 | convolution fusion | flops 471859200 | bytes 5111808 | tf_op jit(solution)/shard_map/dot_general | solution.py:107
  3.7 23.6 %all_to_all.30 = bf16[16,32,512]{2,1,0:T(8,128)(2,1)S(1)} all-to-all(bf16[16,32,512]{2,1,0:T(8,128)(2,1)S(1)} %bitcast.39), channel_id=1, replica_groups=mesh['y'=4,'c'=2,'x'=2,'z'=8,'r'=2] {'x','z'}, dimensions={0} | all-to-all | bytes 1048576 | tf_op jit(solution)/shard_map/all_to_all | solution.py:90
  27.3 0.1 reduce_sum.51
  27.4 18.7 %all_to_all.31 = bf16[16,32,512]{2,1,0:T(8,128)(2,1)S(1)} all-to-all(bf16[16,32,512]{2,1,0:T(8,128)(2,1)S(1)} %broadcast_in_dim.12), channel_id=1, replica_groups=mesh['y'=4,'c'=2,'x'=2,'z'=8,'r'=2] {'x','z'}, dimensions={0} | all-to-all | bytes 1048576 | tf_op jit(solution)/shard_map/all_to_all | solution.py:90
  46.1 0.2 copy.11
  46.3 0.4 fusion.11
  46.8 22.4 %all_to_all.32 = f32[8,64,512]{2,1,0:T(8,128)S(1)} all-to-all(f32[8,64,512]{2,1,0:T(8,128)S(1)} %fusion.11), channel_id=1, replica_groups=mesh['y'=4,'c'=2,'x'=2,'z'=8,'r'=2] {'y','c'}, dimensions={0} | all-to-all | bytes 2097152 | tf_op jit(solution)/shard_map/all_to_all | solution.py:90
  69.2 0.1 reduce_sum.52
  69.3 0.1 broadcast_in_dim.13
  69.4 0.0 copy-start.1
  69.4 18.7 %all_to_all.33 = f32[8,64,512]{2,1,0:T(8,128)S(1)} all-to-all(f32[8,64,512]{2,1,0:T(8,128)S(1)} %broadcast_in_dim.13), channel_id=1, replica_groups=mesh['y'=4,'c'=2,'x'=2,'z'=8,'r'=2] {'y','c'}, dimensions={0} | all-to-all | bytes 2097152 | tf_op jit(solution)/shard_map/all_to_all | solution.py:90
  88.1 0.0 copy-start
  88.1 45.3 %orthonormal.1 = f32[512,512]{1,0:T(8,128)S(1)} custom-call(f32[512,512]{1,0:T(8,128)S(1)} %bitcast.37, bf16[512,512]{1,0:T(8,128)(2,1)S(1)} %bitcast.36), custom_call_target="tpu_custom_call" | custom-call | tf_op jit(solution)/shard_map/orthonormal/pallas_call | solution.py:78
  133.4 0.0 copy-done.1
  133.4 0.0 copy-done
  133.4 0.7 convolution_convert_fusion
  134.1 17.2 %all_to_all.34 = bf16[8,112,512]{2,1,0:T(8,128)(2,1)S(1)} all-to-all(bf16[8,112,512]{2,1,0:T(8,128)(2,1)S(1)} %bitcast.38), channel_id=1, replica_groups=mesh['y'=4,'c'=2,'x'=2,'z'=8,'r'=2] {'y','c'}, dimensions={0} | all-to-all | bytes 1835008 | tf_op jit(solution)/shard_map/all_to_all | solution.py:90
  151.3 0.1 reduce_sum.53
  151.4 14.3 %all_gather.3 = bf16[896,512]{1,0:T(8,128)(2,1)S(1)} all-gather(bf16[112,512]{1,0:T(8,128)(2,1)S(1)} %reduce_sum.53), channel_id=1, replica_groups=mesh['y'=4,'c'=2,'x'=2,'z'=8,'r'=2] {'y','c'}, dimensions={0}, use_global_device_ids=true | all-gather | bytes 1032192 | tf_op jit(solution)/shard_map/all_gather | solution.py:114
  165.7 0.2 fusion
  166.0 12.0 %all_to_all.35 = f32[16,1,512]{2,1,0:T(1,128)S(1)} all-to-all(f32[16,1,512]{2,1,0:T(1,128)S(1)} %broadcast_in_dim.14), channel_id=1, replica_groups=mesh['y'=4,'c'=2,'x'=2,'z'=8,'r'=2] {'x','z'}, dimensions={0} | all-to-all | bytes 65536 | tf_op jit(solution)/shard_map/all_to_all | solution.py:90
  178.1 2.9 %fusion.2 = bf16[512,896]{1,0:T(8,128)(2,1)} fusion(bf16[896,512]{1,0:T(8,128)(2,1)S(1)} %all_gather.3, bf16[1,512,896]{2,1,0:T(8,128)(2,1)} %param.4, f32[512,512]{1,0:T(8,128)S(1)} %orthonormal.1, f32[512]{0:T(512)S(1)} %add_rsqrt_fusion), kind=kOutput, calls=%fused_computation.6 | convolution fusion | flops 472121344 | bytes 3803136 | tf_op jit(solution)/shard_map/dot_general | solution.py:109
  180.9 2.5 %collective-permute-start = (bf16[512,896]{1,0:T(8,128)(2,1)}, bf16[512,896]{1,0:T(8,128)(2,1)}, u32[]{:S(2)}, u32[]{:S(2)}) collective-permute-start(bf16[512,896]{1,0:T(8,128)(2,1)} %fusion.2), channel_id=1, source_target_pairs={{0,1},{1,0},{2,3},{3,2},{4,5},{5,4},{6,7},{7,6},{8,9},{9,8},{10,11... | collective-permute-start | bytes 2752520 | tf_op jit(solution)/shard_map/ppermute | solution.py:122
  183.4 3.5 %fusion.3 = f32[1,512,896]{2,1,0:T(8,128)} fusion(bf16[896,512]{1,0:T(8,128)(2,1)S(1)} %all_gather.3, f32[1,512,896]{2,1,0:T(8,128)} %param.6, bf16[1,512,896]{2,1,0:T(8,128)(2,1)S(1)} %copy-done.1, f32[512,512]{1,0:T(8,128)S(1)} %orthonormal.1), kind=kOutput, calls=%fused_computation.9 | convolution fusion | flops 471859200 | bytes 6553600 | tf_op jit(solution)/shard_map/dot_general | solution.py:109
  186.9 1.5 fusion.1
  188.4 14.6 %collective-permute-done = bf16[512,896]{1,0:T(8,128)(2,1)} collective-permute-done((bf16[512,896]{1,0:T(8,128)(2,1)}, bf16[512,896]{1,0:T(8,128)(2,1)}, u32[]{:S(2)}, u32[]{:S(2)}) %collective-permute-start) | collective-permute-done | bytes 917536 | tf_op jit(solution)/shard_map/ppermute | solution.py:122
  203.0 3.6 %maximum_select_fusion = bf16[2,512,896]{2,1,0:T(8,128)(2,1)} fusion(bf16[1,512,896]{2,1,0:T(8,128)(2,1)} %bitcast.14, bf16[1,512,896]{2,1,0:T(8,128)(2,1)} %bitcast.11, pred[]{:T(512)S(6)} %eq.3), kind=kLoop, calls=%fused_computation.4 | loop fusion | flops 2752512 | bytes 3670017 | tf_op jit(solution)/shard_map/jit(_where)/select_n | solution.py:124
  (4 shorter events, 0.1 us)
Async XLA Ops:
  69.4 63.9 %copy-start.1 = (bf16[1,512,896]{2,1,0:T(8,128)(2,1)S(1)}, bf16[1,512,896]{2,1,0:T(8,128)(2,1)}, u32[]{:S(2)}) copy-start(bf16[1,512,896]{2,1,0:T(8,128)(2,1)} %param.5) | copy-start | bytes 2752516
  88.1 45.3 %copy-start = (f32[1,512,896]{2,1,0:T(8,128)S(1)}, f32[1,512,896]{2,1,0:T(8,128)}, u32[]{:S(2)}) copy-start(f32[1,512,896]{2,1,0:T(8,128)} %param.6) | copy-start | bytes 5505028
  180.9 22.1 %collective-permute-start = (bf16[512,896]{1,0:T(8,128)(2,1)}, bf16[512,896]{1,0:T(8,128)(2,1)}, u32[]{:S(2)}, u32[]{:S(2)}) collective-permute-start(bf16[512,896]{1,0:T(8,128)(2,1)} %fusion.2), channel_id=1, source_target_pairs={{0,1},{1,0},{2,3},{3,2},{4,5},{5,4},{6,7},{7,6},{8,9},{9,8},{10,11... | collective-permute-start | bytes 2752520 | tf_op jit(solution)/shard_map/ppermute | solution.py:122

commit v2 on v1

v2 whole, which is shorter than its diff:
```python
import jax
import jax.numpy as jnp
from jax import lax
from jax.experimental import pallas as pl
from jax.experimental.pallas import tpu as pltpu
from jax.sharding import Mesh
from jax.sharding import PartitionSpec as P

COLS = 14336
TP = ("x", "z")
FSDP = ("y", "c")
F = jnp.float32
B = jnp.bfloat16
N = 512
NB = 128
GRP = 8
GR = 96
RR = 112
VMEM = pl.BlockSpec(memory_space=pltpu.VMEM)
SMEM = pl.BlockSpec(memory_space=pltpu.SMEM)


def call(kernel, outs, scratch=(), smem=0, name=None):
    def run(*args):
        return pl.pallas_call(
            kernel,
            out_shape=[jax.ShapeDtypeStruct(s, d) for s, d in outs],
            in_specs=[SMEM] * smem + [VMEM] * (len(args) - smem),
            out_specs=[VMEM] * len(outs),
            scratch_shapes=list(scratch),
            compiler_params=pltpu.CompilerParams(vmem_limit_bytes=48 * 2**20),
            name=name,
        )(*args)

    return run


def dot(p, q, over):
    return lax.dot_general(p, q, (over, ((), ())), preferred_element_type=F)


NN, NT, TN = ((1,), (0,)), ((1,), (1,)), ((0,), (0,))


def halves(x):
    hi = x.astype(B)
    return hi, (x - hi.astype(F)).astype(B)


def dot3(a, b, over):
    ah, al = halves(a)
    bh, bl = halves(b)
    return dot(ah, bh, over) + (dot(ah, bl, over) + dot(al, bh, over))


def total(v):
    while len(v) > 1:
        v = [v[i] + v[i + 1] if i + 1 < len(v) else v[i] for i in range(0, len(v), 2)]
    return v[0]


def factor(rows, inv_rows):
    n, w, b = len(rows), rows[0].shape[1], GRP
    sub = lax.broadcasted_iota(jnp.int32, (8, w), 0)
    full = lambda v: jnp.broadcast_to(v, (8, w))
    for p in range(n):
        j = 8 * p
        cols = [full(rows[p][:, j + m : j + m + 1]) for m in range(b)]
        d = [[full(cols[m][i : i + 1, :]) for m in range(i + 1)] for i in range(b)]
        row = [full(rows[p][m : m + 1, :]) for m in range(b)]
        erow = [full(inv_rows[p][m : m + 1, :]) for m in range(b)]
        v = [[None] * b for _ in range(b)]
        low = [[None] * b for _ in range(b)]
        for i in range(b):
            rt = lax.rsqrt(d[i][i])
            for m in range(i + 1, b):
                low[m][i] = d[m][i] * rt
            for m in range(i + 1, b):
                for t in range(i + 1, m + 1):
                    d[m][t] = d[m][t] - low[m][i] * low[t][i]
            v[i][i] = rt
            for t in range(i):
                v[i][t] = -(rt * total([low[i][k] * v[k][t] for k in range(t, i)]))
        r = [total([v[i][m] * row[m] for m in range(i + 1)]) for i in range(b)]
        e = [total([v[i][m] * erow[m] for m in range(i + 1)]) for i in range(b)]
        z = [total([v[i][m] * r[i] for i in range(m, b)]) for m in range(b)]
        ze = [total([v[i][m] * e[i] for i in range(m, b)]) for m in range(b)]
        for q in range(p + 1, n):
            c = [full(rows[q][:, j + m : j + m + 1]) for m in range(b)]
            rows[q] = rows[q] - total([c[m] * z[m] for m in range(b)])
            inv_rows[q] = inv_rows[q] - total([c[m] * ze[m] for m in range(b)])
        y = e[0]
        for i in range(1, b):
            y = jnp.where(sub == i, e[i], y)
        inv_rows[p] = y
    return inv_rows


def inverse_factor(a_ref, w_ref):
    ri = lax.broadcasted_iota(jnp.int32, (8, NB), 0)
    ci = lax.broadcasted_iota(jnp.int32, (8, NB), 1)
    for lo in range(0, N, NB):
        hi = lo + NB
        rows = [a_ref[lo + 8 * p : lo + 8 * p + 8, lo:hi] for p in range(NB // 8)]
        inv = factor(rows, [(ci == ri + 8 * p).astype(F) for p in range(NB // 8)])
        wkk = jnp.concatenate(inv, axis=0)
        w_ref[lo:hi, lo:hi] = wkk
        if hi < N:
            w_ref[lo:hi, hi:] = jnp.zeros((NB, N - hi), F)
        if lo > 0:
            w_ref[lo:hi, :lo] = dot3(wkk, w_ref[lo:hi, :lo], NN)
        if hi < N:
            r = dot3(wkk, a_ref[lo:hi, hi:], NN)
            for s in range(hi, N, NB):
                a_ref[s : s + NB, s:] = a_ref[s : s + NB, s:] - dot3(r[:, s - hi : s - hi + NB], r[:, s - hi :], TN)
            upd = dot3(r, w_ref[lo:hi, :hi], TN)
            if lo > 0:
                w_ref[hi:, :lo] = w_ref[hi:, :lo] - upd[:, :lo]
            w_ref[hi:, lo:hi] = -upd[:, lo:]


def pieces_kernel(core, left_ref, blend_ref, keep_g, keep_r, send, right_scr, part):
    right_scr[...] = dot(blend_ref[...], left_ref[...], TN)
    for mine in (True, False):
        c = core[0] if mine else 1 - core[0]
        wide = left_ref[:, pl.ds(pl.multiple_of(c * 256, 256), 256)]
        narrow = left_ref[:, pl.ds(pl.multiple_of(c * 128, 128), 128)]
        part[:256, :] = dot(wide, wide, TN)
        part[256:, :] = dot(narrow, left_ref[:, 256:], TN)
        for y in range(4):
            g = part[y * GR : (y + 1) * GR, :]
            r = right_scr[pl.ds(pl.multiple_of((2 * y + c) * RR, 16), RR), :]
            if mine:
                keep_g[y] = g
                keep_r[y] = r
            else:
                gh, gl = halves(g)
                send[y, :RR, :] = r.astype(B)
                send[y, RR:, :256] = gh
                send[y, RR:, 256:] = gl


def join_kernel(line, keep_g, keep_r, got, own_g, own_r, one, two, three):
    for k, out in enumerate((None, one, two, three)):
        y = line[0] ^ k
        r = keep_r[y] + got[y, :RR, :].astype(F)
        g = keep_g[y] + (got[y, RR:, :256].astype(F) + got[y, RR:, 256:].astype(F))
        if out is None:
            own_g[...] = g
            own_r[...] = r
        else:
            gh, gl = halves(g)
            out[:RR, :] = r.astype(B)
            out[RR:, :256] = gh
            out[RR:, 256:] = gl


def sum_kernel(own_g, own_r, one, two, three, out):
    g, r = own_g[...], own_r[...]
    for got in (one, two, three):
        r = r + got[:RR, :].astype(F)
        g = g + (got[RR:, :256].astype(F) + got[RR:, 256:].astype(F))
    gh, gl = halves(g)
    out[:RR, :] = r.astype(B)
    out[RR:, :256] = gh
    out[RR:, 256:] = gl


def split_kernel(both, right):
    for f in range(8):
        right[f * RR : (f + 1) * RR, :] = both[f, :RR, :]


def solve_kernel(both, left, right_in, w16, ortho, right, squares, a, w):
    for f in range(8):
        y, c = divmod(f, 2)
        g = both[f, RR:, :256].astype(F) + both[f, RR:, 256:].astype(F)
        first = y * GR
        square = max(0, min(GR, 256 - first))
        if square:
            a[c * 256 + first : c * 256 + first + square, c * 256 : c * 256 + 256] = g[:square, :]
        if square < GR:
            at = c * 128 + first + square - 256
            a[at : at + GR - square, 256:] = g[square:, :]
    inverse_factor(a, w)
    wh, wl = halves(w[...])
    w16[...] = wh
    ortho[...] = (dot(left[...], wh, NT) + dot(left[...], wl, NT)).astype(B)
    r = dot(right_in[...], wh, NT) + dot(right_in[...], wl, NT)
    right[...] = r
    squares[...] = jnp.sum(r * r, axis=0, keepdims=True)


def own_kernel(blend, ortho, right, scale, moment, basis):
    r = right[...]
    basis[...] = r * scale[...]
    moment[...] = blend[...] - 0.05 * dot(ortho[...], r.astype(B), NT)


def weight_kernel(side, left0, w0, right0, scale0, weight0, left1, w1, right1, scale1, weight1, own, out):
    for k, refs in enumerate(((left0, w0, right0, scale0, weight0), (left1, w1, right1, scale1, weight1))):
        left, w, right, scale, weight = (ref[...] for ref in refs)
        o = (dot(left, w, NT) * scale).astype(B)
        r = dot(right, w, NT).astype(B)
        new = (weight.astype(F) - 0.3 * dot(o, r, NT)).astype(B)
        if k == 0:
            own[...] = new
        out[side[0] if k == 0 else 1 - side[0]] = new


def exchange(x, axis):
    return lax.all_to_all(x, axis, 0, 0, tiled=True)


def gather(x, axis):
    count = lax.axis_size(axis)
    return exchange(jnp.broadcast_to(x[None], (count, *x.shape)), axis).reshape(-1, x.shape[-1])


def swap(x, axis, bit=1):
    return lax.ppermute(x, axis, [(i, i ^ bit) for i in range(lax.axis_size(axis))])


def body(weights, gradient, momentum, basis):
    index = lambda axis: lax.axis_index(axis).astype(jnp.int32).reshape(1)
    blend = momentum[0] + gradient[0].astype(F)
    blend16 = blend.astype(B)
    part = dot(blend16, basis[0].astype(B), NN).astype(B).reshape(16, -1, N)
    share = jnp.sum(exchange(part, TP).astype(F), axis=0).astype(B)
    left = gather(share, TP)

    keep_g, keep_r, send = call(
        pieces_kernel,
        [((4, GR, 256), F), ((4, RR, N), F), ((4, RR + GR, N), B)],
        [pltpu.VMEM((8 * RR, N), F), pltpu.VMEM((384, 256), F)],
        smem=1,
        name="pieces",
    )(index("c"), left, blend16)
    got = swap(send, "c")
    left_o = swap(left, "r")
    own_g, own_r, *outs = call(
        join_kernel,
        [((GR, 256), F), ((RR, N), F)] + [((RR + GR, N), B)] * 3,
        smem=1,
        name="join",
    )(index("y"), keep_g, keep_r, got)
    arrived = [swap(x, "y", k + 1) for k, x in enumerate(outs)]
    (piece,) = call(sum_kernel, [((RR + GR, N), B)], name="sum")(own_g, own_r, *arrived)
    both = lax.all_gather(piece, FSDP, axis=0, tiled=False)
    (raw,) = call(split_kernel, [((8 * RR, N), B)], name="split")(both)
    raw_o = swap(raw, "r")
    weight, _ = lax.optimization_barrier((weights[0], left))
    weight_o = swap(weight, "r")

    w16, ortho, right, squares = call(
        solve_kernel,
        [((N, N), B), ((N, N), B), ((8 * RR, N), F), ((1, N), F)],
        [pltpu.VMEM((N, N), F), pltpu.VMEM((N, N), F)],
        name="solve",
    )(both, left, raw)
    w16_o = swap(w16, "r")
    scale = lax.rsqrt(jnp.sum(gather(squares, TP), axis=0, keepdims=True) / COLS + 1e-06)
    scale_o = swap(scale, "r")
    moment_new, basis_new = call(own_kernel, [(blend.shape, F), (right.shape, F)], name="own")(
        blend, ortho, right, scale
    )
    weight_new, rollout = call(
        weight_kernel, [(weight.shape, B), ((2, *weight.shape), B)], smem=1, name="weights"
    )(index("r"), left, w16, raw, scale, weights[0], left_o, w16_o, raw_o, scale_o, weight_o)
    return weight_new[None], moment_new[None], basis_new[None], rollout


def solution(mesh):
    finer = Mesh(mesh.devices.reshape(4, 2, 2, 8, 2), ("y", "c", "x", "z", "r"))
    split_specs = P("r", FSDP, TP)
    basis_spec = P("r", TP, None)
    return jax.shard_map(
        body,
        mesh=finer,
        in_specs=(split_specs, split_specs, split_specs, basis_spec),
        out_specs=(split_specs, split_specs, basis_spec, P(None, FSDP, TP)),
        check_vma=False,
    )
```

time: 208 us -> 174 us (0.84)
  blocking collectives: 127 us -> 37.6 us
  waiting for transfers between devices: 14.6 us -> 47.3 us
  starting transfers between devices: 2.46 us -> 23.3 us
  between operations: 0.71 us -> 14.1 us
  local copies, waits for them, and re-layouts: 0.4 us -> 10.7 us
  Pallas kernels: 45.3 us -> 35.7 us
  matrix products: 10.5 us -> 3.05 us
  other arithmetic: 5.64 us -> 2.07 us
    all_to_all x6 -> x2, blocking collectives: 113 us -> 37.6 us  [exchange(): return lax.all_to_all(x, axis, 0, 0, tiled=True)]
    all_gather x0 -> x1, waiting for transfers between devices: none -> 22.4 us  [body(): both = lax.all_gather(piece, FSDP, axis=0, tiled=False)]
    ppermute x1 -> x9, starting transfers between devices: 2.46 us -> 17.3 us  [swap(): lax.ppermute(x, axis, [(i, i ^ bit) for i in range(lax.axis_size(axis))])]
    all_gather x1 -> x0, blocking collectives: 14.3 us -> none  [body(): right = lax.all_gather(right_share.astype(B), FSDP, axis=0, tiled=True)]
    all_to_all x0 -> x1, waiting for transfers between devices: none -> 11 us  [exchange(): return lax.all_to_all(x, axis, 0, 0, tiled=True)]
    unnamed x4 -> x20, local copies, waits for them, and re-layouts: 0.01 us -> 9.85 us
    pallas_call x1 -> x7, Pallas kernels: 45.3 us -> 35.7 us  [run(): pl.pallas_call(kernel, out_shape=[jax.ShapeDtypeStruct(s, d) for s, d in...]
    dot_general x5 -> x1, matrix products: 10.5 us -> 3.05 us  [dot(): return lax.dot_general(p, q, (over, ((), ())), preferred_element_type=F)]
  transfers between devices with their start and end apart: 1 -> 11, of which waited for: 1 -> 6; matrix products, arithmetic and copies ran while one was open for 2% -> 1% of each run, Pallas kernels for 0% -> 16%
where the time goes in v2:
time: 174 us
  waiting for transfers between devices  47.3 us (27%)
  blocking collectives  37.6 us (22%)
  Pallas kernels  35.7 us (21%)
  starting transfers between devices  23.3 us (13%)
  between operations  14.1 us (8%)
  local copies, waits for them, and re-layouts  10.7 us (6%)
  matrix products  3.05 us (2%)
  other arithmetic  2.07 us (1%)
    all_to_all x2, blocking collectives, exchange(): return lax.all_to_all(x, axis, 0, 0, tiled=True)  37.6 us
    pallas_call x7, Pallas kernels, run(): pl.pallas_call(kernel, out_shape=[jax.ShapeDtypeStruct(s, d) for s, d in...  35.7 us
    all_gather x1, waiting for transfers between devices, body(): both = lax.all_gather(piece, FSDP, axis=0, tiled=False)  22.4 us
    ppermute x9, starting transfers between devices, swap(): lax.ppermute(x, axis, [(i, i ^ bit) for i in range(lax.axis_size(axis))])  17.3 us
    ppermute x9, waiting for transfers between devices, swap(): lax.ppermute(x, axis, [(i, i ^ bit) for i in range(lax.axis_size(axis))])  14 us
    all_to_all x1, waiting for transfers between devices, exchange(): return lax.all_to_all(x, axis, 0, 0, tiled=True)  11 us
    unnamed x20, local copies, waits for them, and re-layouts  9.85 us
    all_to_all x1, starting transfers between devices, exchange(): return lax.all_to_all(x, axis, 0, 0, tiled=True)  5.96 us
  transfers between devices with their start and end apart: 11, of which 6 were waited for; matrix products, arithmetic and copies ran while one was open for 1% of the time, Pallas kernels for 16%

profile of v2, /device:TPU:1, one launch (start us, length us, event | category | flops | bytes accessed | tf_op | source)
XLA Modules:
  0.0 173.8 jit_solution(14446518369035224246)
XLA Ops:
  7.2 3.1 %convolution_convert_fusion = bf16[512,512]{1,0:T(8,128)(2,1)S(1)} fusion(f32[1,512,896]{2,1,0:T(8,128)} %param.6, bf16[1,512,896]{2,1,0:T(8,128)(2,1)} %param.5, f32[1,896,512]{2,1,0:T(8,128)} %param.7), kind=kOutput, calls=%fused_computation.1 | convolution fusion | flops 471859200 | bytes 5111808 | tf_op jit(solution)/shard_map/dot_general | solution.py:39
  10.2 23.6 %all_to_all.15 = bf16[16,32,512]{2,1,0:T(8,128)(2,1)S(1)} all-to-all(bf16[16,32,512]{2,1,0:T(8,128)(2,1)S(1)} %bitcast.33), channel_id=1, replica_groups=mesh['y'=4,'c'=2,'x'=2,'z'=8,'r'=2] {'x','z'}, dimensions={0} | all-to-all | bytes 1048576 | tf_op jit(solution)/shard_map/all_to_all | solution.py:212
  33.9 0.8 broadcast_in_dim.24
  34.7 6.0 %all-to-all-start.1 = ((bf16[16,32,512]{2,1,0:T(8,128)(2,1)}), bf16[16,32,512]{2,1,0:T(8,128)(2,1)S(1)}, u32[]{:S(2)}, u32[]{:S(2)}) async-start(bf16[16,32,512]{2,1,0:T(8,128)(2,1)} %broadcast_in_dim.24), calls=%async_computation.1 | async-start | bytes 1048576 | tf_op jit(solution)/shard_map/all_to_all | solution.py:212
  40.8 1.9 %fusion.6 = (bf16[512,896]{1,0:T(8,128)(2,1)S(1)}, f32[512,896]{1,0:T(8,128)S(1)}) fusion(f32[1,512,896]{2,1,0:T(8,128)} %param.6, bf16[1,512,896]{2,1,0:T(8,128)(2,1)} %param.5), kind=kLoop, calls=%fused_computation.8 | loop fusion | flops 1376256 | bytes 5505024 | tf_op jit(solution)/shard_map/convert_element_type | solution.py:227
  42.7 11.0 %all-to-all-done.1 = bf16[16,32,512]{2,1,0:T(8,128)(2,1)S(1)} async-done(((bf16[16,32,512]{2,1,0:T(8,128)(2,1)}), bf16[16,32,512]{2,1,0:T(8,128)(2,1)S(1)}, u32[]{:S(2)}, u32[]{:S(2)}) %all-to-all-start.1) | async-done | bytes 524320 | tf_op jit(solution)/shard_map/all_to_all | solution.py:212
  53.7 1.8 %pieces.1 = (f32[4,96,256]{2,1,0:T(8,128)S(1)}, f32[4,112,512]{2,1,0:T(8,128)S(1)}, bf16[4,208,512]{2,1,0:T(8,128)(2,1)}) custom-call(s32[1]{0:T(128)} %bitcast.6.core, bf16[512,512]{1,0:T(8,128)(2,1)S(1)} %bitcast.21, bf16[512,896]{1,0:T(8,128)(2,1)S(1)} %get-tuple-element.38.blend_ref), custom_call_target="tpu_custom_call" | custom-call | tf_op jit(solution)/shard_map/pieces/pallas_call | solution.py:25
  55.5 0.9 copy-done.3
  57.1 3.1 %collective-permute-start = (bf16[4,208,512]{2,1,0:T(8,128)(2,1)}, bf16[4,208,512]{2,1,0:T(8,128)(2,1)S(1)}, u32[]{:S(2)}, u32[]{:S(2)}) collective-permute-start(bf16[4,208,512]{2,1,0:T(8,128)(2,1)} %get-tuple-element.23), channel_id=1, source_target_pairs={{0,32},{32,0},{1,33},{33,1},{2,34},{34,2},{3,35},{35,3},{4,36},{36... | collective-permute-start | bytes 2555912 | tf_op jit(solution)/shard_map/ppermute | solution.py:221
  60.2 2.2 %collective-permute-done.got = bf16[4,208,512]{2,1,0:T(8,128)(2,1)S(1)} collective-permute-done((bf16[4,208,512]{2,1,0:T(8,128)(2,1)}, bf16[4,208,512]{2,1,0:T(8,128)(2,1)S(1)}, u32[]{:S(2)}, u32[]{:S(2)}) %collective-permute-start) | collective-permute-done | bytes 852000 | tf_op jit(solution)/shard_map/ppermute | solution.py:221
  62.5 1.2 copy-done.4
  63.6 1.0 copy-done.9
  64.8 1.4 collective-permute-start.1
  66.2 2.6 %collective-permute-start.2 = (bf16[208,512]{1,0:T(8,128)(2,1)S(1)}, bf16[208,512]{1,0:T(8,128)(2,1)S(1)}, u32[]{:S(2)}, u32[]{:S(2)}) collective-permute-start(bf16[208,512]{1,0:T(8,128)(2,1)S(1)} %get-tuple-element.27), channel_id=1, source_target_pairs={{0,128},{64,192},{128,0},{192,64},{1,129},{65,193},{129,1},{193,65... | collective-permute-start | bytes 638984 | tf_op jit(solution)/shard_map/ppermute | solution.py:221
  68.8 2.5 %collective-permute-done.1.one = bf16[208,512]{1,0:T(8,128)(2,1)S(1)} collective-permute-done((bf16[208,512]{1,0:T(8,128)(2,1)S(1)}, bf16[208,512]{1,0:T(8,128)(2,1)S(1)}, u32[]{:S(2)}, u32[]{:S(2)}) %collective-permute-start.1) | collective-permute-done | bytes 213024 | tf_op jit(solution)/shard_map/ppermute | solution.py:221
  71.4 7.1 %collective-permute-done.2.two = bf16[208,512]{1,0:T(8,128)(2,1)S(1)} collective-permute-done((bf16[208,512]{1,0:T(8,128)(2,1)S(1)}, bf16[208,512]{1,0:T(8,128)(2,1)S(1)}, u32[]{:S(2)}, u32[]{:S(2)}) %collective-permute-start.2) | collective-permute-done | bytes 213024 | tf_op jit(solution)/shard_map/ppermute | solution.py:221
  78.4 2.1 %collective-permute-done.3.three = bf16[208,512]{1,0:T(8,128)(2,1)S(1)} collective-permute-done((bf16[208,512]{1,0:T(8,128)(2,1)S(1)}, bf16[208,512]{1,0:T(8,128)(2,1)S(1)}, u32[]{:S(2)}, u32[]{:S(2)}) %collective-permute-start.3) | collective-permute-done | bytes 213024 | tf_op jit(solution)/shard_map/ppermute | solution.py:221
  80.6 0.8 sum.1
  81.4 2.5 %collective-permute-start.8 = (bf16[512,896]{1,0:T(8,128)(2,1)}, bf16[512,896]{1,0:T(8,128)(2,1)}, u32[]{:S(2)}, u32[]{:S(2)}) collective-permute-start(bf16[512,896]{1,0:T(8,128)(2,1)} %bitcast.27), channel_id=1, source_target_pairs={{0,1},{1,0},{2,3},{3,2},{4,5},{5,4},{6,7},{7,6},{8,9},{9,8},{10,11... | collective-permute-start | bytes 2752520 | tf_op jit(solution)/shard_map/ppermute | solution.py:221
  83.9 22.4 %all-gather.3.cloned.1.call-done = bf16[1664,512]{1,0:T(8,128)(2,1)} async-done(((bf16[208,512]{1,0:T(8,128)(2,1)}), bf16[1664,512]{1,0:T(8,128)(2,1)}) %all-gather.3.cloned.1.call-update) | async-done | bytes 1703952 | tf_op jit(solution)/shard_map/all_gather | solution.py:249
  106.3 1.5 copy-done
  107.8 2.8 %collective-permute-start.6 = (bf16[896,512]{1,0:T(8,128)(2,1)S(1)}, bf16[896,512]{1,0:T(8,128)(2,1)}, u32[]{:S(2)}, u32[]{:S(2)}) collective-permute-start(bf16[896,512]{1,0:T(8,128)(2,1)S(1)} %split.1.right_in.right0), channel_id=1, source_target_pairs={{0,1},{1,0},{2,3},{3,2},{4,5},{5,4},{6,7},{7,6},{8,9},{9,8},{10,11... | collective-permute-start | bytes 2752520 | tf_op jit(solution)/shard_map/ppermute | solution.py:221
  110.8 24.6 %solve.1 = (bf16[512,512]{1,0:T(8,128)(2,1)}, bf16[512,512]{1,0:T(8,128)(2,1)S(1)}, f32[896,512]{1,0:T(8,128)S(1)}, f32[1,512]{1,0:T(1,128)S(1)}) custom-call(bf16[8,208,512]{2,1,0:T(8,128)(2,1)S(1)} %bitcast.26, bf16[512,512]{1,0:T(8,128)(2,1)S(1)} %bitcast.23, bf16[896,512]{1,0:T(8,128)(2,1)S(1)} %split.1.right_in.right0), custom_call_target="tpu_custom_call" | custom-call | tf_op jit(solution)/shard_map/solve/pallas_call | solution.py:25
  135.5 1.2 copy-done.1
  136.7 0.8 copy-done.6
  137.5 2.7 %collective-permute-start.5 = (bf16[512,512]{1,0:T(8,128)(2,1)}, bf16[512,512]{1,0:T(8,128)(2,1)}, u32[]{:S(2)}, u32[]{:S(2)}) collective-permute-start(bf16[512,512]{1,0:T(8,128)(2,1)} %get-tuple-element.29.w0), channel_id=1, source_target_pairs={{0,1},{1,0},{2,3},{3,2},{4,5},{5,4},{6,7},{7,6},{8,9},{9,8},{10,11... | collective-permute-start | bytes 1572872 | tf_op jit(solution)/shard_map/ppermute | solution.py:221
  140.2 14.0 %all_to_all.16 = f32[16,1,512]{2,1,0:T(1,128)S(1)} all-to-all(f32[16,1,512]{2,1,0:T(1,128)S(1)} %broadcast_in_dim.26), channel_id=1, replica_groups=mesh['y'=4,'c'=2,'x'=2,'z'=8,'r'=2] {'x','z'}, dimensions={0} | all-to-all | bytes 65536 | tf_op jit(solution)/shard_map/all_to_all | solution.py:212
  154.3 1.9 %collective-permute-start.7 = (f32[1,512]{1,0:T(1,128)S(1)}, f32[1,512]{1,0:T(1,128)S(1)}, u32[]{:S(2)}, u32[]{:S(2)}) collective-permute-start(f32[1,512]{1,0:T(1,128)S(1)} %bitcast.29), channel_id=1, source_target_pairs={{0,1},{1,0},{2,3},{3,2},{4,5},{5,4},{6,7},{7,6},{8,9},{9,8},{10,11... | collective-permute-start | bytes 6152 | tf_op jit(solution)/shard_map/ppermute | solution.py:221
  156.1 1.5 copy-done.2
  157.6 1.0 copy-done.7
  158.7 2.3 %own.1 = (f32[512,896]{1,0:T(8,128)}, f32[896,512]{1,0:T(8,128)}) custom-call(f32[512,896]{1,0:T(8,128)S(1)} %get-tuple-element.39.blend, bf16[512,512]{1,0:T(8,128)(2,1)S(1)} %copy-done.7, f32[896,512]{1,0:T(8,128)S(1)} %copy-done.2, f32[1,512]{1,0:T(1,128)S(1)} %bitcast.30), custom_call_target="tpu_custom_call" | custom-call | tf_op jit(solution)/shard_map/own/pallas_call | solution.py:25
  161.0 6.0 %weights.1 = (bf16[512,896]{1,0:T(8,128)(2,1)}, bf16[2,512,896]{2,1,0:T(8,128)(2,1)}) custom-call(s32[1]{0:T(128)} %bitcast.side, bf16[512,512]{1,0:T(8,128)(2,1)S(1)} %bitcast.24, bf16[512,512]{1,0:T(8,128)(2,1)} %get-tuple-element.29.w0, bf16[896,512]{1,0:T(8,128)(2,1)S(1)} %split.1.right_in.right0, f32[1,512]{1,0:T(1,128)S(1)} %bitcast.31, ...), custom_call_target="tpu_custom_call" | custom-call | tf_op jit(solution)/shard_map/weights/pallas_call | solution.py:25
  (27 shorter events, 1.5 us)
Async XLA Ops:
  34.7 18.9 %all-to-all-start.1 = ((bf16[16,32,512]{2,1,0:T(8,128)(2,1)}), bf16[16,32,512]{2,1,0:T(8,128)(2,1)S(1)}, u32[]{:S(2)}, u32[]{:S(2)}) async-start(bf16[16,32,512]{2,1,0:T(8,128)(2,1)} %broadcast_in_dim.24), calls=%async_computation.1 | async-start | bytes 1048576 | tf_op jit(solution)/shard_map/all_to_all | solution.py:212
  40.7 65.5 %all-gather.3.cloned.1.call-start = ((), (), s32[]{:S(2)}) async-start(), calls=%async_computation.3 | async-start | bytes 1916928 | tf_op jit(solution)/shard_map/all_gather | solution.py:249
  55.5 0.9 copy-start.3
  56.4 0.7 copy-start.8
  57.1 5.3 %collective-permute-start = (bf16[4,208,512]{2,1,0:T(8,128)(2,1)}, bf16[4,208,512]{2,1,0:T(8,128)(2,1)S(1)}, u32[]{:S(2)}, u32[]{:S(2)}) collective-permute-start(bf16[4,208,512]{2,1,0:T(8,128)(2,1)} %get-tuple-element.23), channel_id=1, source_target_pairs={{0,32},{32,0},{1,33},{33,1},{2,34},{34,2},{3,35},{35,3},{4,36},{36... | collective-permute-start | bytes 2555912 | tf_op jit(solution)/shard_map/ppermute | solution.py:221
  62.5 1.2 copy-start.4
  63.6 1.0 copy-start.9
  64.8 6.6 %collective-permute-start.1 = (bf16[208,512]{1,0:T(8,128)(2,1)S(1)}, bf16[208,512]{1,0:T(8,128)(2,1)S(1)}, u32[]{:S(2)}, u32[]{:S(2)}) collective-permute-start(bf16[208,512]{1,0:T(8,128)(2,1)S(1)} %get-tuple-element.26), channel_id=1, source_target_pairs={{0,64},{64,0},{128,192},{192,128},{1,65},{65,1},{129,193},{193,129... | collective-permute-start | bytes 638984 | tf_op jit(solution)/shard_map/ppermute | solution.py:221
  66.2 12.2 %collective-permute-start.2 = (bf16[208,512]{1,0:T(8,128)(2,1)S(1)}, bf16[208,512]{1,0:T(8,128)(2,1)S(1)}, u32[]{:S(2)}, u32[]{:S(2)}) collective-permute-start(bf16[208,512]{1,0:T(8,128)(2,1)S(1)} %get-tuple-element.27), channel_id=1, source_target_pairs={{0,128},{64,192},{128,0},{192,64},{1,129},{65,193},{129,1},{193,65... | collective-permute-start | bytes 638984 | tf_op jit(solution)/shard_map/ppermute | solution.py:221
  68.8 11.8 %collective-permute-start.3 = (bf16[208,512]{1,0:T(8,128)(2,1)S(1)}, bf16[208,512]{1,0:T(8,128)(2,1)S(1)}, u32[]{:S(2)}, u32[]{:S(2)}) collective-permute-start(bf16[208,512]{1,0:T(8,128)(2,1)S(1)} %get-tuple-element.28), channel_id=1, source_target_pairs={{0,192},{64,128},{128,64},{192,0},{1,193},{65,129},{129,65},{193,1... | collective-permute-start | bytes 638984 | tf_op jit(solution)/shard_map/ppermute | solution.py:221
  81.4 79.6 %collective-permute-start.8 = (bf16[512,896]{1,0:T(8,128)(2,1)}, bf16[512,896]{1,0:T(8,128)(2,1)}, u32[]{:S(2)}, u32[]{:S(2)}) collective-permute-start(bf16[512,896]{1,0:T(8,128)(2,1)} %bitcast.27), channel_id=1, source_target_pairs={{0,1},{1,0},{2,3},{3,2},{4,5},{5,4},{6,7},{7,6},{8,9},{9,8},{10,11... | collective-permute-start | bytes 2752520 | tf_op jit(solution)/shard_map/ppermute | solution.py:221
  106.3 1.5 copy-start
  107.8 53.2 %collective-permute-start.6 = (bf16[896,512]{1,0:T(8,128)(2,1)S(1)}, bf16[896,512]{1,0:T(8,128)(2,1)}, u32[]{:S(2)}, u32[]{:S(2)}) collective-permute-start(bf16[896,512]{1,0:T(8,128)(2,1)S(1)} %split.1.right_in.right0), channel_id=1, source_target_pairs={{0,1},{1,0},{2,3},{3,2},{4,5},{5,4},{6,7},{7,6},{8,9},{9,8},{10,11... | collective-permute-start | bytes 2752520 | tf_op jit(solution)/shard_map/ppermute | solution.py:221
  110.6 50.4 %collective-permute-start.4 = (bf16[512,512]{1,0:T(8,128)(2,1)S(1)}, bf16[512,512]{1,0:T(8,128)(2,1)}, u32[]{:S(2)}, u32[]{:S(2)}) collective-permute-start(bf16[512,512]{1,0:T(8,128)(2,1)S(1)} %bitcast.22), channel_id=1, source_target_pairs={{0,1},{1,0},{2,3},{3,2},{4,5},{5,4},{6,7},{7,6},{8,9},{9,8},{10,11... | collective-permute-start | bytes 1572872 | tf_op jit(solution)/shard_map/ppermute | solution.py:221
  135.5 1.2 copy-start.1
  136.7 0.8 copy-start.6
  137.5 23.5 %collective-permute-start.5 = (bf16[512,512]{1,0:T(8,128)(2,1)}, bf16[512,512]{1,0:T(8,128)(2,1)}, u32[]{:S(2)}, u32[]{:S(2)}) collective-permute-start(bf16[512,512]{1,0:T(8,128)(2,1)} %get-tuple-element.29.w0), channel_id=1, source_target_pairs={{0,1},{1,0},{2,3},{3,2},{4,5},{5,4},{6,7},{7,6},{8,9},{9,8},{10,11... | collective-permute-start | bytes 1572872 | tf_op jit(solution)/shard_map/ppermute | solution.py:221
  154.3 6.7 %collective-permute-start.7 = (f32[1,512]{1,0:T(1,128)S(1)}, f32[1,512]{1,0:T(1,128)S(1)}, u32[]{:S(2)}, u32[]{:S(2)}) collective-permute-start(f32[1,512]{1,0:T(1,128)S(1)} %bitcast.29), channel_id=1, source_target_pairs={{0,1},{1,0},{2,3},{3,2},{4,5},{5,4},{6,7},{7,6},{8,9},{9,8},{10,11... | collective-permute-start | bytes 6152 | tf_op jit(solution)/shard_map/ppermute | solution.py:221
  156.1 1.5 copy-start.2
  157.6 1.0 copy-start.7
  158.7 2.4 %copy-start.5 = (bf16[1,512,896]{2,1,0:T(8,128)(2,1)S(1)}, bf16[1,512,896]{2,1,0:T(8,128)(2,1)}, u32[]{:S(2)}) copy-start(bf16[1,512,896]{2,1,0:T(8,128)(2,1)} %param.4) | copy-start | bytes 2752516
Sparse Core Ops, SparseCore 0:
  81.5 24.7 all-gather.2

commit v3 on v2

--- a/solution.py
+++ b/solution.py
@@ -20,7 +20,7 @@
 SMEM = pl.BlockSpec(memory_space=pltpu.SMEM)
 
 
-def call(kernel, outs, scratch=(), smem=0, name=None):
+def call(kernel, outs, scratch=(), smem=0, name=None, mib=12):
     def run(*args):
         return pl.pallas_call(
             kernel,
@@ -28,7 +28,7 @@
             in_specs=[SMEM] * smem + [VMEM] * (len(args) - smem),
             out_specs=[VMEM] * len(outs),
             scratch_shapes=list(scratch),
-            compiler_params=pltpu.CompilerParams(vmem_limit_bytes=48 * 2**20),
+            compiler_params=pltpu.CompilerParams(vmem_limit_bytes=mib * 2**20),
             name=name,
         )(*args)
 
@@ -155,26 +155,21 @@
             out[RR:, 256:] = gl
 
 
-def sum_kernel(own_g, own_r, one, two, three, out):
+def sum_kernel(own_g, own_r, one, two, three, piece, share):
     g, r = own_g[...], own_r[...]
     for got in (one, two, three):
         r = r + got[:RR, :].astype(F)
         g = g + (got[RR:, :256].astype(F) + got[RR:, 256:].astype(F))
     gh, gl = halves(g)
-    out[:RR, :] = r.astype(B)
-    out[RR:, :256] = gh
-    out[RR:, 256:] = gl
-
-
-def split_kernel(both, right):
-    for f in range(8):
-        right[f * RR : (f + 1) * RR, :] = both[f, :RR, :]
-
-
-def solve_kernel(both, left, right_in, w16, ortho, right, squares, a, w):
+    share[...] = r.astype(B)
+    piece[:, :256] = gh
+    piece[:, 256:] = gl
+
+
+def solve_kernel(both, left, w16, w_low, ortho, a, w):
     for f in range(8):
         y, c = divmod(f, 2)
-        g = both[f, RR:, :256].astype(F) + both[f, RR:, 256:].astype(F)
+        g = both[f * GR : (f + 1) * GR, :256].astype(F) + both[f * GR : (f + 1) * GR, 256:].astype(F)
         first = y * GR
         square = max(0, min(GR, 256 - first))
         if square:
@@ -185,10 +180,23 @@
     inverse_factor(a, w)
     wh, wl = halves(w[...])
     w16[...] = wh
+    w_low[...] = wl
     ortho[...] = (dot(left[...], wh, NT) + dot(left[...], wl, NT)).astype(B)
-    r = dot(right_in[...], wh, NT) + dot(right_in[...], wl, NT)
-    right[...] = r
-    squares[...] = jnp.sum(r * r, axis=0, keepdims=True)
+
+
+def rows_from(place, k, other_core):
+    y, c = place[0] ^ k, place[1]
+    return pl.ds(pl.multiple_of((2 * y + (1 - c if other_core else c)) * RR, 16), RR)
+
+
+def right_kernel(place, w16, w_low, s0, s1, s2, s3, right, squares):
+    acc = jnp.zeros((1, N), F)
+    for k, s in enumerate((s0, s1, s2, s3)):
+        for slot in range(2):
+            r = dot(s[slot], w16[...], NT) + dot(s[slot], w_low[...], NT)
+            right[rows_from(place, k, slot == 1), :] = r
+            acc = acc + jnp.sum(r * r, axis=0, keepdims=True)
+    squares[...] = acc
 
 
 def own_kernel(blend, ortho, right, scale, moment, basis):
@@ -197,15 +205,17 @@
     moment[...] = blend[...] - 0.05 * dot(ortho[...], r.astype(B), NT)
 
 
-def weight_kernel(side, left0, w0, right0, scale0, weight0, left1, w1, right1, scale1, weight1, own, out):
-    for k, refs in enumerate(((left0, w0, right0, scale0, weight0), (left1, w1, right1, scale1, weight1))):
-        left, w, right, scale, weight = (ref[...] for ref in refs)
+def weight_kernel(place, s0, s1, s2, s3, left0, w0, scale0, weight0, left1, w1, scale1, weight1, own, out, r_ref):
+    for half, refs in enumerate(((left0, w0, scale0, weight0), (left1, w1, scale1, weight1))):
+        left, w, scale, weight = (ref[...] for ref in refs)
         o = (dot(left, w, NT) * scale).astype(B)
-        r = dot(right, w, NT).astype(B)
-        new = (weight.astype(F) - 0.3 * dot(o, r, NT)).astype(B)
-        if k == 0:
+        for k, s in enumerate((s0, s1, s2, s3)):
+            for slot in range(2):
+                r_ref[rows_from(place, k, slot == 1), :] = dot(s[2 * half + slot], w, NT).astype(B)
+        new = (weight.astype(F) - 0.3 * dot(o, r_ref[...], NT)).astype(B)
+        if half == 0:
             own[...] = new
-        out[side[0] if k == 0 else 1 - side[0]] = new
+        out[place[2] if half == 0 else 1 - place[2]] = new
 
 
 def exchange(x, axis):
@@ -245,28 +255,39 @@
         name="join",
     )(index("y"), keep_g, keep_r, got)
     arrived = [swap(x, "y", k + 1) for k, x in enumerate(outs)]
-    (piece,) = call(sum_kernel, [((RR + GR, N), B)], name="sum")(own_g, own_r, *arrived)
-    both = lax.all_gather(piece, FSDP, axis=0, tiled=False)
-    (raw,) = call(split_kernel, [((8 * RR, N), B)], name="split")(both)
-    raw_o = swap(raw, "r")
+    piece, share = call(sum_kernel, [((GR, N), B), ((RR, N), B)], name="sum")(own_g, own_r, *arrived)
+    from_core = swap(share, "c")
+    from_other = swap(share, "r")
+    from_both = lax.ppermute(share, ("c", "r"), [(i, 3 - i) for i in range(4)])
+    gram = lax.all_gather(piece, FSDP, axis=0, tiled=True)
+    stack = [jnp.stack([share, from_core, from_other, from_both])]
+    stack += [swap(stack[0], "y", k) for k in (1, 2, 3)]
     weight, _ = lax.optimization_barrier((weights[0], left))
     weight_o = swap(weight, "r")
 
-    w16, ortho, right, squares = call(
+    w16, w_low, ortho = call(
         solve_kernel,
-        [((N, N), B), ((N, N), B), ((8 * RR, N), F), ((1, N), F)],
+        [((N, N), B)] * 3,
         [pltpu.VMEM((N, N), F), pltpu.VMEM((N, N), F)],
         name="solve",
-    )(both, left, raw)
+    )(gram, left)
     w16_o = swap(w16, "r")
+    place = jnp.concatenate([index("y"), index("c"), index("r")])
+    right, squares = call(right_kernel, [((8 * RR, N), F), ((1, N), F)], smem=1, name="right")(
+        place, w16, w_low, *stack
+    )
     scale = lax.rsqrt(jnp.sum(gather(squares, TP), axis=0, keepdims=True) / COLS + 1e-06)
     scale_o = swap(scale, "r")
     moment_new, basis_new = call(own_kernel, [(blend.shape, F), (right.shape, F)], name="own")(
         blend, ortho, right, scale
     )
     weight_new, rollout = call(
-        weight_kernel, [(weight.shape, B), ((2, *weight.shape), B)], smem=1, name="weights"
-    )(index("r"), left, w16, raw, scale, weights[0], left_o, w16_o, raw_o, scale_o, weight_o)
+        weight_kernel,
+        [(weight.shape, B), ((2, *weight.shape), B)],
+        [pltpu.VMEM((8 * RR, N), B)],
+        smem=1,
+        name="weights",
+    )(place, *stack, left, w16, scale, weights[0], left_o, w16_o, scale_o, weight_o)
     return weight_new[None], moment_new[None], basis_new[None], rollout
 
 

time: 174 us -> 185 us (1.063); the launches traced: 174 us -> 183 us
  blocking collectives: 37.6 us -> 64.6 us
  waiting for transfers between devices: 47.3 us -> 29.2 us
  between operations: 14.1 us -> 0.76 us
  starting transfers between devices: 23.3 us -> 29.8 us
  Pallas kernels: 35.7 us -> 40 us
  local copies, waits for them, and re-layouts: 10.7 us -> 12.9 us
    all_gather x0 -> x1, blocking collectives: none -> 29.6 us  [body(): gram = lax.all_gather(piece, FSDP, axis=0, tiled=True)]
    all_gather x1 -> x0, waiting for transfers between devices: 22.4 us -> none  [body(): both = lax.all_gather(piece, FSDP, axis=0, tiled=False)]
    pallas_call x7, Pallas kernels: 35.7 us -> 40 us  [run(): pl.pallas_call(kernel, out_shape=[jax.ShapeDtypeStruct(s, d) for s, d in...]
    ppermute x9 -> x13, starting transfers between devices: 17.3 us -> 21.4 us  [swap(): lax.ppermute(x, axis, [(i, i ^ bit) for i in range(lax.axis_size(axis))])]
    ppermute x0 -> x1, waiting for transfers between devices: none -> 3.91 us  [body(): from_both = lax.ppermute(share, ('c', 'r'), [(i, 3 - i) for i in range(4)])]
    all_to_all x2, blocking collectives: 37.6 us -> 35 us  [exchange(): return lax.all_to_all(x, axis, 0, 0, tiled=True)]
    ppermute x0 -> x1, starting transfers between devices: none -> 2.38 us  [body(): from_both = lax.ppermute(share, ('c', 'r'), [(i, 3 - i) for i in range(4)])]
    unnamed x20 -> x26, local copies, waits for them, and re-layouts: 9.85 us -> 12 us
  transfers between devices with their start and end apart: 11 -> 15, of which waited for: 6 -> 7; matrix products, arithmetic and copies ran while one was open for 1% -> 1% of each run, Pallas kernels for 16% -> 16%
where the time goes in v3:
time: 185 us; the launch traced here: 183 us
  blocking collectives  64.6 us (35%)
  Pallas kernels  40 us (22%)
  starting transfers between devices  29.8 us (16%)
  waiting for transfers between devices  29.2 us (16%)
  local copies, waits for them, and re-layouts  12.9 us (7%)
  matrix products  3.06 us (2%)
  other arithmetic  2.2 us (1%)
    pallas_call x7, Pallas kernels, run(): pl.pallas_call(kernel, out_shape=[jax.ShapeDtypeStruct(s, d) for s, d in...  40 us
    all_to_all x2, blocking collectives, exchange(): return lax.all_to_all(x, axis, 0, 0, tiled=True)  35 us
    all_gather x1, blocking collectives, body(): gram = lax.all_gather(piece, FSDP, axis=0, tiled=True)  29.6 us
    ppermute x13, starting transfers between devices, swap(): lax.ppermute(x, axis, [(i, i ^ bit) for i in range(lax.axis_size(axis))])  21.4 us
    ppermute x13, waiting for transfers between devices, swap(): lax.ppermute(x, axis, [(i, i ^ bit) for i in range(lax.axis_size(axis))])  14.3 us
    unnamed x26, local copies, waits for them, and re-layouts  12 us
    all_to_all x1, waiting for transfers between devices, exchange(): return lax.all_to_all(x, axis, 0, 0, tiled=True)  11 us
    all_to_all x1, starting transfers between devices, exchange(): return lax.all_to_all(x, axis, 0, 0, tiled=True)  5.96 us
  transfers between devices with their start and end apart: 15, of which 7 were waited for; matrix products, arithmetic and copies ran while one was open for 1% of the time, Pallas kernels for 16%

profile of v3, /device:TPU:1, one launch (start us, length us, event | category | flops | bytes accessed | tf_op | source)
XLA Modules:
  0.0 182.5 jit_solution(4587508826017299624)
XLA Ops:
  0.6 3.1 %convolution_convert_fusion = bf16[512,512]{1,0:T(8,128)(2,1)S(1)} fusion(f32[1,512,896]{2,1,0:T(8,128)} %param.6, bf16[1,512,896]{2,1,0:T(8,128)(2,1)} %param.5, f32[1,896,512]{2,1,0:T(8,128)} %param.7), kind=kOutput, calls=%fused_computation.1 | convolution fusion | flops 471859200 | bytes 5111808 | tf_op jit(solution)/shard_map/dot_general | solution.py:39
  3.7 23.6 %all_to_all.15 = bf16[16,32,512]{2,1,0:T(8,128)(2,1)S(1)} all-to-all(bf16[16,32,512]{2,1,0:T(8,128)(2,1)S(1)} %bitcast.33), channel_id=1, replica_groups=mesh['y'=4,'c'=2,'x'=2,'z'=8,'r'=2] {'x','z'}, dimensions={0} | all-to-all | bytes 1048576 | tf_op jit(solution)/shard_map/all_to_all | solution.py:222
  28.2 6.0 %all-to-all-start.1 = ((bf16[16,32,512]{2,1,0:T(8,128)(2,1)}), bf16[16,32,512]{2,1,0:T(8,128)(2,1)S(1)}, u32[]{:S(2)}, u32[]{:S(2)}) async-start(bf16[16,32,512]{2,1,0:T(8,128)(2,1)} %broadcast_in_dim.24), calls=%async_computation.1 | async-start | bytes 1048576 | tf_op jit(solution)/shard_map/all_to_all | solution.py:222
  34.2 1.9 %fusion.6 = (bf16[512,896]{1,0:T(8,128)(2,1)S(1)}, f32[512,896]{1,0:T(8,128)S(1)}) fusion(f32[1,512,896]{2,1,0:T(8,128)} %param.6, bf16[1,512,896]{2,1,0:T(8,128)(2,1)} %param.5), kind=kLoop, calls=%fused_computation.10 | loop fusion | flops 1376256 | bytes 5505024 | tf_op jit(solution)/shard_map/convert_element_type | solution.py:237
  36.1 11.0 %all-to-all-done.1 = bf16[16,32,512]{2,1,0:T(8,128)(2,1)S(1)} async-done(((bf16[16,32,512]{2,1,0:T(8,128)(2,1)}), bf16[16,32,512]{2,1,0:T(8,128)(2,1)S(1)}, u32[]{:S(2)}, u32[]{:S(2)}) %all-to-all-start.1) | async-done | bytes 524320 | tf_op jit(solution)/shard_map/all_to_all | solution.py:222
  47.1 1.8 pieces.1
  50.6 3.1 %collective-permute-start = (bf16[4,208,512]{2,1,0:T(8,128)(2,1)}, bf16[4,208,512]{2,1,0:T(8,128)(2,1)S(1)}, u32[]{:S(2)}, u32[]{:S(2)}) collective-permute-start(bf16[4,208,512]{2,1,0:T(8,128)(2,1)} %get-tuple-element.26), channel_id=1, source_target_pairs={{0,32},{32,0},{1,33},{33,1},{2,34},{34,2},{3,35},{35,3},{4,36},{36... | collective-permute-start | bytes 2555912 | tf_op jit(solution)/shard_map/ppermute | solution.py:231
  53.7 2.2 %collective-permute-done.got = bf16[4,208,512]{2,1,0:T(8,128)(2,1)S(1)} collective-permute-done((bf16[4,208,512]{2,1,0:T(8,128)(2,1)}, bf16[4,208,512]{2,1,0:T(8,128)(2,1)S(1)}, u32[]{:S(2)}, u32[]{:S(2)}) %collective-permute-start) | collective-permute-done | bytes 852000 | tf_op jit(solution)/shard_map/ppermute | solution.py:231
  55.9 1.2 copy-done.6
  58.3 1.4 collective-permute-start.1
  59.7 2.6 %collective-permute-start.2 = (bf16[208,512]{1,0:T(8,128)(2,1)S(1)}, bf16[208,512]{1,0:T(8,128)(2,1)S(1)}, u32[]{:S(2)}, u32[]{:S(2)}) collective-permute-start(bf16[208,512]{1,0:T(8,128)(2,1)S(1)} %get-tuple-element.30), channel_id=1, source_target_pairs={{0,128},{64,192},{128,0},{192,64},{1,129},{65,193},{129,1},{193,65... | collective-permute-start | bytes 638984 | tf_op jit(solution)/shard_map/ppermute | solution.py:231
  62.3 2.5 %collective-permute-done.1.one = bf16[208,512]{1,0:T(8,128)(2,1)S(1)} collective-permute-done((bf16[208,512]{1,0:T(8,128)(2,1)S(1)}, bf16[208,512]{1,0:T(8,128)(2,1)S(1)}, u32[]{:S(2)}, u32[]{:S(2)}) %collective-permute-start.1) | collective-permute-done | bytes 213024 | tf_op jit(solution)/shard_map/ppermute | solution.py:231
  64.8 7.1 %collective-permute-done.2.two = bf16[208,512]{1,0:T(8,128)(2,1)S(1)} collective-permute-done((bf16[208,512]{1,0:T(8,128)(2,1)S(1)}, bf16[208,512]{1,0:T(8,128)(2,1)S(1)}, u32[]{:S(2)}, u32[]{:S(2)}) %collective-permute-start.2) | collective-permute-done | bytes 213024 | tf_op jit(solution)/shard_map/ppermute | solution.py:231
  71.9 2.1 %collective-permute-done.3.three = bf16[208,512]{1,0:T(8,128)(2,1)S(1)} collective-permute-done((bf16[208,512]{1,0:T(8,128)(2,1)S(1)}, bf16[208,512]{1,0:T(8,128)(2,1)S(1)}, u32[]{:S(2)}, u32[]{:S(2)}) %collective-permute-start.3) | collective-permute-done | bytes 213024 | tf_op jit(solution)/shard_map/ppermute | solution.py:231
  74.2 2.5 %collective-permute-start.5 = (bf16[112,512]{1,0:T(8,128)(2,1)S(1)}, bf16[112,512]{1,0:T(8,128)(2,1)S(1)}, u32[]{:S(2)}, u32[]{:S(2)}) collective-permute-start(bf16[112,512]{1,0:T(8,128)(2,1)S(1)} %get-tuple-element.32), channel_id=1, source_target_pairs={{0,1},{1,0},{2,3},{3,2},{4,5},{5,4},{6,7},{7,6},{8,9},{9,8},{10,11... | collective-permute-start | bytes 344072 | tf_op jit(solution)/shard_map/ppermute | solution.py:231
  76.7 2.4 %collective-permute-start.6 = (bf16[112,512]{1,0:T(8,128)(2,1)S(1)}, bf16[112,512]{1,0:T(8,128)(2,1)S(1)}, u32[]{:S(2)}, u32[]{:S(2)}) collective-permute-start(bf16[112,512]{1,0:T(8,128)(2,1)S(1)} %get-tuple-element.32), channel_id=1, source_target_pairs={{0,33},{1,32},{32,1},{33,0},{2,35},{3,34},{34,3},{35,2},{4,37},{5,... | collective-permute-start | bytes 344072 | tf_op jit(solution)/shard_map/ppermute | solution.py:261
  79.4 3.9 %collective-permute-done.6 = bf16[112,512]{1,0:T(8,128)(2,1)S(1)} collective-permute-done((bf16[112,512]{1,0:T(8,128)(2,1)S(1)}, bf16[112,512]{1,0:T(8,128)(2,1)S(1)}, u32[]{:S(2)}, u32[]{:S(2)}) %collective-permute-start.6) | collective-permute-done | bytes 114720 | tf_op jit(solution)/shard_map/ppermute | solution.py:261
  83.5 3.2 %collective-permute-start.13 = (bf16[512,896]{1,0:T(8,128)(2,1)}, bf16[512,896]{1,0:T(8,128)(2,1)}, u32[]{:S(2)}, u32[]{:S(2)}) collective-permute-start(bf16[512,896]{1,0:T(8,128)(2,1)} %bitcast.14.weight0), channel_id=1, source_target_pairs={{0,1},{1,0},{2,3},{3,2},{4,5},{5,4},{6,7},{7,6},{8,9},{9,8},{10,11... | collective-permute-start | bytes 2752520 | tf_op jit(solution)/shard_map/ppermute | solution.py:231
  86.8 1.0 collective-permute-start.8
  87.8 2.7 %collective-permute-start.9 = (bf16[4,112,512]{2,1,0:T(8,128)(2,1)S(1)}, bf16[4,112,512]{2,1,0:T(8,128)(2,1)}, u32[]{:S(2)}, u32[]{:S(2)}) collective-permute-start(bf16[4,112,512]{2,1,0:T(8,128)(2,1)S(1)} %pad_maximum_fusion.s0), channel_id=1, source_target_pairs={{0,192},{64,128},{128,64},{192,0},{1,193},{65,129},{129,65},{193,1... | collective-permute-start | bytes 1376264 | tf_op jit(solution)/shard_map/ppermute | solution.py:231
  90.5 29.6 %all_gather.3.both = bf16[768,512]{1,0:T(8,128)(2,1)S(1)} all-gather(bf16[96,512]{1,0:T(8,128)(2,1)S(1)} %get-tuple-element.33), channel_id=1, replica_groups=mesh['y'=4,'c'=2,'x'=2,'z'=8,'r'=2] {'y','c'}, dimensions={0}, use_global_device_ids=true | all-gather | bytes 884736 | tf_op jit(solution)/shard_map/all_gather | solution.py:262
  120.1 23.7 %solve.1 = (bf16[512,512]{1,0:T(8,128)(2,1)S(1)}, bf16[512,512]{1,0:T(8,128)(2,1)S(1)}, bf16[512,512]{1,0:T(8,128)(2,1)S(1)}) custom-call(bf16[768,512]{1,0:T(8,128)(2,1)S(1)} %all_gather.3.both, bf16[512,512]{1,0:T(8,128)(2,1)S(1)} %bitcast.26), custom_call_target="tpu_custom_call" | custom-call | tf_op jit(solution)/shard_map/solve/pallas_call | solution.py:25
  146.2 2.9 %collective-permute-start.11 = (bf16[512,512]{1,0:T(8,128)(2,1)S(1)}, bf16[512,512]{1,0:T(8,128)(2,1)}, u32[]{:S(2)}, u32[]{:S(2)}) collective-permute-start(bf16[512,512]{1,0:T(8,128)(2,1)S(1)} %get-tuple-element.34.w16.w0), channel_id=1, source_target_pairs={{0,1},{1,0},{2,3},{3,2},{4,5},{5,4},{6,7},{7,6},{8,9},{9,8},{10,11... | collective-permute-start | bytes 1572872 | tf_op jit(solution)/shard_map/ppermute | solution.py:231
  150.2 1.0 copy-done.8
  151.3 3.9 %right.1 = (f32[896,512]{1,0:T(8,128)S(1)}, f32[1,512]{1,0:T(1,128)S(1)}) custom-call(s32[3]{0:T(128)S(1)} %pad_add_fusion.place, bf16[512,512]{1,0:T(8,128)(2,1)S(1)} %get-tuple-element.34.w16.w0, bf16[512,512]{1,0:T(8,128)(2,1)S(1)} %copy-done.8, bf16[4,112,512]{2,1,0:T(8,128)(2,1)S(1)} %pad_maximum_fusion.s0, bf16[4,112,512]{2,1,0:T(8,128)(2,1)S(1)} %copy-done.3, ...), custom_call_target="tpu_custom_call" | custom-call | tf_op jit(solution)/shard_map/right/pallas_call | solution.py:25
  155.2 1.2 copy-done
  156.4 11.4 %all_to_all.16 = f32[16,1,512]{2,1,0:T(1,128)S(1)} all-to-all(f32[16,1,512]{2,1,0:T(1,128)S(1)} %broadcast_in_dim.26), channel_id=1, replica_groups=mesh['y'=4,'c'=2,'x'=2,'z'=8,'r'=2] {'x','z'}, dimensions={0} | all-to-all | bytes 65536 | tf_op jit(solution)/shard_map/all_to_all | solution.py:222
  167.9 1.7 collective-permute-start.12
  169.6 1.5 copy-done.1
  171.1 1.0 copy-done.10
  172.1 2.3 %own.1 = (f32[512,896]{1,0:T(8,128)}, f32[896,512]{1,0:T(8,128)}) custom-call(f32[512,896]{1,0:T(8,128)S(1)} %get-tuple-element.45.blend, bf16[512,512]{1,0:T(8,128)(2,1)S(1)} %copy-done.10, f32[896,512]{1,0:T(8,128)S(1)} %copy-done.1, f32[1,512]{1,0:T(1,128)S(1)} %bitcast.30), custom_call_target="tpu_custom_call" | custom-call | tf_op jit(solution)/shard_map/own/pallas_call | solution.py:25
  174.5 8.0 %weights.1 = (bf16[512,896]{1,0:T(8,128)(2,1)}, bf16[2,512,896]{2,1,0:T(8,128)(2,1)}) custom-call(s32[3]{0:T(128)S(1)} %pad_add_fusion.place, bf16[4,112,512]{2,1,0:T(8,128)(2,1)S(1)} %pad_maximum_fusion.s0, bf16[4,112,512]{2,1,0:T(8,128)(2,1)S(1)} %copy-done.4, bf16[4,112,512]{2,1,0:T(8,128)(2,1)} %collective-permute-done.8.s2, ...), custom_call_target="tpu_custom_call" | custom-call | tf_op jit(solution)/shard_map/weights/pallas_call | solution.py:25
  (43 shorter events, 8.0 us)
Async XLA Ops:
  28.2 18.9 %all-to-all-start.1 = ((bf16[16,32,512]{2,1,0:T(8,128)(2,1)}), bf16[16,32,512]{2,1,0:T(8,128)(2,1)S(1)}, u32[]{:S(2)}, u32[]{:S(2)}) async-start(bf16[16,32,512]{2,1,0:T(8,128)(2,1)} %broadcast_in_dim.24), calls=%async_computation.1 | async-start | bytes 1048576 | tf_op jit(solution)/shard_map/all_to_all | solution.py:222
  48.9 0.9 copy-start.5
  49.9 0.7 copy-start.11
  50.6 5.3 %collective-permute-start = (bf16[4,208,512]{2,1,0:T(8,128)(2,1)}, bf16[4,208,512]{2,1,0:T(8,128)(2,1)S(1)}, u32[]{:S(2)}, u32[]{:S(2)}) collective-permute-start(bf16[4,208,512]{2,1,0:T(8,128)(2,1)} %get-tuple-element.26), channel_id=1, source_target_pairs={{0,32},{32,0},{1,33},{33,1},{2,34},{34,2},{3,35},{35,3},{4,36},{36... | collective-permute-start | bytes 2555912 | tf_op jit(solution)/shard_map/ppermute | solution.py:231
  55.9 1.2 copy-start.6
  57.1 1.0 copy-start.12
  58.3 6.6 %collective-permute-start.1 = (bf16[208,512]{1,0:T(8,128)(2,1)S(1)}, bf16[208,512]{1,0:T(8,128)(2,1)S(1)}, u32[]{:S(2)}, u32[]{:S(2)}) collective-permute-start(bf16[208,512]{1,0:T(8,128)(2,1)S(1)} %get-tuple-element.29), channel_id=1, source_target_pairs={{0,64},{64,0},{128,192},{192,128},{1,65},{65,1},{129,193},{193,129... | collective-permute-start | bytes 638984 | tf_op jit(solution)/shard_map/ppermute | solution.py:231
  59.7 12.2 %collective-permute-start.2 = (bf16[208,512]{1,0:T(8,128)(2,1)S(1)}, bf16[208,512]{1,0:T(8,128)(2,1)S(1)}, u32[]{:S(2)}, u32[]{:S(2)}) collective-permute-start(bf16[208,512]{1,0:T(8,128)(2,1)S(1)} %get-tuple-element.30), channel_id=1, source_target_pairs={{0,128},{64,192},{128,0},{192,64},{1,129},{65,193},{129,1},{193,65... | collective-permute-start | bytes 638984 | tf_op jit(solution)/shard_map/ppermute | solution.py:231
  62.3 11.8 %collective-permute-start.3 = (bf16[208,512]{1,0:T(8,128)(2,1)S(1)}, bf16[208,512]{1,0:T(8,128)(2,1)S(1)}, u32[]{:S(2)}, u32[]{:S(2)}) collective-permute-start(bf16[208,512]{1,0:T(8,128)(2,1)S(1)} %get-tuple-element.31), channel_id=1, source_target_pairs={{0,192},{64,128},{128,64},{192,0},{1,193},{65,129},{129,65},{193,1... | collective-permute-start | bytes 638984 | tf_op jit(solution)/shard_map/ppermute | solution.py:231
  74.2 5.2 %collective-permute-start.5 = (bf16[112,512]{1,0:T(8,128)(2,1)S(1)}, bf16[112,512]{1,0:T(8,128)(2,1)S(1)}, u32[]{:S(2)}, u32[]{:S(2)}) collective-permute-start(bf16[112,512]{1,0:T(8,128)(2,1)S(1)} %get-tuple-element.32), channel_id=1, source_target_pairs={{0,1},{1,0},{2,3},{3,2},{4,5},{5,4},{6,7},{7,6},{8,9},{9,8},{10,11... | collective-permute-start | bytes 344072 | tf_op jit(solution)/shard_map/ppermute | solution.py:231
  76.7 6.6 %collective-permute-start.6 = (bf16[112,512]{1,0:T(8,128)(2,1)S(1)}, bf16[112,512]{1,0:T(8,128)(2,1)S(1)}, u32[]{:S(2)}, u32[]{:S(2)}) collective-permute-start(bf16[112,512]{1,0:T(8,128)(2,1)S(1)} %get-tuple-element.32), channel_id=1, source_target_pairs={{0,33},{1,32},{32,1},{33,0},{2,35},{3,34},{34,3},{35,2},{4,37},{5,... | collective-permute-start | bytes 344072 | tf_op jit(solution)/shard_map/ppermute | solution.py:261
  79.1 4.2 %collective-permute-start.4 = (bf16[112,512]{1,0:T(8,128)(2,1)S(1)}, bf16[112,512]{1,0:T(8,128)(2,1)S(1)}, u32[]{:S(2)}, u32[]{:S(2)}) collective-permute-start(bf16[112,512]{1,0:T(8,128)(2,1)S(1)} %get-tuple-element.32), channel_id=1, source_target_pairs={{0,32},{32,0},{1,33},{33,1},{2,34},{34,2},{3,35},{35,3},{4,36},{36... | collective-permute-start | bytes 344072 | tf_op jit(solution)/shard_map/ppermute | solution.py:231
  83.4 62.0 %collective-permute-start.7 = (bf16[4,112,512]{2,1,0:T(8,128)(2,1)S(1)}, bf16[4,112,512]{2,1,0:T(8,128)(2,1)S(1)}, u32[]{:S(2)}, u32[]{:S(2)}) collective-permute-start(bf16[4,112,512]{2,1,0:T(8,128)(2,1)S(1)} %pad_maximum_fusion.s0), channel_id=1, source_target_pairs={{0,64},{64,0},{128,192},{192,128},{1,65},{65,1},{129,193},{193,129... | collective-permute-start | bytes 1376264 | tf_op jit(solution)/shard_map/ppermute | solution.py:231
  83.5 91.0 %collective-permute-start.13 = (bf16[512,896]{1,0:T(8,128)(2,1)}, bf16[512,896]{1,0:T(8,128)(2,1)}, u32[]{:S(2)}, u32[]{:S(2)}) collective-permute-start(bf16[512,896]{1,0:T(8,128)(2,1)} %bitcast.14.weight0), channel_id=1, source_target_pairs={{0,1},{1,0},{2,3},{3,2},{4,5},{5,4},{6,7},{7,6},{8,9},{9,8},{10,11... | collective-permute-start | bytes 2752520 | tf_op jit(solution)/shard_map/ppermute | solution.py:231
  86.7 87.8 %collective-permute-start.10 = (bf16[512,512]{1,0:T(8,128)(2,1)S(1)}, bf16[512,512]{1,0:T(8,128)(2,1)}, u32[]{:S(2)}, u32[]{:S(2)}) collective-permute-start(bf16[512,512]{1,0:T(8,128)(2,1)S(1)} %bitcast.25), channel_id=1, source_target_pairs={{0,1},{1,0},{2,3},{3,2},{4,5},{5,4},{6,7},{7,6},{8,9},{9,8},{10,11... | collective-permute-start | bytes 1572872 | tf_op jit(solution)/shard_map/ppermute | solution.py:231
  86.8 62.4 %collective-permute-start.8 = (bf16[4,112,512]{2,1,0:T(8,128)(2,1)S(1)}, bf16[4,112,512]{2,1,0:T(8,128)(2,1)}, u32[]{:S(2)}, u32[]{:S(2)}) collective-permute-start(bf16[4,112,512]{2,1,0:T(8,128)(2,1)S(1)} %pad_maximum_fusion.s0), channel_id=1, source_target_pairs={{0,128},{64,192},{128,0},{192,64},{1,129},{65,193},{129,1},{193,65... | collective-permute-start | bytes 1376264 | tf_op jit(solution)/shard_map/ppermute | solution.py:231
  87.8 61.4 %collective-permute-start.9 = (bf16[4,112,512]{2,1,0:T(8,128)(2,1)S(1)}, bf16[4,112,512]{2,1,0:T(8,128)(2,1)}, u32[]{:S(2)}, u32[]{:S(2)}) collective-permute-start(bf16[4,112,512]{2,1,0:T(8,128)(2,1)S(1)} %pad_maximum_fusion.s0), channel_id=1, source_target_pairs={{0,192},{64,128},{128,64},{192,0},{1,193},{65,129},{129,65},{193,1... | collective-permute-start | bytes 1376264 | tf_op jit(solution)/shard_map/ppermute | solution.py:231
  143.8 0.8 copy-start.7
  144.6 0.8 copy-start.9
  145.4 0.8 copy-start.2
  146.2 28.3 %collective-permute-start.11 = (bf16[512,512]{1,0:T(8,128)(2,1)S(1)}, bf16[512,512]{1,0:T(8,128)(2,1)}, u32[]{:S(2)}, u32[]{:S(2)}) collective-permute-start(bf16[512,512]{1,0:T(8,128)(2,1)S(1)} %get-tuple-element.34.w16.w0), channel_id=1, source_target_pairs={{0,1},{1,0},{2,3},{3,2},{4,5},{5,4},{6,7},{7,6},{8,9},{9,8},{10,11... | collective-permute-start | bytes 1572872 | tf_op jit(solution)/shard_map/ppermute | solution.py:231
  149.2 1.0 copy-start.3
  150.2 1.0 copy-start.8
  155.2 1.2 copy-start
  167.9 6.6 %collective-permute-start.12 = (f32[1,512]{1,0:T(1,128)S(1)}, f32[1,512]{1,0:T(1,128)S(1)}, u32[]{:S(2)}, u32[]{:S(2)}) collective-permute-start(f32[1,512]{1,0:T(1,128)S(1)} %bitcast.29), channel_id=1, source_target_pairs={{0,1},{1,0},{2,3},{3,2},{4,5},{5,4},{6,7},{7,6},{8,9},{9,8},{10,11... | collective-permute-start | bytes 6152 | tf_op jit(solution)/shard_map/ppermute | solution.py:231
  169.6 1.5 copy-start.1
  171.1 1.0 copy-start.10
  172.1 2.4 %copy-start.4 = (bf16[4,112,512]{2,1,0:T(8,128)(2,1)S(1)}, bf16[4,112,512]{2,1,0:T(8,128)(2,1)}, u32[]{:S(2)}) copy-start(bf16[4,112,512]{2,1,0:T(8,128)(2,1)} %copy-done.2) | copy-start | bytes 1376260

commit v4 on v2

--- a/solution.py
+++ b/solution.py
@@ -20,15 +20,15 @@
 SMEM = pl.BlockSpec(memory_space=pltpu.SMEM)
 
 
-def call(kernel, outs, scratch=(), smem=0, name=None):
+def call(kernel, outs, scratch=(), smem=0, name=None, mib=12, out_spec=VMEM):
     def run(*args):
         return pl.pallas_call(
             kernel,
             out_shape=[jax.ShapeDtypeStruct(s, d) for s, d in outs],
             in_specs=[SMEM] * smem + [VMEM] * (len(args) - smem),
-            out_specs=[VMEM] * len(outs),
+            out_specs=[out_spec] * len(outs),
             scratch_shapes=list(scratch),
-            compiler_params=pltpu.CompilerParams(vmem_limit_bytes=48 * 2**20),
+            compiler_params=pltpu.CompilerParams(vmem_limit_bytes=mib * 2**20),
             name=name,
         )(*args)
 
@@ -119,10 +119,19 @@
             w_ref[hi:, lo:hi] = -upd[:, lo:]
 
 
-def pieces_kernel(core, left_ref, blend_ref, keep_g, keep_r, send, right_scr, part):
+def spread_kernel(pieces, out):
+    share = pieces[0].astype(F)
+    for k in range(1, pieces.shape[0]):
+        share = share + pieces[k].astype(F)
+    share = share.astype(B)
+    for k in range(out.shape[0]):
+        out[k] = share
+
+
+def pieces_kernel(place, left_ref, blend_ref, keep_g, keep_r, send, right_scr, part):
     right_scr[...] = dot(blend_ref[...], left_ref[...], TN)
     for mine in (True, False):
-        c = core[0] if mine else 1 - core[0]
+        c = place[1] if mine else 1 - place[1]
         wide = left_ref[:, pl.ds(pl.multiple_of(c * 256, 256), 256)]
         narrow = left_ref[:, pl.ds(pl.multiple_of(c * 128, 128), 128)]
         part[:256, :] = dot(wide, wide, TN)
@@ -134,54 +143,63 @@
                 keep_g[y] = g
                 keep_r[y] = r
             else:
-                gh, gl = halves(g)
-                send[y, :RR, :] = r.astype(B)
-                send[y, RR:, :256] = gh
-                send[y, RR:, 256:] = gl
-
-
-def join_kernel(line, keep_g, keep_r, got, own_g, own_r, one, two, three):
+                packed(send.at[y], g, r)
+
+
+def packed(out, g, r):
+    gh, gl = halves(g)
+    out[:RR, :] = r.astype(B)
+    out[RR:, :256] = gh
+    out[RR:, 256:] = gl
+
+
+def gram_of(ref):
+    return ref[RR:, :256].astype(F) + ref[RR:, 256:].astype(F)
+
+
+def join_kernel(place, keep_g, keep_r, got, own_g, own_r, one, two, three):
     for k, out in enumerate((None, one, two, three)):
-        y = line[0] ^ k
+        y = place[0] ^ k
         r = keep_r[y] + got[y, :RR, :].astype(F)
-        g = keep_g[y] + (got[y, RR:, :256].astype(F) + got[y, RR:, 256:].astype(F))
+        g = keep_g[y] + gram_of(got.at[y])
         if out is None:
             own_g[...] = g
             own_r[...] = r
         else:
-            gh, gl = halves(g)
-            out[:RR, :] = r.astype(B)
-            out[RR:, :256] = gh
-            out[RR:, 256:] = gl
+            packed(out, g, r)
 
 
 def sum_kernel(own_g, own_r, one, two, three, out):
     g, r = own_g[...], own_r[...]
     for got in (one, two, three):
         r = r + got[:RR, :].astype(F)
-        g = g + (got[RR:, :256].astype(F) + got[RR:, 256:].astype(F))
-    gh, gl = halves(g)
-    out[:RR, :] = r.astype(B)
-    out[RR:, :256] = gh
-    out[RR:, 256:] = gl
-
-
-def split_kernel(both, right):
-    for f in range(8):
-        right[f * RR : (f + 1) * RR, :] = both[f, :RR, :]
-
-
-def solve_kernel(both, left, right_in, w16, ortho, right, squares, a, w):
-    for f in range(8):
-        y, c = divmod(f, 2)
-        g = both[f, RR:, :256].astype(F) + both[f, RR:, 256:].astype(F)
+        g = g + gram_of(got)
+    packed(out, g, r)
+
+
+def line_kernel(place, own, one, two, three, out):
+    for k, got in enumerate((own, one, two, three)):
+        out[place[0] ^ k] = got[...]
+
+
+def rows_kernel(place, own, got, right):
+    for y in range(4):
+        for c, part in ((place[1], own), (1 - place[1], got)):
+            right[pl.ds(pl.multiple_of((2 * y + c) * RR, 16), RR), :] = part[y, :RR, :]
+
+
+def solve_kernel(place, own, got, left, right_in, w16, ortho, right, squares, a, w):
+    for y in range(4):
         first = y * GR
         square = max(0, min(GR, 256 - first))
-        if square:
-            a[c * 256 + first : c * 256 + first + square, c * 256 : c * 256 + 256] = g[:square, :]
-        if square < GR:
-            at = c * 128 + first + square - 256
-            a[at : at + GR - square, 256:] = g[square:, :]
+        for c, part in ((place[1], own), (1 - place[1], got)):
+            g = gram_of(part.at[y])
+            if square:
+                rows = pl.ds(pl.multiple_of(c * 256 + first, 32), square)
+                a[rows, pl.ds(pl.multiple_of(c * 256, 256), 256)] = g[:square, :]
+            if square < GR:
+                rows = pl.ds(pl.multiple_of(c * 128 + first + square - 256, 32), GR - square)
+                a[rows, 256:] = g[square:, :]
     inverse_factor(a, w)
     wh, wl = halves(w[...])
     w16[...] = wh
@@ -191,43 +209,51 @@
     squares[...] = jnp.sum(r * r, axis=0, keepdims=True)
 
 
-def own_kernel(blend, ortho, right, scale, moment, basis):
-    r = right[...]
-    basis[...] = r * scale[...]
-    moment[...] = blend[...] - 0.05 * dot(ortho[...], r.astype(B), NT)
-
-
-def weight_kernel(side, left0, w0, right0, scale0, weight0, left1, w1, right1, scale1, weight1, own, out):
-    for k, refs in enumerate(((left0, w0, right0, scale0, weight0), (left1, w1, right1, scale1, weight1))):
-        left, w, right, scale, weight = (ref[...] for ref in refs)
-        o = (dot(left, w, NT) * scale).astype(B)
-        r = dot(right, w, NT).astype(B)
-        new = (weight.astype(F) - 0.3 * dot(o, r, NT)).astype(B)
-        if k == 0:
-            own[...] = new
-        out[side[0] if k == 0 else 1 - side[0]] = new
+def last_kernel(
+    place, sums, momentum, gradient, ortho, right, left0, w0, right0, weight0, left1, w1, right1, weight1,
+    out_weight, out_moment, out_basis, out_rollout, weight, moment, basis, sems,
+):
+    scales = lax.rsqrt(jnp.sum(sums[...], axis=0) / COLS + 1e-06)
+    first = place[2] == 0
+    scale = [jnp.where(first, scales[0:1], scales[1:2]), jnp.where(first, scales[1:2], scales[0:1])]
+    basis[...] = right[...] * scale[0]
+    copies = [pltpu.make_async_copy(basis, out_basis, sems.at[0])]
+    copies[-1].start()
+    blend = momentum[...] + gradient[...].astype(F)
+    moment[...] = blend - 0.05 * dot(ortho[...], right[...].astype(B), NT)
+    copies.append(pltpu.make_async_copy(moment, out_moment, sems.at[1]))
+    copies[-1].start()
+    for half, refs in enumerate(((left0, w0, right0, weight0), (left1, w1, right1, weight1))):
+        left, w, raw, old = (ref[...] for ref in refs)
+        o = (dot(left, w, NT) * scale[half]).astype(B)
+        r = dot(raw, w, NT).astype(B)
+        weight[half] = (old.astype(F) - 0.3 * dot(o, r, NT)).astype(B)
+        side = place[2] if half == 0 else 1 - place[2]
+        copies.append(pltpu.make_async_copy(weight.at[half], out_rollout.at[side], sems.at[2 + half]))
+        copies[-1].start()
+        if half == 0:
+            copies.append(pltpu.make_async_copy(weight.at[0], out_weight, sems.at[4]))
+            copies[-1].start()
+    for copy in copies:
+        copy.wait()
 
 
 def exchange(x, axis):
     return lax.all_to_all(x, axis, 0, 0, tiled=True)
 
 
-def gather(x, axis):
-    count = lax.axis_size(axis)
-    return exchange(jnp.broadcast_to(x[None], (count, *x.shape)), axis).reshape(-1, x.shape[-1])
-
-
 def swap(x, axis, bit=1):
     return lax.ppermute(x, axis, [(i, i ^ bit) for i in range(lax.axis_size(axis))])
 
 
 def body(weights, gradient, momentum, basis):
-    index = lambda axis: lax.axis_index(axis).astype(jnp.int32).reshape(1)
-    blend = momentum[0] + gradient[0].astype(F)
-    blend16 = blend.astype(B)
+    place = jnp.stack([lax.axis_index(axis) for axis in ("y", "c", "r")]).astype(jnp.int32)
+    place, basis = lax.optimization_barrier((place, basis))
+    momentum, gradient = momentum[0], gradient[0]
+    blend16 = (momentum + gradient.astype(F)).astype(B)
     part = dot(blend16, basis[0].astype(B), NN).astype(B).reshape(16, -1, N)
-    share = jnp.sum(exchange(part, TP).astype(F), axis=0).astype(B)
-    left = gather(share, TP)
+    (copies,) = call(spread_kernel, [(part.shape, B)], name="spread")(exchange(part, TP))
+    left = exchange(copies, TP).reshape(-1, N)
 
     keep_g, keep_r, send = call(
         pieces_kernel,
@@ -235,20 +261,23 @@
         [pltpu.VMEM((8 * RR, N), F), pltpu.VMEM((384, 256), F)],
         smem=1,
         name="pieces",
-    )(index("c"), left, blend16)
+    )(place, left, blend16)
     got = swap(send, "c")
-    left_o = swap(left, "r")
     own_g, own_r, *outs = call(
         join_kernel,
         [((GR, 256), F), ((RR, N), F)] + [((RR + GR, N), B)] * 3,
         smem=1,
         name="join",
-    )(index("y"), keep_g, keep_r, got)
+    )(place, keep_g, keep_r, got)
     arrived = [swap(x, "y", k + 1) for k, x in enumerate(outs)]
     (piece,) = call(sum_kernel, [((RR + GR, N), B)], name="sum")(own_g, own_r, *arrived)
-    both = lax.all_gather(piece, FSDP, axis=0, tiled=False)
-    (raw,) = call(split_kernel, [((8 * RR, N), B)], name="split")(both)
+    (line,) = call(line_kernel, [((4, RR + GR, N), B)], smem=1, name="line")(
+        place, piece, *[swap(piece, "y", k) for k in (1, 2, 3)]
+    )
+    other_core = swap(line, "c")
+    (raw,) = call(rows_kernel, [((8 * RR, N), B)], smem=1, name="rows")(place, line, other_core)
     raw_o = swap(raw, "r")
+    left_o = swap(left, "r")
     weight, _ = lax.optimization_barrier((weights[0], left))
     weight_o = swap(weight, "r")
 
@@ -256,17 +285,21 @@
         solve_kernel,
         [((N, N), B), ((N, N), B), ((8 * RR, N), F), ((1, N), F)],
         [pltpu.VMEM((N, N), F), pltpu.VMEM((N, N), F)],
+        smem=1,
         name="solve",
-    )(both, left, raw)
+    )(place, line, other_core, left, raw)
     w16_o = swap(w16, "r")
-    scale = lax.rsqrt(jnp.sum(gather(squares, TP), axis=0, keepdims=True) / COLS + 1e-06)
-    scale_o = swap(scale, "r")
-    moment_new, basis_new = call(own_kernel, [(blend.shape, F), (right.shape, F)], name="own")(
-        blend, ortho, right, scale
-    )
-    weight_new, rollout = call(
-        weight_kernel, [(weight.shape, B), ((2, *weight.shape), B)], smem=1, name="weights"
-    )(index("r"), left, w16, raw, scale, weights[0], left_o, w16_o, raw_o, scale_o, weight_o)
+    sums = exchange(jnp.broadcast_to(squares[None], (32, 1, N)), ("x", "z", "r")).reshape(16, 2, N)
+    wide, tall = weight.shape, right.shape
+    weight_new, moment_new, basis_new, rollout = call(
+        last_kernel,
+        [(wide, B), (wide, F), (tall, F), ((2, *wide), B)],
+        [pltpu.VMEM((2, *wide), B), pltpu.VMEM(wide, F), pltpu.VMEM(tall, F), pltpu.SemaphoreType.DMA((5,))],
+        smem=1,
+        name="last",
+        mib=24,
+        out_spec=pl.BlockSpec(memory_space=pl.ANY),
+    )(place, sums, momentum, gradient, ortho, right, left, w16, raw, weights[0], left_o, w16_o, raw_o, weight_o)
     return weight_new[None], moment_new[None], basis_new[None], rollout
 
 

time: 174 us -> 165 us (0.948)
  blocking collectives: 37.6 us -> 53.5 us
  between operations: 14.1 us -> 0.99 us
  waiting for transfers between devices: 47.3 us -> 34.9 us
  local copies, waits for them, and re-layouts: 10.7 us -> 6.6 us
  Pallas kernels: 35.7 us -> 38.8 us
  starting transfers between devices: 23.3 us -> 25.6 us
    all_gather x1 -> x0, waiting for transfers between devices: 22.4 us -> none  [body(): both = lax.all_gather(piece, FSDP, axis=0, tiled=False)]
    all_to_all x2, blocking collectives: 37.6 us -> 53.5 us  [exchange(): return lax.all_to_all(x, axis, 0, 0, tiled=True)]
    ppermute x9 -> x12, waiting for transfers between devices: 14 us -> 23 us  [swap(): lax.ppermute(x, axis, [(i, i ^ bit) for i in range(lax.axis_size(axis))])]
    unnamed x20 -> x16, local copies, waits for them, and re-layouts: 9.85 us -> 6.53 us
    pallas_call x7 -> x8, Pallas kernels: 35.7 us -> 38.8 us  [run(): pl.pallas_call(kernel, out_shape=[jax.ShapeDtypeStruct(s, d) for s, d in...]
    ppermute x9 -> x12, starting transfers between devices: 17.3 us -> 19.6 us  [swap(): lax.ppermute(x, axis, [(i, i ^ bit) for i in range(lax.axis_size(axis))])]
  transfers between devices with their start and end apart: 11 -> 13, of which waited for: 6 -> 6; matrix products, arithmetic and copies ran while one was open for 1% -> 1% of each run, Pallas kernels for 16% -> 17%
where the time goes in v4:
time: 165 us
  blocking collectives  53.5 us (32%)
  Pallas kernels  38.8 us (24%)
  waiting for transfers between devices  34.9 us (21%)
  starting transfers between devices  25.6 us (16%)
  local copies, waits for them, and re-layouts  6.6 us (4%)
  matrix products  3.05 us (2%)
    all_to_all x2, blocking collectives, exchange(): return lax.all_to_all(x, axis, 0, 0, tiled=True)  53.5 us
    pallas_call x8, Pallas kernels, run(): pl.pallas_call(kernel, out_shape=[jax.ShapeDtypeStruct(s, d) for s, d in...  38.8 us
    ppermute x12, waiting for transfers between devices, swap(): lax.ppermute(x, axis, [(i, i ^ bit) for i in range(lax.axis_size(axis))])  23 us
    ppermute x12, starting transfers between devices, swap(): lax.ppermute(x, axis, [(i, i ^ bit) for i in range(lax.axis_size(axis))])  19.6 us
    all_to_all x1, waiting for transfers between devices, exchange(): return lax.all_to_all(x, axis, 0, 0, tiled=True)  11.8 us
    unnamed x16, local copies, waits for them, and re-layouts  6.53 us
    all_to_all x1, starting transfers between devices, exchange(): return lax.all_to_all(x, axis, 0, 0, tiled=True)  5.96 us
  transfers between devices with their start and end apart: 13, of which 6 were waited for; matrix products, arithmetic and copies ran while one was open for 1% of the time, Pallas kernels for 17%

profile of v4, /device:TPU:1, one launch (start us, length us, event | category | flops | bytes accessed | tf_op | source)
XLA Modules:
  0.0 164.6 jit_solution(13956693661177058947)
XLA Ops:
  0.7 3.1 %convolution_convert_fusion = bf16[512,512]{1,0:T(8,128)(2,1)S(1)} fusion(f32[1,512,896]{2,1,0:T(8,128)} %param.6, bf16[1,512,896]{2,1,0:T(8,128)(2,1)} %param.5, f32[1,896,512]{2,1,0:T(8,128)} %param.7), kind=kOutput, calls=%fused_computation.2 | convolution fusion | flops 471859200 | bytes 5111808 | tf_op jit(solution)/shard_map/dot_general | solution.py:39
  3.8 23.9 %all_to_all.15.pieces = bf16[16,32,512]{2,1,0:T(8,128)(2,1)S(1)} all-to-all(bf16[16,32,512]{2,1,0:T(8,128)(2,1)S(1)} %bitcast.27), channel_id=1, replica_groups=mesh['y'=4,'c'=2,'x'=2,'z'=8,'r'=2] {'x','z'}, dimensions={0} | all-to-all | bytes 1048576 | tf_op jit(solution)/shard_map/all_to_all | solution.py:242
  27.8 0.8 copy-done.3
  28.5 6.0 %all-to-all-start.1 = ((bf16[16,32,512]{2,1,0:T(8,128)(2,1)}), bf16[16,32,512]{2,1,0:T(8,128)(2,1)S(1)}, u32[]{:S(2)}, u32[]{:S(2)}) async-start(bf16[16,32,512]{2,1,0:T(8,128)(2,1)} %copy-done.3), calls=%async_computation.1 | async-start | bytes 1048576 | tf_op jit(solution)/shard_map/all_to_all | solution.py:242
  34.5 1.1 add_convert_fusion.blend_ref
  35.6 11.8 %all-to-all-done.1 = bf16[16,32,512]{2,1,0:T(8,128)(2,1)S(1)} async-done(((bf16[16,32,512]{2,1,0:T(8,128)(2,1)}), bf16[16,32,512]{2,1,0:T(8,128)(2,1)S(1)}, u32[]{:S(2)}, u32[]{:S(2)}) %all-to-all-start.1) | async-done | bytes 524320 | tf_op jit(solution)/shard_map/all_to_all | solution.py:242
  47.5 1.2 copy-done.2
  48.6 1.6 pieces.1
  50.2 3.2 %collective-permute-start = (bf16[4,208,512]{2,1,0:T(8,128)(2,1)S(1)}, bf16[4,208,512]{2,1,0:T(8,128)(2,1)S(1)}, u32[]{:S(2)}, u32[]{:S(2)}) collective-permute-start(bf16[4,208,512]{2,1,0:T(8,128)(2,1)S(1)} %get-tuple-element.27), channel_id=1, source_target_pairs={{0,32},{32,0},{1,33},{33,1},{2,34},{34,2},{3,35},{35,3},{4,36},{36... | collective-permute-start | bytes 2555912 | tf_op jit(solution)/shard_map/ppermute | solution.py:246
  53.4 2.0 %collective-permute-done.got = bf16[4,208,512]{2,1,0:T(8,128)(2,1)S(1)} collective-permute-done((bf16[4,208,512]{2,1,0:T(8,128)(2,1)S(1)}, bf16[4,208,512]{2,1,0:T(8,128)(2,1)S(1)}, u32[]{:S(2)}, u32[]{:S(2)}) %collective-permute-start) | collective-permute-done | bytes 852000 | tf_op jit(solution)/shard_map/ppermute | solution.py:246
  55.4 0.7 join.1
  56.1 1.4 collective-permute-start.1
  57.5 2.6 %collective-permute-start.2 = (bf16[208,512]{1,0:T(8,128)(2,1)S(1)}, bf16[208,512]{1,0:T(8,128)(2,1)S(1)}, u32[]{:S(2)}, u32[]{:S(2)}) collective-permute-start(bf16[208,512]{1,0:T(8,128)(2,1)S(1)} %get-tuple-element.31), channel_id=1, source_target_pairs={{0,128},{64,192},{128,0},{192,64},{1,129},{65,193},{129,1},{193,65... | collective-permute-start | bytes 638984 | tf_op jit(solution)/shard_map/ppermute | solution.py:246
  60.2 2.5 %collective-permute-done.1.one = bf16[208,512]{1,0:T(8,128)(2,1)S(1)} collective-permute-done((bf16[208,512]{1,0:T(8,128)(2,1)S(1)}, bf16[208,512]{1,0:T(8,128)(2,1)S(1)}, u32[]{:S(2)}, u32[]{:S(2)}) %collective-permute-start.1) | collective-permute-done | bytes 213024 | tf_op jit(solution)/shard_map/ppermute | solution.py:246
  62.7 7.1 %collective-permute-done.2.two = bf16[208,512]{1,0:T(8,128)(2,1)S(1)} collective-permute-done((bf16[208,512]{1,0:T(8,128)(2,1)S(1)}, bf16[208,512]{1,0:T(8,128)(2,1)S(1)}, u32[]{:S(2)}, u32[]{:S(2)}) %collective-permute-start.2) | collective-permute-done | bytes 213024 | tf_op jit(solution)/shard_map/ppermute | solution.py:246
  69.8 2.1 %collective-permute-done.3.three = bf16[208,512]{1,0:T(8,128)(2,1)S(1)} collective-permute-done((bf16[208,512]{1,0:T(8,128)(2,1)S(1)}, bf16[208,512]{1,0:T(8,128)(2,1)S(1)}, u32[]{:S(2)}, u32[]{:S(2)}) %collective-permute-start.3) | collective-permute-done | bytes 213024 | tf_op jit(solution)/shard_map/ppermute | solution.py:246
  72.2 3.1 %collective-permute-start.4 = (bf16[208,512]{1,0:T(8,128)(2,1)S(1)}, bf16[208,512]{1,0:T(8,128)(2,1)S(1)}, u32[]{:S(2)}, u32[]{:S(2)}) collective-permute-start(bf16[208,512]{1,0:T(8,128)(2,1)S(1)} %sum.1.own), channel_id=1, source_target_pairs={{0,64},{64,0},{128,192},{192,128},{1,65},{65,1},{129,193},{193,129... | collective-permute-start | bytes 638984 | tf_op jit(solution)/shard_map/ppermute | solution.py:246
  75.4 9.2 %collective-permute-done.6.three = bf16[208,512]{1,0:T(8,128)(2,1)S(1)} collective-permute-done((bf16[208,512]{1,0:T(8,128)(2,1)S(1)}, bf16[208,512]{1,0:T(8,128)(2,1)S(1)}, u32[]{:S(2)}, u32[]{:S(2)}) %collective-permute-start.6) | collective-permute-done | bytes 213024 | tf_op jit(solution)/shard_map/ppermute | solution.py:246
  84.6 0.6 line.1.own
  85.2 1.7 %collective-permute-start.7 = (bf16[4,208,512]{2,1,0:T(8,128)(2,1)S(1)}, bf16[4,208,512]{2,1,0:T(8,128)(2,1)S(1)}, u32[]{:S(2)}, u32[]{:S(2)}) collective-permute-start(bf16[4,208,512]{2,1,0:T(8,128)(2,1)S(1)} %line.1.own), channel_id=1, source_target_pairs={{0,32},{32,0},{1,33},{33,1},{2,34},{34,2},{3,35},{35,3},{4,36},{36... | collective-permute-start | bytes 2555912 | tf_op jit(solution)/shard_map/ppermute | solution.py:246
  86.9 2.5 %collective-permute-start.11 = (bf16[512,896]{1,0:T(8,128)(2,1)}, bf16[512,896]{1,0:T(8,128)(2,1)}, u32[]{:S(2)}, u32[]{:S(2)}) collective-permute-start(bf16[512,896]{1,0:T(8,128)(2,1)} %bitcast.10.weight0), channel_id=1, source_target_pairs={{0,1},{1,0},{2,3},{3,2},{4,5},{5,4},{6,7},{7,6},{8,9},{9,8},{10,11... | collective-permute-start | bytes 2752520 | tf_op jit(solution)/shard_map/ppermute | solution.py:246
  89.3 1.5 rows.1.right_in.right0
  90.9 2.0 %collective-permute-start.10 = (bf16[896,512]{1,0:T(8,128)(2,1)}, bf16[896,512]{1,0:T(8,128)(2,1)}, u32[]{:S(2)}, u32[]{:S(2)}) collective-permute-start(bf16[896,512]{1,0:T(8,128)(2,1)} %rows.1.right_in.right0), channel_id=1, source_target_pairs={{0,1},{1,0},{2,3},{3,2},{4,5},{5,4},{6,7},{7,6},{8,9},{9,8},{10,11... | collective-permute-start | bytes 2752520 | tf_op jit(solution)/shard_map/ppermute | solution.py:246
  92.9 1.0 collective-permute-start.8
  93.9 25.9 %solve.1 = (bf16[512,512]{1,0:T(8,128)(2,1)}, bf16[512,512]{1,0:T(8,128)(2,1)S(1)}, f32[896,512]{1,0:T(8,128)S(1)}, f32[1,512]{1,0:T(1,128)S(1)}) custom-call(s32[3]{0:T(128)S(1)} %pad_add_fusion.place, bf16[4,208,512]{2,1,0:T(8,128)(2,1)S(1)} %line.1.own, bf16[4,208,512]{2,1,0:T(8,128)(2,1)S(1)} %collective-permute-done.7.got, ...), custom_call_target="tpu_custom_call" | custom-call | tf_op jit(solution)/shard_map/solve/pallas_call | solution.py:25
  119.7 1.2 copy-done.4
  121.0 0.8 copy-done.6
  121.8 2.0 %collective-permute-start.9 = (bf16[512,512]{1,0:T(8,128)(2,1)}, bf16[512,512]{1,0:T(8,128)(2,1)}, u32[]{:S(2)}, u32[]{:S(2)}) collective-permute-start(bf16[512,512]{1,0:T(8,128)(2,1)} %get-tuple-element.36.w0), channel_id=1, source_target_pairs={{0,1},{1,0},{2,3},{3,2},{4,5},{5,4},{6,7},{7,6},{8,9},{9,8},{10,11... | collective-permute-start | bytes 1572872 | tf_op jit(solution)/shard_map/ppermute | solution.py:246
  123.8 29.6 %all_to_all.16 = f32[32,1,512]{2,1,0:T(1,128)S(1)} all-to-all(f32[32,1,512]{2,1,0:T(1,128)S(1)} %broadcast_in_dim.18), channel_id=1, replica_groups=mesh['y'=4,'c'=2,'x'=2,'z'=8,'r'=2] {'x','z','r'}, dimensions={0} | all-to-all | bytes 131072 | tf_op jit(solution)/shard_map/all_to_all | solution.py:242
  153.6 1.5 copy-done.5
  155.1 1.0 copy-done.7
  156.2 8.2 %last.1 = (bf16[512,896]{1,0:T(8,128)(2,1)}, f32[512,896]{1,0:T(8,128)}, f32[896,512]{1,0:T(8,128)}, bf16[2,512,896]{2,1,0:T(8,128)(2,1)}) custom-call(s32[3]{0:T(128)S(1)} %pad_add_fusion.place, f32[16,2,512]{2,1,0:T(2,128)S(1)} %reshape.24.sums, f32[512,896]{1,0:T(8,128)S(1)} %bitcast.20, bf16[512,896]{1,0:T(8,128)(2,1)S(1)} %bitcast.25, ...), custom_call_target="tpu_custom_call" | custom-call | tf_op jit(solution)/shard_map/last/pallas_call | solution.py:25
  (26 shorter events, 0.7 us)
Async XLA Ops:
  3.8 30.7 %copy-start = (f32[1,512,896]{2,1,0:T(8,128)S(1)}, f32[1,512,896]{2,1,0:T(8,128)}, u32[]{:S(2)}) copy-start(f32[1,512,896]{2,1,0:T(8,128)} %param.6) | copy-start | bytes 5505028
  3.8 30.7 %copy-start.1 = (bf16[1,512,896]{2,1,0:T(8,128)(2,1)S(1)}, bf16[1,512,896]{2,1,0:T(8,128)(2,1)}, u32[]{:S(2)}) copy-start(bf16[1,512,896]{2,1,0:T(8,128)(2,1)} %param.5) | copy-start | bytes 2752516
  27.7 0.8 copy-start.3
  28.5 18.9 %all-to-all-start.1 = ((bf16[16,32,512]{2,1,0:T(8,128)(2,1)}), bf16[16,32,512]{2,1,0:T(8,128)(2,1)S(1)}, u32[]{:S(2)}, u32[]{:S(2)}) async-start(bf16[16,32,512]{2,1,0:T(8,128)(2,1)} %copy-done.3), calls=%async_computation.1 | async-start | bytes 1048576 | tf_op jit(solution)/shard_map/all_to_all | solution.py:242
  47.5 1.2 copy-start.2
  50.2 5.2 %collective-permute-start = (bf16[4,208,512]{2,1,0:T(8,128)(2,1)S(1)}, bf16[4,208,512]{2,1,0:T(8,128)(2,1)S(1)}, u32[]{:S(2)}, u32[]{:S(2)}) collective-permute-start(bf16[4,208,512]{2,1,0:T(8,128)(2,1)S(1)} %get-tuple-element.27), channel_id=1, source_target_pairs={{0,32},{32,0},{1,33},{33,1},{2,34},{34,2},{3,35},{35,3},{4,36},{36... | collective-permute-start | bytes 2555912 | tf_op jit(solution)/shard_map/ppermute | solution.py:246
  56.1 6.6 %collective-permute-start.1 = (bf16[208,512]{1,0:T(8,128)(2,1)S(1)}, bf16[208,512]{1,0:T(8,128)(2,1)S(1)}, u32[]{:S(2)}, u32[]{:S(2)}) collective-permute-start(bf16[208,512]{1,0:T(8,128)(2,1)S(1)} %get-tuple-element.30), channel_id=1, source_target_pairs={{0,64},{64,0},{128,192},{192,128},{1,65},{65,1},{129,193},{193,129... | collective-permute-start | bytes 638984 | tf_op jit(solution)/shard_map/ppermute | solution.py:246
  57.5 12.2 %collective-permute-start.2 = (bf16[208,512]{1,0:T(8,128)(2,1)S(1)}, bf16[208,512]{1,0:T(8,128)(2,1)S(1)}, u32[]{:S(2)}, u32[]{:S(2)}) collective-permute-start(bf16[208,512]{1,0:T(8,128)(2,1)S(1)} %get-tuple-element.31), channel_id=1, source_target_pairs={{0,128},{64,192},{128,0},{192,64},{1,129},{65,193},{129,1},{193,65... | collective-permute-start | bytes 638984 | tf_op jit(solution)/shard_map/ppermute | solution.py:246
  60.2 11.8 %collective-permute-start.3 = (bf16[208,512]{1,0:T(8,128)(2,1)S(1)}, bf16[208,512]{1,0:T(8,128)(2,1)S(1)}, u32[]{:S(2)}, u32[]{:S(2)}) collective-permute-start(bf16[208,512]{1,0:T(8,128)(2,1)S(1)} %get-tuple-element.32), channel_id=1, source_target_pairs={{0,192},{64,128},{128,64},{192,0},{1,193},{65,129},{129,65},{193,1... | collective-permute-start | bytes 638984 | tf_op jit(solution)/shard_map/ppermute | solution.py:246
  72.0 12.6 %collective-permute-start.6 = (bf16[208,512]{1,0:T(8,128)(2,1)S(1)}, bf16[208,512]{1,0:T(8,128)(2,1)S(1)}, u32[]{:S(2)}, u32[]{:S(2)}) collective-permute-start(bf16[208,512]{1,0:T(8,128)(2,1)S(1)} %sum.1.own), channel_id=1, source_target_pairs={{0,192},{64,128},{128,64},{192,0},{1,193},{65,129},{129,65},{193,1... | collective-permute-start | bytes 638984 | tf_op jit(solution)/shard_map/ppermute | solution.py:246
  72.2 12.4 %collective-permute-start.5 = (bf16[208,512]{1,0:T(8,128)(2,1)S(1)}, bf16[208,512]{1,0:T(8,128)(2,1)S(1)}, u32[]{:S(2)}, u32[]{:S(2)}) collective-permute-start(bf16[208,512]{1,0:T(8,128)(2,1)S(1)} %sum.1.own), channel_id=1, source_target_pairs={{0,128},{64,192},{128,0},{192,64},{1,129},{65,193},{129,1},{193,65... | collective-permute-start | bytes 638984 | tf_op jit(solution)/shard_map/ppermute | solution.py:246
  72.2 12.4 %collective-permute-start.4 = (bf16[208,512]{1,0:T(8,128)(2,1)S(1)}, bf16[208,512]{1,0:T(8,128)(2,1)S(1)}, u32[]{:S(2)}, u32[]{:S(2)}) collective-permute-start(bf16[208,512]{1,0:T(8,128)(2,1)S(1)} %sum.1.own), channel_id=1, source_target_pairs={{0,64},{64,0},{128,192},{192,128},{1,65},{65,1},{129,193},{193,129... | collective-permute-start | bytes 638984 | tf_op jit(solution)/shard_map/ppermute | solution.py:246
  85.2 4.1 %collective-permute-start.7 = (bf16[4,208,512]{2,1,0:T(8,128)(2,1)S(1)}, bf16[4,208,512]{2,1,0:T(8,128)(2,1)S(1)}, u32[]{:S(2)}, u32[]{:S(2)}) collective-permute-start(bf16[4,208,512]{2,1,0:T(8,128)(2,1)S(1)} %line.1.own), channel_id=1, source_target_pairs={{0,32},{32,0},{1,33},{33,1},{2,34},{34,2},{3,35},{35,3},{4,36},{36... | collective-permute-start | bytes 2555912 | tf_op jit(solution)/shard_map/ppermute | solution.py:246
  86.9 66.7 %collective-permute-start.11 = (bf16[512,896]{1,0:T(8,128)(2,1)}, bf16[512,896]{1,0:T(8,128)(2,1)}, u32[]{:S(2)}, u32[]{:S(2)}) collective-permute-start(bf16[512,896]{1,0:T(8,128)(2,1)} %bitcast.10.weight0), channel_id=1, source_target_pairs={{0,1},{1,0},{2,3},{3,2},{4,5},{5,4},{6,7},{7,6},{8,9},{9,8},{10,11... | collective-permute-start | bytes 2752520 | tf_op jit(solution)/shard_map/ppermute | solution.py:246
  90.9 62.7 %collective-permute-start.10 = (bf16[896,512]{1,0:T(8,128)(2,1)}, bf16[896,512]{1,0:T(8,128)(2,1)}, u32[]{:S(2)}, u32[]{:S(2)}) collective-permute-start(bf16[896,512]{1,0:T(8,128)(2,1)} %rows.1.right_in.right0), channel_id=1, source_target_pairs={{0,1},{1,0},{2,3},{3,2},{4,5},{5,4},{6,7},{7,6},{8,9},{9,8},{10,11... | collective-permute-start | bytes 2752520 | tf_op jit(solution)/shard_map/ppermute | solution.py:246
  92.9 60.7 %collective-permute-start.8 = (bf16[512,512]{1,0:T(8,128)(2,1)S(1)}, bf16[512,512]{1,0:T(8,128)(2,1)}, u32[]{:S(2)}, u32[]{:S(2)}) collective-permute-start(bf16[512,512]{1,0:T(8,128)(2,1)S(1)} %bitcast.22), channel_id=1, source_target_pairs={{0,1},{1,0},{2,3},{3,2},{4,5},{5,4},{6,7},{7,6},{8,9},{9,8},{10,11... | collective-permute-start | bytes 1572872 | tf_op jit(solution)/shard_map/ppermute | solution.py:246
  119.7 1.2 copy-start.4
  121.0 0.8 copy-start.6
  121.8 31.9 %collective-permute-start.9 = (bf16[512,512]{1,0:T(8,128)(2,1)}, bf16[512,512]{1,0:T(8,128)(2,1)}, u32[]{:S(2)}, u32[]{:S(2)}) collective-permute-start(bf16[512,512]{1,0:T(8,128)(2,1)} %get-tuple-element.36.w0), channel_id=1, source_target_pairs={{0,1},{1,0},{2,3},{3,2},{4,5},{5,4},{6,7},{7,6},{8,9},{9,8},{10,11... | collective-permute-start | bytes 1572872 | tf_op jit(solution)/shard_map/ppermute | solution.py:246
  153.6 1.5 copy-start.5
  155.1 1.0 copy-start.7

commit v5 on v4

--- a/solution.py
+++ b/solution.py
@@ -202,7 +202,9 @@
                 a[rows, 256:] = g[square:, :]
     inverse_factor(a, w)
     wh, wl = halves(w[...])
-    w16[...] = wh
+    w16[:256, :] = wh[256:, :]
+    w16[256:, :256] = wh[:128, :256]
+    w16[256:, 256:] = wh[128:256, :256]
     ortho[...] = (dot(left[...], wh, NT) + dot(left[...], wl, NT)).astype(B)
     r = dot(right_in[...], wh, NT) + dot(right_in[...], wl, NT)
     right[...] = r
@@ -211,11 +213,16 @@
 
 def last_kernel(
     place, sums, momentum, gradient, ortho, right, left0, w0, right0, weight0, left1, w1, right1, weight1,
-    out_weight, out_moment, out_basis, out_rollout, weight, moment, basis, sems,
+    out_weight, out_moment, out_basis, out_rollout, weight, moment, basis, w, sems,
 ):
-    scales = lax.rsqrt(jnp.sum(sums[...], axis=0) / COLS + 1e-06)
+    scales = []
+    for side in range(2):
+        squares = sums[side]
+        for k in range(2 + side, 32, 2):
+            squares = squares + sums[k]
+        scales.append(lax.rsqrt(squares / COLS + 1e-06))
     first = place[2] == 0
-    scale = [jnp.where(first, scales[0:1], scales[1:2]), jnp.where(first, scales[1:2], scales[0:1])]
+    scale = [jnp.where(first, *scales), jnp.where(first, *scales[::-1])]
     basis[...] = right[...] * scale[0]
     copies = [pltpu.make_async_copy(basis, out_basis, sems.at[0])]
     copies[-1].start()
@@ -224,10 +231,14 @@
     copies.append(pltpu.make_async_copy(moment, out_moment, sems.at[1]))
     copies[-1].start()
     for half, refs in enumerate(((left0, w0, right0, weight0), (left1, w1, right1, weight1))):
-        left, w, raw, old = (ref[...] for ref in refs)
-        o = (dot(left, w, NT) * scale[half]).astype(B)
-        r = dot(raw, w, NT).astype(B)
-        weight[half] = (old.astype(F) - 0.3 * dot(o, r, NT)).astype(B)
+        left, packed_w, raw, old = refs
+        w[256:, :] = packed_w[:256, :]
+        w[:128, :256] = packed_w[256:, :256]
+        w[128:256, :256] = packed_w[256:, 256:]
+        w[:256, 256:] = jnp.zeros((256, 256), B)
+        o = (dot(left[...], w[...], NT) * scale[half]).astype(B)
+        r = dot(raw[...], w[...], NT).astype(B)
+        weight[half] = (old[...].astype(F) - 0.3 * dot(o, r, NT)).astype(B)
         side = place[2] if half == 0 else 1 - place[2]
         copies.append(pltpu.make_async_copy(weight.at[half], out_rollout.at[side], sems.at[2 + half]))
         copies[-1].start()
@@ -252,6 +263,7 @@
     momentum, gradient = momentum[0], gradient[0]
     blend16 = (momentum + gradient.astype(F)).astype(B)
     part = dot(blend16, basis[0].astype(B), NN).astype(B).reshape(16, -1, N)
+    blend16, part = lax.optimization_barrier((blend16, part))
     (copies,) = call(spread_kernel, [(part.shape, B)], name="spread")(exchange(part, TP))
     left = exchange(copies, TP).reshape(-1, N)
 
@@ -263,6 +275,9 @@
         name="pieces",
     )(place, left, blend16)
     got = swap(send, "c")
+    left_o = swap(left, "r")
+    weight, _ = lax.optimization_barrier((weights[0], left))
+    weight_o = swap(weight, "r")
     own_g, own_r, *outs = call(
         join_kernel,
         [((GR, 256), F), ((RR, N), F)] + [((RR + GR, N), B)] * 3,
@@ -274,27 +289,25 @@
     (line,) = call(line_kernel, [((4, RR + GR, N), B)], smem=1, name="line")(
         place, piece, *[swap(piece, "y", k) for k in (1, 2, 3)]
     )
+    line, left_o, weight_o = lax.optimization_barrier((line, left_o, weight_o))
     other_core = swap(line, "c")
     (raw,) = call(rows_kernel, [((8 * RR, N), B)], smem=1, name="rows")(place, line, other_core)
     raw_o = swap(raw, "r")
-    left_o = swap(left, "r")
-    weight, _ = lax.optimization_barrier((weights[0], left))
-    weight_o = swap(weight, "r")
 
     w16, ortho, right, squares = call(
         solve_kernel,
-        [((N, N), B), ((N, N), B), ((8 * RR, N), F), ((1, N), F)],
+        [((384, N), B), ((N, N), B), ((8 * RR, N), F), ((1, N), F)],
         [pltpu.VMEM((N, N), F), pltpu.VMEM((N, N), F)],
         smem=1,
         name="solve",
     )(place, line, other_core, left, raw)
     w16_o = swap(w16, "r")
-    sums = exchange(jnp.broadcast_to(squares[None], (32, 1, N)), ("x", "z", "r")).reshape(16, 2, N)
+    sums = exchange(jnp.broadcast_to(squares[None], (32, 1, N)), ("x", "z", "r"))
     wide, tall = weight.shape, right.shape
     weight_new, moment_new, basis_new, rollout = call(
         last_kernel,
         [(wide, B), (wide, F), (tall, F), ((2, *wide), B)],
-        [pltpu.VMEM((2, *wide), B), pltpu.VMEM(wide, F), pltpu.VMEM(tall, F), pltpu.SemaphoreType.DMA((5,))],
+        [pltpu.VMEM((2, *wide), B), pltpu.VMEM(wide, F), pltpu.VMEM(tall, F), pltpu.VMEM((N, N), B), pltpu.SemaphoreType.DMA((5,))],
         smem=1,
         name="last",
         mib=24,

time: 165 us -> 143 us (0.87)
  waiting for transfers between devices: 34.9 us -> 24.9 us
  starting transfers between devices: 25.6 us -> 17.7 us
  local copies, waits for them, and re-layouts: 6.6 us -> 0.51 us
  blocking collectives: 53.5 us -> 57.9 us
  Pallas kernels: 38.8 us -> 35.2 us
    all_to_all x1 -> x0, waiting for transfers between devices: 11.8 us -> none  [exchange(): return lax.all_to_all(x, axis, 0, 0, tiled=True)]
    unnamed x16 -> x6, local copies, waits for them, and re-layouts: 6.53 us -> 0.47 us
    all_to_all x1 -> x0, starting transfers between devices: 5.96 us -> none  [exchange(): return lax.all_to_all(x, axis, 0, 0, tiled=True)]
    all_to_all x2 -> x3, blocking collectives: 53.5 us -> 57.9 us  [exchange(): return lax.all_to_all(x, axis, 0, 0, tiled=True)]
    pallas_call x8, Pallas kernels: 38.8 us -> 35.2 us  [run(): pl.pallas_call(kernel, out_shape=[jax.ShapeDtypeStruct(s, d) for s, d in...]
    ppermute x12, starting transfers between devices: 19.6 us -> 17.7 us  [swap(): lax.ppermute(x, axis, [(i, i ^ bit) for i in range(lax.axis_size(axis))])]
    ppermute x12, waiting for transfers between devices: 23 us -> 24.9 us  [swap(): lax.ppermute(x, axis, [(i, i ^ bit) for i in range(lax.axis_size(axis))])]
  transfers between devices with their start and end apart: 13 -> 12, of which waited for: 6 -> 6; matrix products, arithmetic and copies ran while one was open for 1% -> 0% of each run, Pallas kernels for 17% -> 19%
where the time goes in v5:
time: 143 us; the launch traced here: 142 us
  blocking collectives  57.9 us (40%)
  Pallas kernels  35.2 us (25%)
  waiting for transfers between devices  24.9 us (17%)
  starting transfers between devices  17.7 us (12%)
  matrix products  2.25 us (2%)
  other arithmetic  2.16 us (2%)
    all_to_all x3, blocking collectives, exchange(): return lax.all_to_all(x, axis, 0, 0, tiled=True)  57.9 us
    pallas_call x8, Pallas kernels, run(): pl.pallas_call(kernel, out_shape=[jax.ShapeDtypeStruct(s, d) for s, d in...  35.2 us
    ppermute x12, waiting for transfers between devices, swap(): lax.ppermute(x, axis, [(i, i ^ bit) for i in range(lax.axis_size(axis))])  24.9 us
    ppermute x12, starting transfers between devices, swap(): lax.ppermute(x, axis, [(i, i ^ bit) for i in range(lax.axis_size(axis))])  17.7 us
  transfers between devices with their start and end apart: 12, of which 6 were waited for; matrix products, arithmetic and copies ran while one was open for 0% of the time, Pallas kernels for 19%

profile of v5, /device:TPU:1, one launch (start us, length us, event | category | flops | bytes accessed | tf_op | source)
XLA Modules:
  0.0 141.6 jit_solution(17119934465470523443)
XLA Ops:
  0.6 0.1 pad_add_fusion.place
  0.7 2.1 %add_convert_fusion.1.blend_ref = bf16[512,896]{1,0:T(8,128)(2,1)S(1)} fusion(bf16[1,512,896]{2,1,0:T(8,128)(2,1)} %param.5, f32[1,512,896]{2,1,0:T(8,128)} %param.6), kind=kLoop, calls=%fused_computation.1 | loop fusion | flops 1376256 | bytes 3670016 | tf_op jit(solution)/shard_map/convert_element_type | solution.py:264
  2.8 0.2 copy-done
  3.0 0.2 copy-done.1
  3.3 2.2 %convolution_convert_fusion = bf16[512,512]{1,0:T(8,128)(2,1)S(1)} fusion(f32[1,512,896]{2,1,0:T(8,128)S(1)} %copy-done, bf16[1,512,896]{2,1,0:T(8,128)(2,1)S(1)} %copy-done.1, f32[1,896,512]{2,1,0:T(8,128)} %param.7), kind=kOutput, calls=%fused_computation.2 | convolution fusion | flops 471859200 | bytes 5111808 | tf_op jit(solution)/shard_map/dot_general | solution.py:39
  5.5 23.5 %all_to_all.15.pieces = bf16[16,32,512]{2,1,0:T(8,128)(2,1)S(1)} all-to-all(bf16[16,32,512]{2,1,0:T(8,128)(2,1)S(1)} %bitcast.29), channel_id=1, replica_groups=mesh['y'=4,'c'=2,'x'=2,'z'=8,'r'=2] {'x','z'}, dimensions={0} | all-to-all | bytes 1048576 | tf_op jit(solution)/shard_map/all_to_all | solution.py:253
  29.1 0.1 spread.1
  29.2 18.9 %all_to_all.16 = bf16[16,32,512]{2,1,0:T(8,128)(2,1)S(1)} all-to-all(bf16[16,32,512]{2,1,0:T(8,128)(2,1)S(1)} %spread.1), channel_id=1, replica_groups=mesh['y'=4,'c'=2,'x'=2,'z'=8,'r'=2] {'x','z'}, dimensions={0} | all-to-all | bytes 1048576 | tf_op jit(solution)/shard_map/all_to_all | solution.py:253
  48.1 1.6 %pieces.1 = (f32[4,96,256]{2,1,0:T(8,128)S(1)}, f32[4,112,512]{2,1,0:T(8,128)S(1)}, bf16[4,208,512]{2,1,0:T(8,128)(2,1)S(1)}) custom-call(s32[3]{0:T(128)S(1)} %pad_add_fusion.place, bf16[512,512]{1,0:T(8,128)(2,1)S(1)} %bitcast.21, bf16[512,896]{1,0:T(8,128)(2,1)S(1)} %add_convert_fusion.1.blend_ref), custom_call_target="tpu_custom_call" | custom-call | tf_op jit(solution)/shard_map/pieces/pallas_call | solution.py:25
  49.6 3.2 %collective-permute-start = (bf16[4,208,512]{2,1,0:T(8,128)(2,1)S(1)}, bf16[4,208,512]{2,1,0:T(8,128)(2,1)S(1)}, u32[]{:S(2)}, u32[]{:S(2)}) collective-permute-start(bf16[4,208,512]{2,1,0:T(8,128)(2,1)S(1)} %get-tuple-element.34), channel_id=1, source_target_pairs={{0,32},{32,0},{1,33},{33,1},{2,34},{34,2},{3,35},{35,3},{4,36},{36... | collective-permute-start | bytes 2555912 | tf_op jit(solution)/shard_map/ppermute | solution.py:257
  52.8 2.5 %collective-permute-start.8 = (bf16[512,896]{1,0:T(8,128)(2,1)S(1)}, bf16[512,896]{1,0:T(8,128)(2,1)S(1)}, u32[]{:S(2)}, u32[]{:S(2)}) collective-permute-start(bf16[512,896]{1,0:T(8,128)(2,1)S(1)} %bitcast.26), channel_id=1, source_target_pairs={{0,1},{1,0},{2,3},{3,2},{4,5},{5,4},{6,7},{7,6},{8,9},{9,8},{10,11... | collective-permute-start | bytes 2752520 | tf_op jit(solution)/shard_map/ppermute | solution.py:257
  55.3 0.5 collective-permute-start.7
  55.8 0.7 join.1
  56.5 1.4 collective-permute-start.1
  57.9 2.6 %collective-permute-start.2 = (bf16[208,512]{1,0:T(8,128)(2,1)S(1)}, bf16[208,512]{1,0:T(8,128)(2,1)S(1)}, u32[]{:S(2)}, u32[]{:S(2)}) collective-permute-start(bf16[208,512]{1,0:T(8,128)(2,1)S(1)} %get-tuple-element.38), channel_id=1, source_target_pairs={{0,128},{64,192},{128,0},{192,64},{1,129},{65,193},{129,1},{193,65... | collective-permute-start | bytes 638984 | tf_op jit(solution)/shard_map/ppermute | solution.py:257
  60.5 2.2 %collective-permute-done.1.one = bf16[208,512]{1,0:T(8,128)(2,1)S(1)} collective-permute-done((bf16[208,512]{1,0:T(8,128)(2,1)S(1)}, bf16[208,512]{1,0:T(8,128)(2,1)S(1)}, u32[]{:S(2)}, u32[]{:S(2)}) %collective-permute-start.1) | collective-permute-done | bytes 213024 | tf_op jit(solution)/shard_map/ppermute | solution.py:257
  62.8 7.1 %collective-permute-done.2.two = bf16[208,512]{1,0:T(8,128)(2,1)S(1)} collective-permute-done((bf16[208,512]{1,0:T(8,128)(2,1)S(1)}, bf16[208,512]{1,0:T(8,128)(2,1)S(1)}, u32[]{:S(2)}, u32[]{:S(2)}) %collective-permute-start.2) | collective-permute-done | bytes 213024 | tf_op jit(solution)/shard_map/ppermute | solution.py:257
  69.8 2.5 %collective-permute-done.3.three = bf16[208,512]{1,0:T(8,128)(2,1)S(1)} collective-permute-done((bf16[208,512]{1,0:T(8,128)(2,1)S(1)}, bf16[208,512]{1,0:T(8,128)(2,1)S(1)}, u32[]{:S(2)}, u32[]{:S(2)}) %collective-permute-start.3) | collective-permute-done | bytes 213024 | tf_op jit(solution)/shard_map/ppermute | solution.py:257
  72.3 0.1 sum.1.own
  72.4 0.2 collective-permute-start.6
  72.6 3.1 %collective-permute-start.4 = (bf16[208,512]{1,0:T(8,128)(2,1)S(1)}, bf16[208,512]{1,0:T(8,128)(2,1)S(1)}, u32[]{:S(2)}, u32[]{:S(2)}) collective-permute-start(bf16[208,512]{1,0:T(8,128)(2,1)S(1)} %sum.1.own), channel_id=1, source_target_pairs={{0,64},{64,0},{128,192},{192,128},{1,65},{65,1},{129,193},{193,129... | collective-permute-start | bytes 638984 | tf_op jit(solution)/shard_map/ppermute | solution.py:257
  75.8 9.2 %collective-permute-done.6.three = bf16[208,512]{1,0:T(8,128)(2,1)S(1)} collective-permute-done((bf16[208,512]{1,0:T(8,128)(2,1)S(1)}, bf16[208,512]{1,0:T(8,128)(2,1)S(1)}, u32[]{:S(2)}, u32[]{:S(2)}) %collective-permute-start.6) | collective-permute-done | bytes 213024 | tf_op jit(solution)/shard_map/ppermute | solution.py:257
  85.0 0.6 line.1.own
  85.6 1.9 %collective-permute-done.7.left1 = bf16[512,512]{1,0:T(8,128)(2,1)S(1)} collective-permute-done((bf16[512,512]{1,0:T(8,128)(2,1)S(1)}, bf16[512,512]{1,0:T(8,128)(2,1)S(1)}, u32[]{:S(2)}, u32[]{:S(2)}) %collective-permute-start.7) | collective-permute-done | bytes 524320 | tf_op jit(solution)/shard_map/ppermute | solution.py:257
  87.5 0.9 collective-permute-start.9
  88.4 2.0 %collective-permute-done.9.got = bf16[4,208,512]{2,1,0:T(8,128)(2,1)S(1)} collective-permute-done((bf16[4,208,512]{2,1,0:T(8,128)(2,1)S(1)}, bf16[4,208,512]{2,1,0:T(8,128)(2,1)S(1)}, u32[]{:S(2)}, u32[]{:S(2)}) %collective-permute-start.9) | collective-permute-done | bytes 852000 | tf_op jit(solution)/shard_map/ppermute | solution.py:257
  90.4 0.6 rows.1.right_in.right0
  91.0 2.7 %collective-permute-start.11 = (bf16[896,512]{1,0:T(8,128)(2,1)S(1)}, bf16[896,512]{1,0:T(8,128)(2,1)S(1)}, u32[]{:S(2)}, u32[]{:S(2)}) collective-permute-start(bf16[896,512]{1,0:T(8,128)(2,1)S(1)} %rows.1.right_in.right0), channel_id=1, source_target_pairs={{0,1},{1,0},{2,3},{3,2},{4,5},{5,4},{6,7},{7,6},{8,9},{9,8},{10,11... | collective-permute-start | bytes 2752520 | tf_op jit(solution)/shard_map/ppermute | solution.py:257
  93.7 25.3 %solve.1 = (bf16[384,512]{1,0:T(8,128)(2,1)S(1)}, bf16[512,512]{1,0:T(8,128)(2,1)S(1)}, f32[896,512]{1,0:T(8,128)S(1)}, f32[1,512]{1,0:T(1,128)S(1)}) custom-call(s32[3]{0:T(128)S(1)} %pad_add_fusion.place, bf16[4,208,512]{2,1,0:T(8,128)(2,1)S(1)} %line.1.own, bf16[4,208,512]{2,1,0:T(8,128)(2,1)S(1)} %collective-permute-done.9.got, ...), custom_call_target="tpu_custom_call" | custom-call | tf_op jit(solution)/shard_map/solve/pallas_call | solution.py:25
  119.0 0.6 collective-permute-start.10
  119.6 15.5 %all_to_all.17.sums = f32[32,1,512]{2,1,0:T(1,128)S(1)} all-to-all(f32[32,1,512]{2,1,0:T(1,128)S(1)} %broadcast_in_dim.18), channel_id=1, replica_groups=mesh['y'=4,'c'=2,'x'=2,'z'=8,'r'=2] {'x','z','r'}, dimensions={0} | all-to-all | bytes 131072 | tf_op jit(solution)/shard_map/all_to_all | solution.py:253
  135.1 6.3 %last.1 = (bf16[512,896]{1,0:T(8,128)(2,1)}, f32[512,896]{1,0:T(8,128)}, f32[896,512]{1,0:T(8,128)}, bf16[2,512,896]{2,1,0:T(8,128)(2,1)}) custom-call(s32[3]{0:T(128)S(1)} %pad_add_fusion.place, f32[32,1,512]{2,1,0:T(1,128)S(1)} %all_to_all.17.sums, f32[512,896]{1,0:T(8,128)S(1)} %bitcast.20, bf16[512,896]{1,0:T(8,128)(2,1)S(1)} %bitcast.25, ...), custom_call_target="tpu_custom_call" | custom-call | tf_op jit(solution)/shard_map/last/pallas_call | solution.py:25
  (13 shorter events, 0.1 us)
Async XLA Ops:
  0.7 2.3 %copy-start = (f32[1,512,896]{2,1,0:T(8,128)S(1)}, f32[1,512,896]{2,1,0:T(8,128)}, u32[]{:S(2)}) copy-start(f32[1,512,896]{2,1,0:T(8,128)} %param.6) | copy-start | bytes 5505028
  0.7 2.6 %copy-start.1 = (bf16[1,512,896]{2,1,0:T(8,128)(2,1)S(1)}, bf16[1,512,896]{2,1,0:T(8,128)(2,1)}, u32[]{:S(2)}) copy-start(bf16[1,512,896]{2,1,0:T(8,128)(2,1)} %param.5) | copy-start | bytes 2752516
  29.1 23.7 %copy-start.2 = (bf16[1,512,896]{2,1,0:T(8,128)(2,1)S(1)}, bf16[1,512,896]{2,1,0:T(8,128)(2,1)}, u32[]{:S(2)}) copy-start(bf16[1,512,896]{2,1,0:T(8,128)(2,1)} %param.4) | copy-start | bytes 2752516
  49.6 6.2 %collective-permute-start = (bf16[4,208,512]{2,1,0:T(8,128)(2,1)S(1)}, bf16[4,208,512]{2,1,0:T(8,128)(2,1)S(1)}, u32[]{:S(2)}, u32[]{:S(2)}) collective-permute-start(bf16[4,208,512]{2,1,0:T(8,128)(2,1)S(1)} %get-tuple-element.34), channel_id=1, source_target_pairs={{0,32},{32,0},{1,33},{33,1},{2,34},{34,2},{3,35},{35,3},{4,36},{36... | collective-permute-start | bytes 2555912 | tf_op jit(solution)/shard_map/ppermute | solution.py:257
  52.8 34.7 %collective-permute-start.8 = (bf16[512,896]{1,0:T(8,128)(2,1)S(1)}, bf16[512,896]{1,0:T(8,128)(2,1)S(1)}, u32[]{:S(2)}, u32[]{:S(2)}) collective-permute-start(bf16[512,896]{1,0:T(8,128)(2,1)S(1)} %bitcast.26), channel_id=1, source_target_pairs={{0,1},{1,0},{2,3},{3,2},{4,5},{5,4},{6,7},{7,6},{8,9},{9,8},{10,11... | collective-permute-start | bytes 2752520 | tf_op jit(solution)/shard_map/ppermute | solution.py:257
  55.3 32.2 %collective-permute-start.7 = (bf16[512,512]{1,0:T(8,128)(2,1)S(1)}, bf16[512,512]{1,0:T(8,128)(2,1)S(1)}, u32[]{:S(2)}, u32[]{:S(2)}) collective-permute-start(bf16[512,512]{1,0:T(8,128)(2,1)S(1)} %bitcast.22), channel_id=1, source_target_pairs={{0,1},{1,0},{2,3},{3,2},{4,5},{5,4},{6,7},{7,6},{8,9},{9,8},{10,11... | collective-permute-start | bytes 1572872 | tf_op jit(solution)/shard_map/ppermute | solution.py:257
  56.5 6.2 %collective-permute-start.1 = (bf16[208,512]{1,0:T(8,128)(2,1)S(1)}, bf16[208,512]{1,0:T(8,128)(2,1)S(1)}, u32[]{:S(2)}, u32[]{:S(2)}) collective-permute-start(bf16[208,512]{1,0:T(8,128)(2,1)S(1)} %get-tuple-element.37), channel_id=1, source_target_pairs={{0,64},{64,0},{128,192},{192,128},{1,65},{65,1},{129,193},{193,129... | collective-permute-start | bytes 638984 | tf_op jit(solution)/shard_map/ppermute | solution.py:257
  57.9 11.9 %collective-permute-start.2 = (bf16[208,512]{1,0:T(8,128)(2,1)S(1)}, bf16[208,512]{1,0:T(8,128)(2,1)S(1)}, u32[]{:S(2)}, u32[]{:S(2)}) collective-permute-start(bf16[208,512]{1,0:T(8,128)(2,1)S(1)} %get-tuple-element.38), channel_id=1, source_target_pairs={{0,128},{64,192},{128,0},{192,64},{1,129},{65,193},{129,1},{193,65... | collective-permute-start | bytes 638984 | tf_op jit(solution)/shard_map/ppermute | solution.py:257
  60.5 11.8 %collective-permute-start.3 = (bf16[208,512]{1,0:T(8,128)(2,1)S(1)}, bf16[208,512]{1,0:T(8,128)(2,1)S(1)}, u32[]{:S(2)}, u32[]{:S(2)}) collective-permute-start(bf16[208,512]{1,0:T(8,128)(2,1)S(1)} %get-tuple-element.39), channel_id=1, source_target_pairs={{0,192},{64,128},{128,64},{192,0},{1,193},{65,129},{129,65},{193,1... | collective-permute-start | bytes 638984 | tf_op jit(solution)/shard_map/ppermute | solution.py:257
  72.4 12.6 %collective-permute-start.6 = (bf16[208,512]{1,0:T(8,128)(2,1)S(1)}, bf16[208,512]{1,0:T(8,128)(2,1)S(1)}, u32[]{:S(2)}, u32[]{:S(2)}) collective-permute-start(bf16[208,512]{1,0:T(8,128)(2,1)S(1)} %sum.1.own), channel_id=1, source_target_pairs={{0,192},{64,128},{128,64},{192,0},{1,193},{65,129},{129,65},{193,1... | collective-permute-start | bytes 638984 | tf_op jit(solution)/shard_map/ppermute | solution.py:257
  72.6 12.4 %collective-permute-start.5 = (bf16[208,512]{1,0:T(8,128)(2,1)S(1)}, bf16[208,512]{1,0:T(8,128)(2,1)S(1)}, u32[]{:S(2)}, u32[]{:S(2)}) collective-permute-start(bf16[208,512]{1,0:T(8,128)(2,1)S(1)} %sum.1.own), channel_id=1, source_target_pairs={{0,128},{64,192},{128,0},{192,64},{1,129},{65,193},{129,1},{193,65... | collective-permute-start | bytes 638984 | tf_op jit(solution)/shard_map/ppermute | solution.py:257
  72.6 12.4 %collective-permute-start.4 = (bf16[208,512]{1,0:T(8,128)(2,1)S(1)}, bf16[208,512]{1,0:T(8,128)(2,1)S(1)}, u32[]{:S(2)}, u32[]{:S(2)}) collective-permute-start(bf16[208,512]{1,0:T(8,128)(2,1)S(1)} %sum.1.own), channel_id=1, source_target_pairs={{0,64},{64,0},{128,192},{192,128},{1,65},{65,1},{129,193},{193,129... | collective-permute-start | bytes 638984 | tf_op jit(solution)/shard_map/ppermute | solution.py:257
  87.5 2.9 %collective-permute-start.9 = (bf16[4,208,512]{2,1,0:T(8,128)(2,1)S(1)}, bf16[4,208,512]{2,1,0:T(8,128)(2,1)S(1)}, u32[]{:S(2)}, u32[]{:S(2)}) collective-permute-start(bf16[4,208,512]{2,1,0:T(8,128)(2,1)S(1)} %line.1.own), channel_id=1, source_target_pairs={{0,32},{32,0},{1,33},{33,1},{2,34},{34,2},{3,35},{35,3},{4,36},{36... | collective-permute-start | bytes 2555912 | tf_op jit(solution)/shard_map/ppermute | solution.py:257
  91.0 44.2 %collective-permute-start.11 = (bf16[896,512]{1,0:T(8,128)(2,1)S(1)}, bf16[896,512]{1,0:T(8,128)(2,1)S(1)}, u32[]{:S(2)}, u32[]{:S(2)}) collective-permute-start(bf16[896,512]{1,0:T(8,128)(2,1)S(1)} %rows.1.right_in.right0), channel_id=1, source_target_pairs={{0,1},{1,0},{2,3},{3,2},{4,5},{5,4},{6,7},{7,6},{8,9},{9,8},{10,11... | collective-permute-start | bytes 2752520 | tf_op jit(solution)/shard_map/ppermute | solution.py:257
  119.0 16.2 %collective-permute-start.10 = (bf16[384,512]{1,0:T(8,128)(2,1)S(1)}, bf16[384,512]{1,0:T(8,128)(2,1)S(1)}, u32[]{:S(2)}, u32[]{:S(2)}) collective-permute-start(bf16[384,512]{1,0:T(8,128)(2,1)S(1)} %get-tuple-element.45.w0), channel_id=1, source_target_pairs={{0,1},{1,0},{2,3},{3,2},{4,5},{5,4},{6,7},{7,6},{8,9},{9,8},{10,11... | collective-permute-start | bytes 1179656 | tf_op jit(solution)/shard_map/ppermute | solution.py:257

commit v6 on v5

--- a/solution.py
+++ b/solution.py
@@ -59,16 +59,18 @@
     return v[0]
 
 
-def factor(rows, inv_rows):
+def factor(rows):
     n, w, b = len(rows), rows[0].shape[1], GRP
     sub = lax.broadcasted_iota(jnp.int32, (8, w), 0)
+    lane = lax.broadcasted_iota(jnp.int32, (8, w), 1)
     full = lambda v: jnp.broadcast_to(v, (8, w))
     for p in range(n):
         j = 8 * p
         cols = [full(rows[p][:, j + m : j + m + 1]) for m in range(b)]
         d = [[full(cols[m][i : i + 1, :]) for m in range(i + 1)] for i in range(b)]
-        row = [full(rows[p][m : m + 1, :]) for m in range(b)]
-        erow = [full(inv_rows[p][m : m + 1, :]) for m in range(b)]
+        group = (lane >= j) & (lane < j + b)
+        own = jnp.where(group, jnp.where(lane == sub + j, 1.0, 0.0), rows[p])
+        row = [full(own[m : m + 1, :]) for m in range(b)]
         v = [[None] * b for _ in range(b)]
         low = [[None] * b for _ in range(b)]
         for i in range(b):
@@ -82,28 +84,31 @@
             for t in range(i):
                 v[i][t] = -(rt * total([low[i][k] * v[k][t] for k in range(t, i)]))
         r = [total([v[i][m] * row[m] for m in range(i + 1)]) for i in range(b)]
-        e = [total([v[i][m] * erow[m] for m in range(i + 1)]) for i in range(b)]
         z = [total([v[i][m] * r[i] for i in range(m, b)]) for m in range(b)]
-        ze = [total([v[i][m] * e[i] for i in range(m, b)]) for m in range(b)]
-        for q in range(p + 1, n):
+        for q in range(p + 1, min(p + 2, n)):
             c = [full(rows[q][:, j + m : j + m + 1]) for m in range(b)]
-            rows[q] = rows[q] - total([c[m] * z[m] for m in range(b)])
-            inv_rows[q] = inv_rows[q] - total([c[m] * ze[m] for m in range(b)])
-        y = e[0]
+            rows[q] = jnp.where(group, 0.0, rows[q]) - total([c[m] * z[m] for m in range(b)])
+        if p + 2 < n:
+            far = jnp.concatenate(rows[p + 2 :], axis=0)
+            terms = z[0]
+            for m in range(1, b):
+                terms = jnp.where(sub == m, z[m], terms)
+            update = dot3(jnp.where(group[:1], far, 0.0), jnp.concatenate([terms] * (w // 8), axis=0), NN)
+            far = jnp.where(group[:1], 0.0, far) - update
+            for q in range(p + 2, n):
+                rows[q] = far[8 * (q - p - 2) : 8 * (q - p - 1), :]
+        y = r[0]
         for i in range(1, b):
-            y = jnp.where(sub == i, e[i], y)
-        inv_rows[p] = y
-    return inv_rows
+            y = jnp.where(sub == i, r[i], y)
+        rows[p] = jnp.where(lane < j + b, y, 0.0)
+    return rows
 
 
 def inverse_factor(a_ref, w_ref):
-    ri = lax.broadcasted_iota(jnp.int32, (8, NB), 0)
-    ci = lax.broadcasted_iota(jnp.int32, (8, NB), 1)
     for lo in range(0, N, NB):
         hi = lo + NB
         rows = [a_ref[lo + 8 * p : lo + 8 * p + 8, lo:hi] for p in range(NB // 8)]
-        inv = factor(rows, [(ci == ri + 8 * p).astype(F) for p in range(NB // 8)])
-        wkk = jnp.concatenate(inv, axis=0)
+        wkk = jnp.concatenate(factor(rows), axis=0)
         w_ref[lo:hi, lo:hi] = wkk
         if hi < N:
             w_ref[lo:hi, hi:] = jnp.zeros((NB, N - hi), F)
@@ -117,6 +122,35 @@
             if lo > 0:
                 w_ref[hi:, :lo] = w_ref[hi:, :lo] - upd[:, :lo]
             w_ref[hi:, lo:hi] = -upd[:, lo:]
+
+
+def front_kernel(momentum, gradient, basis, part, blend, basis16):
+    @pl.when(pl.program_id(0) == 0)
+    def _():
+        basis16[...] = basis[...].astype(B)
+
+    x = (momentum[...] + gradient[...].astype(F)).astype(B)
+    blend[...] = x
+    part[...] = dot(x, basis16[...], NN).astype(B)
+
+
+def front(momentum, gradient, basis):
+    rows, cols = momentum.shape
+    step = rows // 4
+    return pl.pallas_call(
+        front_kernel,
+        grid=(4,),
+        out_shape=[jax.ShapeDtypeStruct((rows, N), B), jax.ShapeDtypeStruct((rows, cols), B)],
+        in_specs=[
+            pl.BlockSpec((step, cols), lambda i: (i, 0)),
+            pl.BlockSpec((step, cols), lambda i: (i, 0)),
+            pl.BlockSpec((cols, N), lambda i: (0, 0)),
+        ],
+        out_specs=[pl.BlockSpec((step, N), lambda i: (i, 0)), pl.BlockSpec((step, cols), lambda i: (i, 0))],
+        scratch_shapes=[pltpu.VMEM((cols, N), B)],
+        compiler_params=pltpu.CompilerParams(vmem_limit_bytes=16 * 2**20),
+        name="front",
+    )(momentum, gradient, basis)
 
 
 def spread_kernel(pieces, out):
@@ -261,9 +295,8 @@
     place = jnp.stack([lax.axis_index(axis) for axis in ("y", "c", "r")]).astype(jnp.int32)
     place, basis = lax.optimization_barrier((place, basis))
     momentum, gradient = momentum[0], gradient[0]
-    blend16 = (momentum + gradient.astype(F)).astype(B)
-    part = dot(blend16, basis[0].astype(B), NN).astype(B).reshape(16, -1, N)
-    blend16, part = lax.optimization_barrier((blend16, part))
+    part, blend16 = front(momentum, gradient, basis[0])
+    part = part.reshape(16, -1, N)
     (copies,) = call(spread_kernel, [(part.shape, B)], name="spread")(exchange(part, TP))
     left = exchange(copies, TP).reshape(-1, N)
 
@@ -275,24 +308,23 @@
         name="pieces",
     )(place, left, blend16)
     got = swap(send, "c")
-    left_o = swap(left, "r")
-    weight, _ = lax.optimization_barrier((weights[0], left))
-    weight_o = swap(weight, "r")
     own_g, own_r, *outs = call(
         join_kernel,
         [((GR, 256), F), ((RR, N), F)] + [((RR + GR, N), B)] * 3,
         smem=1,
         name="join",
     )(place, keep_g, keep_r, got)
+    early_left, weight, *outs = lax.optimization_barrier((left, weights[0], *outs))
+    left_o, weight_o = swap(early_left, "r"), swap(weight, "r")
     arrived = [swap(x, "y", k + 1) for k, x in enumerate(outs)]
     (piece,) = call(sum_kernel, [((RR + GR, N), B)], name="sum")(own_g, own_r, *arrived)
     (line,) = call(line_kernel, [((4, RR + GR, N), B)], smem=1, name="line")(
         place, piece, *[swap(piece, "y", k) for k in (1, 2, 3)]
     )
-    line, left_o, weight_o = lax.optimization_barrier((line, left_o, weight_o))
     other_core = swap(line, "c")
     (raw,) = call(rows_kernel, [((8 * RR, N), B)], smem=1, name="rows")(place, line, other_core)
     raw_o = swap(raw, "r")
+    left, left_o, weight_o = lax.optimization_barrier((left, left_o, weight_o))
 
     w16, ortho, right, squares = call(
         solve_kernel,

time: 143 us -> 165 us (1.15)
  waiting for transfers between devices: 24.9 us -> 51.3 us
  Pallas kernels: 35.2 us -> 30.4 us
  local copies, waits for them, and re-layouts: 0.51 us -> 4.23 us
  starting transfers between devices: 17.7 us -> 20.4 us
  matrix products: 2.25 us -> 0 us
  other arithmetic: 2.16 us -> 0.08 us
  blocking collectives: 57.9 us -> 56.2 us
    ppermute x12, waiting for transfers between devices: 24.9 us -> 51.3 us  [swap(): lax.ppermute(x, axis, [(i, i ^ bit) for i in range(lax.axis_size(axis))])]
    pallas_call x8, Pallas kernels: 35.2 us -> 29 us  [run(): pl.pallas_call(kernel, out_shape=[jax.ShapeDtypeStruct(s, d) for s, d in...]
    unnamed x6 -> x12, local copies, waits for them, and re-layouts: 0.47 us -> 4.2 us
    ppermute x12, starting transfers between devices: 17.7 us -> 20.4 us  [swap(): lax.ppermute(x, axis, [(i, i ^ bit) for i in range(lax.axis_size(axis))])]
    dot_general x1 -> x0, matrix products: 2.25 us -> none  [dot(): return lax.dot_general(p, q, (over, ((), ())), preferred_element_type=F)]
    convert_element_type x1 -> x0, other arithmetic: 2.09 us -> none  [body(): blend16 = (momentum + gradient.astype(F)).astype(B)]
    all_to_all x3, blocking collectives: 57.9 us -> 56.2 us  [exchange(): return lax.all_to_all(x, axis, 0, 0, tiled=True)]
  transfers between devices with their start and end apart: 12 -> 12, of which waited for: 6 -> 6; matrix products, arithmetic and copies ran while one was open for 0% -> 0% of each run, Pallas kernels for 19% -> 12%
where the time goes in v6:
time: 165 us; the launch traced here: 164 us
  blocking collectives  56.2 us (34%)
  waiting for transfers between devices  51.3 us (31%)
  Pallas kernels  30.4 us (18%)
  starting transfers between devices  20.4 us (12%)
  local copies, waits for them, and re-layouts  4.23 us (3%)
    all_to_all x3, blocking collectives, exchange(): return lax.all_to_all(x, axis, 0, 0, tiled=True)  56.2 us
    ppermute x12, waiting for transfers between devices, swap(): lax.ppermute(x, axis, [(i, i ^ bit) for i in range(lax.axis_size(axis))])  51.3 us
    pallas_call x8, Pallas kernels, run(): pl.pallas_call(kernel, out_shape=[jax.ShapeDtypeStruct(s, d) for s, d in...  29 us
    ppermute x12, starting transfers between devices, swap(): lax.ppermute(x, axis, [(i, i ^ bit) for i in range(lax.axis_size(axis))])  20.4 us
    unnamed x12, local copies, waits for them, and re-layouts  4.2 us
  transfers between devices with their start and end apart: 12, of which 6 were waited for; matrix products, arithmetic and copies ran while one was open for 0% of the time, Pallas kernels for 12%

profile of v6, /device:TPU:1, one launch (start us, length us, event | category | flops | bytes accessed | tf_op | source)
XLA Modules:
  0.0 163.6 jit_solution(8797141433456554364)
XLA Ops:
  0.6 0.1 pad_add_fusion.place
  0.7 1.5 copy-done
  2.2 1.2 copy-done.2
  3.4 1.5 copy-done.4
  4.9 1.4 front.1
  6.3 23.6 %all_to_all.15.pieces = bf16[16,32,512]{2,1,0:T(8,128)(2,1)S(1)} all-to-all(bf16[16,32,512]{2,1,0:T(8,128)(2,1)S(1)} %bitcast.24), channel_id=1, replica_groups=mesh['y'=4,'c'=2,'x'=2,'z'=8,'r'=2] {'x','z'}, dimensions={0} | all-to-all | bytes 1048576 | tf_op jit(solution)/shard_map/all_to_all | solution.py:287
  29.9 0.1 spread.1
  30.0 18.7 %all_to_all.16 = bf16[16,32,512]{2,1,0:T(8,128)(2,1)S(1)} all-to-all(bf16[16,32,512]{2,1,0:T(8,128)(2,1)S(1)} %spread.1), channel_id=1, replica_groups=mesh['y'=4,'c'=2,'x'=2,'z'=8,'r'=2] {'x','z'}, dimensions={0} | all-to-all | bytes 1048576 | tf_op jit(solution)/shard_map/all_to_all | solution.py:287
  48.7 1.6 pieces.1
  50.2 3.2 %collective-permute-start = (bf16[4,208,512]{2,1,0:T(8,128)(2,1)S(1)}, bf16[4,208,512]{2,1,0:T(8,128)(2,1)S(1)}, u32[]{:S(2)}, u32[]{:S(2)}) collective-permute-start(bf16[4,208,512]{2,1,0:T(8,128)(2,1)S(1)} %get-tuple-element.38), channel_id=1, source_target_pairs={{0,32},{32,0},{1,33},{33,1},{2,34},{34,2},{3,35},{35,3},{4,36},{36... | collective-permute-start | bytes 2555912 | tf_op jit(solution)/shard_map/ppermute | solution.py:291
  53.4 2.0 %collective-permute-done.got = bf16[4,208,512]{2,1,0:T(8,128)(2,1)S(1)} collective-permute-done((bf16[4,208,512]{2,1,0:T(8,128)(2,1)S(1)}, bf16[4,208,512]{2,1,0:T(8,128)(2,1)S(1)}, u32[]{:S(2)}, u32[]{:S(2)}) %collective-permute-start) | collective-permute-done | bytes 852000 | tf_op jit(solution)/shard_map/ppermute | solution.py:291
  55.4 0.7 join.1
  56.2 1.4 collective-permute-start.1
  57.5 2.6 %collective-permute-start.2 = (bf16[208,512]{1,0:T(8,128)(2,1)S(1)}, bf16[208,512]{1,0:T(8,128)(2,1)S(1)}, u32[]{:S(2)}, u32[]{:S(2)}) collective-permute-start(bf16[208,512]{1,0:T(8,128)(2,1)S(1)} %get-tuple-element.45), channel_id=1, source_target_pairs={{0,128},{64,192},{128,0},{192,64},{1,129},{65,193},{129,1},{193,65... | collective-permute-start | bytes 638984 | tf_op jit(solution)/shard_map/ppermute | solution.py:291
  60.2 2.6 %collective-permute-done.1.one = bf16[208,512]{1,0:T(8,128)(2,1)S(1)} collective-permute-done((bf16[208,512]{1,0:T(8,128)(2,1)S(1)}, bf16[208,512]{1,0:T(8,128)(2,1)S(1)}, u32[]{:S(2)}, u32[]{:S(2)}) %collective-permute-start.1) | collective-permute-done | bytes 213024 | tf_op jit(solution)/shard_map/ppermute | solution.py:291
  62.7 7.1 %collective-permute-done.2.two = bf16[208,512]{1,0:T(8,128)(2,1)S(1)} collective-permute-done((bf16[208,512]{1,0:T(8,128)(2,1)S(1)}, bf16[208,512]{1,0:T(8,128)(2,1)S(1)}, u32[]{:S(2)}, u32[]{:S(2)}) %collective-permute-start.2) | collective-permute-done | bytes 213024 | tf_op jit(solution)/shard_map/ppermute | solution.py:291
  69.8 2.1 %collective-permute-done.3.three = bf16[208,512]{1,0:T(8,128)(2,1)S(1)} collective-permute-done((bf16[208,512]{1,0:T(8,128)(2,1)S(1)}, bf16[208,512]{1,0:T(8,128)(2,1)S(1)}, u32[]{:S(2)}, u32[]{:S(2)}) %collective-permute-start.3) | collective-permute-done | bytes 213024 | tf_op jit(solution)/shard_map/ppermute | solution.py:291
  71.9 0.1 sum.1.own
  72.0 0.2 collective-permute-start.6
  72.2 3.1 %collective-permute-start.4 = (bf16[208,512]{1,0:T(8,128)(2,1)S(1)}, bf16[208,512]{1,0:T(8,128)(2,1)S(1)}, u32[]{:S(2)}, u32[]{:S(2)}) collective-permute-start(bf16[208,512]{1,0:T(8,128)(2,1)S(1)} %sum.1.own), channel_id=1, source_target_pairs={{0,64},{64,0},{128,192},{192,128},{1,65},{65,1},{129,193},{193,129... | collective-permute-start | bytes 638984 | tf_op jit(solution)/shard_map/ppermute | solution.py:291
  75.4 9.2 %collective-permute-done.6.three = bf16[208,512]{1,0:T(8,128)(2,1)S(1)} collective-permute-done((bf16[208,512]{1,0:T(8,128)(2,1)S(1)}, bf16[208,512]{1,0:T(8,128)(2,1)S(1)}, u32[]{:S(2)}, u32[]{:S(2)}) %collective-permute-start.6) | collective-permute-done | bytes 213024 | tf_op jit(solution)/shard_map/ppermute | solution.py:291
  84.6 0.6 line.1.own
  85.2 1.7 %collective-permute-start.7 = (bf16[4,208,512]{2,1,0:T(8,128)(2,1)S(1)}, bf16[4,208,512]{2,1,0:T(8,128)(2,1)S(1)}, u32[]{:S(2)}, u32[]{:S(2)}) collective-permute-start(bf16[4,208,512]{2,1,0:T(8,128)(2,1)S(1)} %line.1.own), channel_id=1, source_target_pairs={{0,32},{32,0},{1,33},{33,1},{2,34},{34,2},{3,35},{35,3},{4,36},{36... | collective-permute-start | bytes 2555912 | tf_op jit(solution)/shard_map/ppermute | solution.py:291
  86.9 2.5 %collective-permute-start.9 = (bf16[512,896]{1,0:T(8,128)(2,1)S(1)}, bf16[512,896]{1,0:T(8,128)(2,1)S(1)}, u32[]{:S(2)}, u32[]{:S(2)}) collective-permute-start(bf16[512,896]{1,0:T(8,128)(2,1)S(1)} %bitcast.22), channel_id=1, source_target_pairs={{0,1},{1,0},{2,3},{3,2},{4,5},{5,4},{6,7},{7,6},{8,9},{9,8},{10,11... | collective-permute-start | bytes 2752520 | tf_op jit(solution)/shard_map/ppermute | solution.py:291
  89.4 0.5 collective-permute-start.8
  89.9 0.6 rows.1.right_in.right0
  90.5 2.7 %collective-permute-start.11 = (bf16[896,512]{1,0:T(8,128)(2,1)S(1)}, bf16[896,512]{1,0:T(8,128)(2,1)S(1)}, u32[]{:S(2)}, u32[]{:S(2)}) collective-permute-start(bf16[896,512]{1,0:T(8,128)(2,1)S(1)} %rows.1.right_in.right0), channel_id=1, source_target_pairs={{0,1},{1,0},{2,3},{3,2},{4,5},{5,4},{6,7},{7,6},{8,9},{9,8},{10,11... | collective-permute-start | bytes 2752520 | tf_op jit(solution)/shard_map/ppermute | solution.py:291
  93.2 28.3 %collective-permute-done.8.left1 = bf16[512,512]{1,0:T(8,128)(2,1)S(1)} collective-permute-done((bf16[512,512]{1,0:T(8,128)(2,1)S(1)}, bf16[512,512]{1,0:T(8,128)(2,1)S(1)}, u32[]{:S(2)}, u32[]{:S(2)}) %collective-permute-start.8) | collective-permute-done | bytes 524320 | tf_op jit(solution)/shard_map/ppermute | solution.py:291
  121.6 19.0 %solve.1 = (bf16[384,512]{1,0:T(8,128)(2,1)S(1)}, bf16[512,512]{1,0:T(8,128)(2,1)S(1)}, f32[896,512]{1,0:T(8,128)S(1)}, f32[1,512]{1,0:T(1,128)S(1)}) custom-call(s32[3]{0:T(128)S(1)} %pad_add_fusion.place, bf16[4,208,512]{2,1,0:T(8,128)(2,1)S(1)} %line.1.own, bf16[4,208,512]{2,1,0:T(8,128)(2,1)S(1)} %collective-permute-done.7.got, ...), custom_call_target="tpu_custom_call" | custom-call | tf_op jit(solution)/shard_map/solve/pallas_call | solution.py:25
  140.6 2.5 %collective-permute-start.10 = (bf16[384,512]{1,0:T(8,128)(2,1)S(1)}, bf16[384,512]{1,0:T(8,128)(2,1)S(1)}, u32[]{:S(2)}, u32[]{:S(2)}) collective-permute-start(bf16[384,512]{1,0:T(8,128)(2,1)S(1)} %get-tuple-element.53.w0), channel_id=1, source_target_pairs={{0,1},{1,0},{2,3},{3,2},{4,5},{5,4},{6,7},{7,6},{8,9},{9,8},{10,11... | collective-permute-start | bytes 1179656 | tf_op jit(solution)/shard_map/ppermute | solution.py:291
  143.1 13.9 %all_to_all.17.sums = f32[32,1,512]{2,1,0:T(1,128)S(1)} all-to-all(f32[32,1,512]{2,1,0:T(1,128)S(1)} %broadcast_in_dim.18), channel_id=1, replica_groups=mesh['y'=4,'c'=2,'x'=2,'z'=8,'r'=2] {'x','z','r'}, dimensions={0} | all-to-all | bytes 131072 | tf_op jit(solution)/shard_map/all_to_all | solution.py:287
  157.1 6.4 %last.1 = (bf16[512,896]{1,0:T(8,128)(2,1)}, f32[512,896]{1,0:T(8,128)}, f32[896,512]{1,0:T(8,128)}, bf16[2,512,896]{2,1,0:T(8,128)(2,1)}) custom-call(s32[3]{0:T(128)S(1)} %pad_add_fusion.place, f32[32,1,512]{2,1,0:T(1,128)S(1)} %all_to_all.17.sums, f32[512,896]{1,0:T(8,128)S(1)} %bitcast.18, bf16[512,896]{1,0:T(8,128)(2,1)S(1)} %bitcast.20, ...), custom_call_target="tpu_custom_call" | custom-call | tf_op jit(solution)/shard_map/last/pallas_call | solution.py:25
  (18 shorter events, 0.1 us)
Async XLA Ops:
  0.7 1.5 copy-start
  2.2 1.2 copy-start.2
  3.4 1.5 copy-start.4
  50.2 5.2 %collective-permute-start = (bf16[4,208,512]{2,1,0:T(8,128)(2,1)S(1)}, bf16[4,208,512]{2,1,0:T(8,128)(2,1)S(1)}, u32[]{:S(2)}, u32[]{:S(2)}) collective-permute-start(bf16[4,208,512]{2,1,0:T(8,128)(2,1)S(1)} %get-tuple-element.38), channel_id=1, source_target_pairs={{0,32},{32,0},{1,33},{33,1},{2,34},{34,2},{3,35},{35,3},{4,36},{36... | collective-permute-start | bytes 2555912 | tf_op jit(solution)/shard_map/ppermute | solution.py:291
  56.2 30.7 %copy-start.5 = (bf16[1,512,896]{2,1,0:T(8,128)(2,1)S(1)}, bf16[1,512,896]{2,1,0:T(8,128)(2,1)}, u32[]{:S(2)}) copy-start(bf16[1,512,896]{2,1,0:T(8,128)(2,1)} %param.4) | copy-start | bytes 2752516
  56.2 6.6 %collective-permute-start.1 = (bf16[208,512]{1,0:T(8,128)(2,1)S(1)}, bf16[208,512]{1,0:T(8,128)(2,1)S(1)}, u32[]{:S(2)}, u32[]{:S(2)}) collective-permute-start(bf16[208,512]{1,0:T(8,128)(2,1)S(1)} %get-tuple-element.44), channel_id=1, source_target_pairs={{0,64},{64,0},{128,192},{192,128},{1,65},{65,1},{129,193},{193,129... | collective-permute-start | bytes 638984 | tf_op jit(solution)/shard_map/ppermute | solution.py:291
  57.5 12.2 %collective-permute-start.2 = (bf16[208,512]{1,0:T(8,128)(2,1)S(1)}, bf16[208,512]{1,0:T(8,128)(2,1)S(1)}, u32[]{:S(2)}, u32[]{:S(2)}) collective-permute-start(bf16[208,512]{1,0:T(8,128)(2,1)S(1)} %get-tuple-element.45), channel_id=1, source_target_pairs={{0,128},{64,192},{128,0},{192,64},{1,129},{65,193},{129,1},{193,65... | collective-permute-start | bytes 638984 | tf_op jit(solution)/shard_map/ppermute | solution.py:291
  60.2 11.8 %collective-permute-start.3 = (bf16[208,512]{1,0:T(8,128)(2,1)S(1)}, bf16[208,512]{1,0:T(8,128)(2,1)S(1)}, u32[]{:S(2)}, u32[]{:S(2)}) collective-permute-start(bf16[208,512]{1,0:T(8,128)(2,1)S(1)} %get-tuple-element.46), channel_id=1, source_target_pairs={{0,192},{64,128},{128,64},{192,0},{1,193},{65,129},{129,65},{193,1... | collective-permute-start | bytes 638984 | tf_op jit(solution)/shard_map/ppermute | solution.py:291
  72.0 12.6 %collective-permute-start.6 = (bf16[208,512]{1,0:T(8,128)(2,1)S(1)}, bf16[208,512]{1,0:T(8,128)(2,1)S(1)}, u32[]{:S(2)}, u32[]{:S(2)}) collective-permute-start(bf16[208,512]{1,0:T(8,128)(2,1)S(1)} %sum.1.own), channel_id=1, source_target_pairs={{0,192},{64,128},{128,64},{192,0},{1,193},{65,129},{129,65},{193,1... | collective-permute-start | bytes 638984 | tf_op jit(solution)/shard_map/ppermute | solution.py:291
  72.2 12.4 %collective-permute-start.5 = (bf16[208,512]{1,0:T(8,128)(2,1)S(1)}, bf16[208,512]{1,0:T(8,128)(2,1)S(1)}, u32[]{:S(2)}, u32[]{:S(2)}) collective-permute-start(bf16[208,512]{1,0:T(8,128)(2,1)S(1)} %sum.1.own), channel_id=1, source_target_pairs={{0,128},{64,192},{128,0},{192,64},{1,129},{65,193},{129,1},{193,65... | collective-permute-start | bytes 638984 | tf_op jit(solution)/shard_map/ppermute | solution.py:291
  72.2 12.4 %collective-permute-start.4 = (bf16[208,512]{1,0:T(8,128)(2,1)S(1)}, bf16[208,512]{1,0:T(8,128)(2,1)S(1)}, u32[]{:S(2)}, u32[]{:S(2)}) collective-permute-start(bf16[208,512]{1,0:T(8,128)(2,1)S(1)} %sum.1.own), channel_id=1, source_target_pairs={{0,64},{64,0},{128,192},{192,128},{1,65},{65,1},{129,193},{193,129... | collective-permute-start | bytes 638984 | tf_op jit(solution)/shard_map/ppermute | solution.py:291
  85.2 4.7 %collective-permute-start.7 = (bf16[4,208,512]{2,1,0:T(8,128)(2,1)S(1)}, bf16[4,208,512]{2,1,0:T(8,128)(2,1)S(1)}, u32[]{:S(2)}, u32[]{:S(2)}) collective-permute-start(bf16[4,208,512]{2,1,0:T(8,128)(2,1)S(1)} %line.1.own), channel_id=1, source_target_pairs={{0,32},{32,0},{1,33},{33,1},{2,34},{34,2},{3,35},{35,3},{4,36},{36... | collective-permute-start | bytes 2555912 | tf_op jit(solution)/shard_map/ppermute | solution.py:291
  86.9 34.7 %collective-permute-start.9 = (bf16[512,896]{1,0:T(8,128)(2,1)S(1)}, bf16[512,896]{1,0:T(8,128)(2,1)S(1)}, u32[]{:S(2)}, u32[]{:S(2)}) collective-permute-start(bf16[512,896]{1,0:T(8,128)(2,1)S(1)} %bitcast.22), channel_id=1, source_target_pairs={{0,1},{1,0},{2,3},{3,2},{4,5},{5,4},{6,7},{7,6},{8,9},{9,8},{10,11... | collective-permute-start | bytes 2752520 | tf_op jit(solution)/shard_map/ppermute | solution.py:291
  89.4 32.2 %collective-permute-start.8 = (bf16[512,512]{1,0:T(8,128)(2,1)S(1)}, bf16[512,512]{1,0:T(8,128)(2,1)S(1)}, u32[]{:S(2)}, u32[]{:S(2)}) collective-permute-start(bf16[512,512]{1,0:T(8,128)(2,1)S(1)} %bitcast.14), channel_id=1, source_target_pairs={{0,1},{1,0},{2,3},{3,2},{4,5},{5,4},{6,7},{7,6},{8,9},{9,8},{10,11... | collective-permute-start | bytes 1572872 | tf_op jit(solution)/shard_map/ppermute | solution.py:291
  90.5 66.5 %copy-start.1 = (f32[1,512,896]{2,1,0:T(8,128)S(1)}, f32[1,512,896]{2,1,0:T(8,128)}, u32[]{:S(2)}) copy-start(f32[1,512,896]{2,1,0:T(8,128)} %param.6) | copy-start | bytes 5505028
  90.5 66.5 %copy-start.3 = (bf16[1,512,896]{2,1,0:T(8,128)(2,1)S(1)}, bf16[1,512,896]{2,1,0:T(8,128)(2,1)}, u32[]{:S(2)}) copy-start(bf16[1,512,896]{2,1,0:T(8,128)(2,1)} %param.5) | copy-start | bytes 2752516
  90.5 66.5 %collective-permute-start.11 = (bf16[896,512]{1,0:T(8,128)(2,1)S(1)}, bf16[896,512]{1,0:T(8,128)(2,1)S(1)}, u32[]{:S(2)}, u32[]{:S(2)}) collective-permute-start(bf16[896,512]{1,0:T(8,128)(2,1)S(1)} %rows.1.right_in.right0), channel_id=1, source_target_pairs={{0,1},{1,0},{2,3},{3,2},{4,5},{5,4},{6,7},{7,6},{8,9},{9,8},{10,11... | collective-permute-start | bytes 2752520 | tf_op jit(solution)/shard_map/ppermute | solution.py:291
  140.6 16.5 %collective-permute-start.10 = (bf16[384,512]{1,0:T(8,128)(2,1)S(1)}, bf16[384,512]{1,0:T(8,128)(2,1)S(1)}, u32[]{:S(2)}, u32[]{:S(2)}) collective-permute-start(bf16[384,512]{1,0:T(8,128)(2,1)S(1)} %get-tuple-element.53.w0), channel_id=1, source_target_pairs={{0,1},{1,0},{2,3},{3,2},{4,5},{5,4},{6,7},{7,6},{8,9},{9,8},{10,11... | collective-permute-start | bytes 1179656 | tf_op jit(solution)/shard_map/ppermute | solution.py:291

commit v7 on v6

--- a/solution.py
+++ b/solution.py
@@ -16,6 +16,7 @@
 GRP = 8
 GR = 96
 RR = 112
+EARLY = 384
 VMEM = pl.BlockSpec(memory_space=pltpu.VMEM)
 SMEM = pl.BlockSpec(memory_space=pltpu.SMEM)
 
@@ -124,31 +125,41 @@
             w_ref[hi:, lo:hi] = -upd[:, lo:]
 
 
-def front_kernel(momentum, gradient, basis, part, blend, basis16):
-    @pl.when(pl.program_id(0) == 0)
-    def _():
-        basis16[...] = basis[...].astype(B)
-
-    x = (momentum[...] + gradient[...].astype(F)).astype(B)
-    blend[...] = x
-    part[...] = dot(x, basis16[...], NN).astype(B)
+def front_kernel(momentum, gradient, basis, part, blend, m_ref, g_ref, b_ref, sems):
+    steps = 4
+    step = m_ref.shape[0] // steps
+    copies = [pltpu.make_async_copy(basis, b_ref, sems.at[2 * steps])]
+    for k in range(steps):
+        rows = pl.ds(k * step, step)
+        copies.append(pltpu.make_async_copy(momentum.at[rows], m_ref.at[rows], sems.at[2 * k]))
+        copies.append(pltpu.make_async_copy(gradient.at[rows], g_ref.at[rows], sems.at[2 * k + 1]))
+    for copy in copies:
+        copy.start()
+    copies[0].wait()
+    basis16 = b_ref[...].astype(B)
+    for k in range(steps):
+        copies[2 * k + 1].wait()
+        copies[2 * k + 2].wait()
+        rows = pl.ds(k * step, step)
+        x = (m_ref[rows] + g_ref[rows].astype(F)).astype(B)
+        blend[rows] = x
+        part[rows] = dot(x, basis16, NN).astype(B)
 
 
 def front(momentum, gradient, basis):
     rows, cols = momentum.shape
-    step = rows // 4
     return pl.pallas_call(
         front_kernel,
-        grid=(4,),
         out_shape=[jax.ShapeDtypeStruct((rows, N), B), jax.ShapeDtypeStruct((rows, cols), B)],
-        in_specs=[
-            pl.BlockSpec((step, cols), lambda i: (i, 0)),
-            pl.BlockSpec((step, cols), lambda i: (i, 0)),
-            pl.BlockSpec((cols, N), lambda i: (0, 0)),
+        in_specs=[pl.BlockSpec(memory_space=pltpu.HBM)] * 3,
+        out_specs=[VMEM] * 2,
+        scratch_shapes=[
+            pltpu.VMEM((rows, cols), F),
+            pltpu.VMEM((rows, cols), B),
+            pltpu.VMEM((cols, N), F),
+            pltpu.SemaphoreType.DMA((9,)),
         ],
-        out_specs=[pl.BlockSpec((step, N), lambda i: (i, 0)), pl.BlockSpec((step, cols), lambda i: (i, 0))],
-        scratch_shapes=[pltpu.VMEM((cols, N), B)],
-        compiler_params=pltpu.CompilerParams(vmem_limit_bytes=16 * 2**20),
+        compiler_params=pltpu.CompilerParams(vmem_limit_bytes=60 * 2**20),
         name="front",
     )(momentum, gradient, basis)
 
@@ -216,7 +227,12 @@
         out[place[0] ^ k] = got[...]
 
 
-def rows_kernel(place, own, got, right):
+def rows_kernel(place, own, got, weight, right):
+    late = weight.shape[0] - EARLY
+    wide = weight.shape[1] - N
+    right[8 * RR : 8 * RR + late, :] = weight[EARLY:, :N]
+    right[8 * RR + late :, :wide] = weight[EARLY:, N:]
+    right[8 * RR + late :, wide:] = jnp.zeros((late, N - wide), B)
     for y in range(4):
         for c, part in ((place[1], own), (1 - place[1], got)):
             right[pl.ds(pl.multiple_of((2 * y + c) * RR, 16), RR), :] = part[y, :RR, :]
@@ -240,7 +256,8 @@
     w16[256:, :256] = wh[:128, :256]
     w16[256:, 256:] = wh[128:256, :256]
     ortho[...] = (dot(left[...], wh, NT) + dot(left[...], wl, NT)).astype(B)
-    r = dot(right_in[...], wh, NT) + dot(right_in[...], wl, NT)
+    raw = right_in[: 8 * RR, :]
+    r = dot(raw, wh, NT) + dot(raw, wl, NT)
     right[...] = r
     squares[...] = jnp.sum(r * r, axis=0, keepdims=True)
 
@@ -271,8 +288,16 @@
         w[128:256, :256] = packed_w[256:, 256:]
         w[:256, 256:] = jnp.zeros((256, 256), B)
         o = (dot(left[...], w[...], NT) * scale[half]).astype(B)
-        r = dot(raw[...], w[...], NT).astype(B)
-        weight[half] = (old[...].astype(F) - 0.3 * dot(o, r, NT)).astype(B)
+        r = dot(raw[: 8 * RR, :], w[...], NT).astype(B)
+        update = 0.3 * dot(o, r, NT)
+        if half == 0:
+            weight[half] = (old[...].astype(F) - update).astype(B)
+        else:
+            late, wide = update.shape[0] - EARLY, update.shape[1] - N
+            weight[half, :EARLY] = (old[...].astype(F) - update[:EARLY]).astype(B)
+            low, high = raw[8 * RR : 8 * RR + late, :], raw[8 * RR + late :, :wide]
+            weight[half, EARLY:, :N] = (low.astype(F) - update[EARLY:, :N]).astype(B)
+            weight[half, EARLY:, N:] = (high.astype(F) - update[EARLY:, N:]).astype(B)
         side = place[2] if half == 0 else 1 - place[2]
         copies.append(pltpu.make_async_copy(weight.at[half], out_rollout.at[side], sems.at[2 + half]))
         copies[-1].start()
@@ -308,23 +333,25 @@
         name="pieces",
     )(place, left, blend16)
     got = swap(send, "c")
+    left_o = swap(left, "r")
+    weight, _ = lax.optimization_barrier((weights[0, :EARLY], left))
+    weight_o = swap(weight, "r")
     own_g, own_r, *outs = call(
         join_kernel,
         [((GR, 256), F), ((RR, N), F)] + [((RR + GR, N), B)] * 3,
         smem=1,
         name="join",
     )(place, keep_g, keep_r, got)
-    early_left, weight, *outs = lax.optimization_barrier((left, weights[0], *outs))
-    left_o, weight_o = swap(early_left, "r"), swap(weight, "r")
     arrived = [swap(x, "y", k + 1) for k, x in enumerate(outs)]
     (piece,) = call(sum_kernel, [((RR + GR, N), B)], name="sum")(own_g, own_r, *arrived)
     (line,) = call(line_kernel, [((4, RR + GR, N), B)], smem=1, name="line")(
         place, piece, *[swap(piece, "y", k) for k in (1, 2, 3)]
     )
+    line, left_o, weight_o = lax.optimization_barrier((line, left_o, weight_o))
     other_core = swap(line, "c")
-    (raw,) = call(rows_kernel, [((8 * RR, N), B)], smem=1, name="rows")(place, line, other_core)
+    late = 2 * (weights.shape[1] - EARLY)
+    (raw,) = call(rows_kernel, [((8 * RR + late, N), B)], smem=1, name="rows")(place, line, other_core, weights[0])
     raw_o = swap(raw, "r")
-    left, left_o, weight_o = lax.optimization_barrier((left, left_o, weight_o))
 
     w16, ortho, right, squares = call(
         solve_kernel,
@@ -335,7 +362,7 @@
     )(place, line, other_core, left, raw)
     w16_o = swap(w16, "r")
     sums = exchange(jnp.broadcast_to(squares[None], (32, 1, N)), ("x", "z", "r"))
-    wide, tall = weight.shape, right.shape
+    wide, tall = momentum.shape, right.shape
     weight_new, moment_new, basis_new, rollout = call(
         last_kernel,
         [(wide, B), (wide, F), (tall, F), ((2, *wide), B)],

time: 165 us -> 134 us (0.81)
  waiting for transfers between devices: 51.3 us -> 23 us
  local copies, waits for them, and re-layouts: 4.23 us -> 0.11 us
  Pallas kernels: 30.4 us -> 32.9 us
  blocking collectives: 56.2 us -> 58.3 us
  starting transfers between devices: 20.4 us -> 18.6 us
    ppermute x12, waiting for transfers between devices: 51.3 us -> 23 us  [swap(): lax.ppermute(x, axis, [(i, i ^ bit) for i in range(lax.axis_size(axis))])]
    unnamed x12 -> x8, local copies, waits for them, and re-layouts: 4.2 us -> 0.02 us
    pallas_call x1, Pallas kernels: 1.37 us -> 3.87 us  [front(): pl.pallas_call(front_kernel, out_shape=[jax.ShapeDtypeStruct((rows, N), B...]
    all_to_all x3, blocking collectives: 56.2 us -> 58.3 us  [exchange(): return lax.all_to_all(x, axis, 0, 0, tiled=True)]
    ppermute x12, starting transfers between devices: 20.4 us -> 18.6 us  [swap(): lax.ppermute(x, axis, [(i, i ^ bit) for i in range(lax.axis_size(axis))])]
  transfers between devices with their start and end apart: 12 -> 12, of which waited for: 6 -> 5; matrix products, arithmetic and copies ran while one was open for 0% -> 0% of each run, Pallas kernels for 12% -> 15%
where the time goes in v7:
time: 134 us
  blocking collectives  58.3 us (44%)
  Pallas kernels  32.9 us (25%)
  waiting for transfers between devices  23 us (17%)
  starting transfers between devices  18.6 us (14%)
    all_to_all x3, blocking collectives, exchange(): return lax.all_to_all(x, axis, 0, 0, tiled=True)  58.3 us
    pallas_call x8, Pallas kernels, run(): pl.pallas_call(kernel, out_shape=[jax.ShapeDtypeStruct(s, d) for s, d in...  29 us
    ppermute x12, waiting for transfers between devices, swap(): lax.ppermute(x, axis, [(i, i ^ bit) for i in range(lax.axis_size(axis))])  23 us
    ppermute x12, starting transfers between devices, swap(): lax.ppermute(x, axis, [(i, i ^ bit) for i in range(lax.axis_size(axis))])  18.6 us
    pallas_call x1, Pallas kernels, front(): pl.pallas_call(front_kernel, out_shape=[jax.ShapeDtypeStruct((rows, N), B...  3.87 us
  transfers between devices with their start and end apart: 12, of which 5 were waited for; matrix products, arithmetic and copies ran while one was open for 0% of the time, Pallas kernels for 15%

profile of v7, /device:TPU:1, one launch (start us, length us, event | category | flops | bytes accessed | tf_op | source)
XLA Modules:
  0.0 134.0 jit_solution(9392487884839896295)
XLA Ops:
  0.6 0.1 pad_add_fusion.place
  0.7 3.9 %front.1 = (bf16[512,512]{1,0:T(8,128)(2,1)}, bf16[512,896]{1,0:T(8,128)(2,1)}) custom-call(f32[512,896]{1,0:T(8,128)} %bitcast.19, bf16[512,896]{1,0:T(8,128)(2,1)} %bitcast.23, f32[896,512]{1,0:T(8,128)} %bitcast.26), custom_call_target="tpu_custom_call" | custom-call | tf_op jit(solution)/shard_map/front/pallas_call | solution.py:151
  4.6 0.0 copy-start.3
  4.6 23.9 %all_to_all.15.pieces = bf16[16,32,512]{2,1,0:T(8,128)(2,1)S(1)} all-to-all(bf16[16,32,512]{2,1,0:T(8,128)(2,1)} %bitcast.27), channel_id=1, replica_groups=mesh['y'=4,'c'=2,'x'=2,'z'=8,'r'=2] {'x','z'}, dimensions={0} | all-to-all | bytes 1048576 | tf_op jit(solution)/shard_map/all_to_all | solution.py:312
  28.5 0.1 spread.1
  28.6 18.8 %all_to_all.16 = bf16[16,32,512]{2,1,0:T(8,128)(2,1)S(1)} all-to-all(bf16[16,32,512]{2,1,0:T(8,128)(2,1)S(1)} %spread.1), channel_id=1, replica_groups=mesh['y'=4,'c'=2,'x'=2,'z'=8,'r'=2] {'x','z'}, dimensions={0} | all-to-all | bytes 1048576 | tf_op jit(solution)/shard_map/all_to_all | solution.py:312
  47.5 1.6 %pieces.1 = (f32[4,96,256]{2,1,0:T(8,128)S(1)}, f32[4,112,512]{2,1,0:T(8,128)S(1)}, bf16[4,208,512]{2,1,0:T(8,128)(2,1)S(1)}) custom-call(s32[3]{0:T(128)S(1)} %pad_add_fusion.place, bf16[512,512]{1,0:T(8,128)(2,1)S(1)} %bitcast.15, bf16[512,896]{1,0:T(8,128)(2,1)S(1)} %copy-done.3), custom_call_target="tpu_custom_call" | custom-call | tf_op jit(solution)/shard_map/pieces/pallas_call | solution.py:26
  49.0 3.2 %collective-permute-start = (bf16[4,208,512]{2,1,0:T(8,128)(2,1)S(1)}, bf16[4,208,512]{2,1,0:T(8,128)(2,1)S(1)}, u32[]{:S(2)}, u32[]{:S(2)}) collective-permute-start(bf16[4,208,512]{2,1,0:T(8,128)(2,1)S(1)} %get-tuple-element.34), channel_id=1, source_target_pairs={{0,32},{32,0},{1,33},{33,1},{2,34},{34,2},{3,35},{35,3},{4,36},{36... | collective-permute-start | bytes 2555912 | tf_op jit(solution)/shard_map/ppermute | solution.py:316
  52.2 0.1 slice_bitcast_fusion
  52.3 2.5 %collective-permute-start.8 = (bf16[384,896]{1,0:T(8,128)(2,1)S(1)}, bf16[384,896]{1,0:T(8,128)(2,1)S(1)}, u32[]{:S(2)}, u32[]{:S(2)}) collective-permute-start(bf16[384,896]{1,0:T(8,128)(2,1)S(1)} %slice_bitcast_fusion), channel_id=1, source_target_pairs={{0,1},{1,0},{2,3},{3,2},{4,5},{5,4},{6,7},{7,6},{8,9},{9,8},{10,11... | collective-permute-start | bytes 2064392 | tf_op jit(solution)/shard_map/ppermute | solution.py:316
  54.8 0.5 collective-permute-start.7
  55.4 0.7 join.1
  56.1 1.4 %collective-permute-start.1 = (bf16[208,512]{1,0:T(8,128)(2,1)S(1)}, bf16[208,512]{1,0:T(8,128)(2,1)S(1)}, u32[]{:S(2)}, u32[]{:S(2)}) collective-permute-start(bf16[208,512]{1,0:T(8,128)(2,1)S(1)} %get-tuple-element.37), channel_id=1, source_target_pairs={{0,64},{64,0},{128,192},{192,128},{1,65},{65,1},{129,193},{193,129... | collective-permute-start | bytes 638984 | tf_op jit(solution)/shard_map/ppermute | solution.py:316
  57.5 2.6 %collective-permute-start.2 = (bf16[208,512]{1,0:T(8,128)(2,1)S(1)}, bf16[208,512]{1,0:T(8,128)(2,1)S(1)}, u32[]{:S(2)}, u32[]{:S(2)}) collective-permute-start(bf16[208,512]{1,0:T(8,128)(2,1)S(1)} %get-tuple-element.38), channel_id=1, source_target_pairs={{0,128},{64,192},{128,0},{192,64},{1,129},{65,193},{129,1},{193,65... | collective-permute-start | bytes 638984 | tf_op jit(solution)/shard_map/ppermute | solution.py:316
  60.1 2.3 %collective-permute-done.1.one = bf16[208,512]{1,0:T(8,128)(2,1)S(1)} collective-permute-done((bf16[208,512]{1,0:T(8,128)(2,1)S(1)}, bf16[208,512]{1,0:T(8,128)(2,1)S(1)}, u32[]{:S(2)}, u32[]{:S(2)}) %collective-permute-start.1) | collective-permute-done | bytes 213024 | tf_op jit(solution)/shard_map/ppermute | solution.py:316
  62.4 7.0 %collective-permute-done.2.two = bf16[208,512]{1,0:T(8,128)(2,1)S(1)} collective-permute-done((bf16[208,512]{1,0:T(8,128)(2,1)S(1)}, bf16[208,512]{1,0:T(8,128)(2,1)S(1)}, u32[]{:S(2)}, u32[]{:S(2)}) %collective-permute-start.2) | collective-permute-done | bytes 213024 | tf_op jit(solution)/shard_map/ppermute | solution.py:316
  69.4 2.4 %collective-permute-done.3.three = bf16[208,512]{1,0:T(8,128)(2,1)S(1)} collective-permute-done((bf16[208,512]{1,0:T(8,128)(2,1)S(1)}, bf16[208,512]{1,0:T(8,128)(2,1)S(1)}, u32[]{:S(2)}, u32[]{:S(2)}) %collective-permute-start.3) | collective-permute-done | bytes 213024 | tf_op jit(solution)/shard_map/ppermute | solution.py:316
  71.8 0.1 sum.1.own
  71.9 0.1 collective-permute-start.6
  72.1 0.1 collective-permute-start.5
  72.1 3.1 %collective-permute-start.4 = (bf16[208,512]{1,0:T(8,128)(2,1)S(1)}, bf16[208,512]{1,0:T(8,128)(2,1)S(1)}, u32[]{:S(2)}, u32[]{:S(2)}) collective-permute-start(bf16[208,512]{1,0:T(8,128)(2,1)S(1)} %sum.1.own), channel_id=1, source_target_pairs={{0,64},{64,0},{128,192},{192,128},{1,65},{65,1},{129,193},{193,129... | collective-permute-start | bytes 638984 | tf_op jit(solution)/shard_map/ppermute | solution.py:316
  75.3 9.2 %collective-permute-done.6.three = bf16[208,512]{1,0:T(8,128)(2,1)S(1)} collective-permute-done((bf16[208,512]{1,0:T(8,128)(2,1)S(1)}, bf16[208,512]{1,0:T(8,128)(2,1)S(1)}, u32[]{:S(2)}, u32[]{:S(2)}) %collective-permute-start.6) | collective-permute-done | bytes 213024 | tf_op jit(solution)/shard_map/ppermute | solution.py:316
  84.5 0.6 line.1.own
  85.1 1.7 %collective-permute-start.9 = (bf16[4,208,512]{2,1,0:T(8,128)(2,1)S(1)}, bf16[4,208,512]{2,1,0:T(8,128)(2,1)S(1)}, u32[]{:S(2)}, u32[]{:S(2)}) collective-permute-start(bf16[4,208,512]{2,1,0:T(8,128)(2,1)S(1)} %line.1.own), channel_id=1, source_target_pairs={{0,32},{32,0},{1,33},{33,1},{2,34},{34,2},{3,35},{35,3},{4,36},{36... | collective-permute-start | bytes 2555912 | tf_op jit(solution)/shard_map/ppermute | solution.py:316
  86.8 2.0 %collective-permute-done.9.got = bf16[4,208,512]{2,1,0:T(8,128)(2,1)S(1)} collective-permute-done((bf16[4,208,512]{2,1,0:T(8,128)(2,1)S(1)}, bf16[4,208,512]{2,1,0:T(8,128)(2,1)S(1)}, u32[]{:S(2)}, u32[]{:S(2)}) %collective-permute-start.9) | collective-permute-done | bytes 852000 | tf_op jit(solution)/shard_map/ppermute | solution.py:316
  88.8 0.6 rows.1.right_in.right0
  89.4 0.0 copy-start
  89.5 2.7 %collective-permute-start.11 = (bf16[1152,512]{1,0:T(8,128)(2,1)S(1)}, bf16[1152,512]{1,0:T(8,128)(2,1)S(1)}, u32[]{:S(2)}, u32[]{:S(2)}) collective-permute-start(bf16[1152,512]{1,0:T(8,128)(2,1)S(1)} %rows.1.right_in.right0), channel_id=1, source_target_pairs={{0,1},{1,0},{2,3},{3,2},{4,5},{5,4},{6,7},{7,6},{8,9},{9,8},{10,11... | collective-permute-start | bytes 3538952 | tf_op jit(solution)/shard_map/ppermute | solution.py:316
  92.2 19.0 %solve.1 = (bf16[384,512]{1,0:T(8,128)(2,1)S(1)}, bf16[512,512]{1,0:T(8,128)(2,1)S(1)}, f32[896,512]{1,0:T(8,128)S(1)}, f32[1,512]{1,0:T(1,128)S(1)}) custom-call(s32[3]{0:T(128)S(1)} %pad_add_fusion.place, bf16[4,208,512]{2,1,0:T(8,128)(2,1)S(1)} %line.1.own, bf16[4,208,512]{2,1,0:T(8,128)(2,1)S(1)} %collective-permute-done.9.got, ...), custom_call_target="tpu_custom_call" | custom-call | tf_op jit(solution)/shard_map/solve/pallas_call | solution.py:26
  111.2 0.6 collective-permute-start.10
  111.8 15.6 %all_to_all.17.sums = f32[32,1,512]{2,1,0:T(1,128)S(1)} all-to-all(f32[32,1,512]{2,1,0:T(1,128)S(1)} %broadcast_in_dim.18), channel_id=1, replica_groups=mesh['y'=4,'c'=2,'x'=2,'z'=8,'r'=2] {'x','z','r'}, dimensions={0} | all-to-all | bytes 131072 | tf_op jit(solution)/shard_map/all_to_all | solution.py:312
  127.4 6.4 %last.1 = (bf16[512,896]{1,0:T(8,128)(2,1)}, f32[512,896]{1,0:T(8,128)}, f32[896,512]{1,0:T(8,128)}, bf16[2,512,896]{2,1,0:T(8,128)(2,1)}) custom-call(s32[3]{0:T(128)S(1)} %pad_add_fusion.place, f32[32,1,512]{2,1,0:T(1,128)S(1)} %all_to_all.17.sums, f32[512,896]{1,0:T(8,128)S(1)} %bitcast.20, bf16[512,896]{1,0:T(8,128)(2,1)S(1)} %bitcast.24, ...), custom_call_target="tpu_custom_call" | custom-call | tf_op jit(solution)/shard_map/last/pallas_call | solution.py:26
  (15 shorter events, 0.1 us)
Async XLA Ops:
  4.6 42.9 %copy-start.3 = (bf16[512,896]{1,0:T(8,128)(2,1)S(1)}, bf16[512,896]{1,0:T(8,128)(2,1)}, u32[]{:S(2)}) copy-start(bf16[512,896]{1,0:T(8,128)(2,1)} %get-tuple-element.31.blend_ref) | copy-start | bytes 2752516
  28.5 23.7 %copy-start.1 = (bf16[1,512,896]{2,1,0:T(8,128)(2,1)S(1)}, bf16[1,512,896]{2,1,0:T(8,128)(2,1)}, u32[]{:S(2)}) copy-start(bf16[1,512,896]{2,1,0:T(8,128)(2,1)} %param.4) | copy-start | bytes 2752516
  49.0 6.3 %collective-permute-start = (bf16[4,208,512]{2,1,0:T(8,128)(2,1)S(1)}, bf16[4,208,512]{2,1,0:T(8,128)(2,1)S(1)}, u32[]{:S(2)}, u32[]{:S(2)}) collective-permute-start(bf16[4,208,512]{2,1,0:T(8,128)(2,1)S(1)} %get-tuple-element.34), channel_id=1, source_target_pairs={{0,32},{32,0},{1,33},{33,1},{2,34},{34,2},{3,35},{35,3},{4,36},{36... | collective-permute-start | bytes 2555912 | tf_op jit(solution)/shard_map/ppermute | solution.py:316
  52.3 32.8 %collective-permute-start.8 = (bf16[384,896]{1,0:T(8,128)(2,1)S(1)}, bf16[384,896]{1,0:T(8,128)(2,1)S(1)}, u32[]{:S(2)}, u32[]{:S(2)}) collective-permute-start(bf16[384,896]{1,0:T(8,128)(2,1)S(1)} %slice_bitcast_fusion), channel_id=1, source_target_pairs={{0,1},{1,0},{2,3},{3,2},{4,5},{5,4},{6,7},{7,6},{8,9},{9,8},{10,11... | collective-permute-start | bytes 2064392 | tf_op jit(solution)/shard_map/ppermute | solution.py:316
  54.8 30.3 %collective-permute-start.7 = (bf16[512,512]{1,0:T(8,128)(2,1)S(1)}, bf16[512,512]{1,0:T(8,128)(2,1)S(1)}, u32[]{:S(2)}, u32[]{:S(2)}) collective-permute-start(bf16[512,512]{1,0:T(8,128)(2,1)S(1)} %bitcast.16), channel_id=1, source_target_pairs={{0,1},{1,0},{2,3},{3,2},{4,5},{5,4},{6,7},{7,6},{8,9},{9,8},{10,11... | collective-permute-start | bytes 1572872 | tf_op jit(solution)/shard_map/ppermute | solution.py:316
  56.1 6.3 %collective-permute-start.1 = (bf16[208,512]{1,0:T(8,128)(2,1)S(1)}, bf16[208,512]{1,0:T(8,128)(2,1)S(1)}, u32[]{:S(2)}, u32[]{:S(2)}) collective-permute-start(bf16[208,512]{1,0:T(8,128)(2,1)S(1)} %get-tuple-element.37), channel_id=1, source_target_pairs={{0,64},{64,0},{128,192},{192,128},{1,65},{65,1},{129,193},{193,129... | collective-permute-start | bytes 638984 | tf_op jit(solution)/shard_map/ppermute | solution.py:316
  57.5 12.0 %collective-permute-start.2 = (bf16[208,512]{1,0:T(8,128)(2,1)S(1)}, bf16[208,512]{1,0:T(8,128)(2,1)S(1)}, u32[]{:S(2)}, u32[]{:S(2)}) collective-permute-start(bf16[208,512]{1,0:T(8,128)(2,1)S(1)} %get-tuple-element.38), channel_id=1, source_target_pairs={{0,128},{64,192},{128,0},{192,64},{1,129},{65,193},{129,1},{193,65... | collective-permute-start | bytes 638984 | tf_op jit(solution)/shard_map/ppermute | solution.py:316
  60.1 11.8 %collective-permute-start.3 = (bf16[208,512]{1,0:T(8,128)(2,1)S(1)}, bf16[208,512]{1,0:T(8,128)(2,1)S(1)}, u32[]{:S(2)}, u32[]{:S(2)}) collective-permute-start(bf16[208,512]{1,0:T(8,128)(2,1)S(1)} %get-tuple-element.39), channel_id=1, source_target_pairs={{0,192},{64,128},{128,64},{192,0},{1,193},{65,129},{129,65},{193,1... | collective-permute-start | bytes 638984 | tf_op jit(solution)/shard_map/ppermute | solution.py:316
  71.9 12.6 %collective-permute-start.6 = (bf16[208,512]{1,0:T(8,128)(2,1)S(1)}, bf16[208,512]{1,0:T(8,128)(2,1)S(1)}, u32[]{:S(2)}, u32[]{:S(2)}) collective-permute-start(bf16[208,512]{1,0:T(8,128)(2,1)S(1)} %sum.1.own), channel_id=1, source_target_pairs={{0,192},{64,128},{128,64},{192,0},{1,193},{65,129},{129,65},{193,1... | collective-permute-start | bytes 638984 | tf_op jit(solution)/shard_map/ppermute | solution.py:316
  72.1 12.4 %collective-permute-start.5 = (bf16[208,512]{1,0:T(8,128)(2,1)S(1)}, bf16[208,512]{1,0:T(8,128)(2,1)S(1)}, u32[]{:S(2)}, u32[]{:S(2)}) collective-permute-start(bf16[208,512]{1,0:T(8,128)(2,1)S(1)} %sum.1.own), channel_id=1, source_target_pairs={{0,128},{64,192},{128,0},{192,64},{1,129},{65,193},{129,1},{193,65... | collective-permute-start | bytes 638984 | tf_op jit(solution)/shard_map/ppermute | solution.py:316
  72.1 12.4 %collective-permute-start.4 = (bf16[208,512]{1,0:T(8,128)(2,1)S(1)}, bf16[208,512]{1,0:T(8,128)(2,1)S(1)}, u32[]{:S(2)}, u32[]{:S(2)}) collective-permute-start(bf16[208,512]{1,0:T(8,128)(2,1)S(1)} %sum.1.own), channel_id=1, source_target_pairs={{0,64},{64,0},{128,192},{192,128},{1,65},{65,1},{129,193},{193,129... | collective-permute-start | bytes 638984 | tf_op jit(solution)/shard_map/ppermute | solution.py:316
  85.1 3.7 %collective-permute-start.9 = (bf16[4,208,512]{2,1,0:T(8,128)(2,1)S(1)}, bf16[4,208,512]{2,1,0:T(8,128)(2,1)S(1)}, u32[]{:S(2)}, u32[]{:S(2)}) collective-permute-start(bf16[4,208,512]{2,1,0:T(8,128)(2,1)S(1)} %line.1.own), channel_id=1, source_target_pairs={{0,32},{32,0},{1,33},{33,1},{2,34},{34,2},{3,35},{35,3},{4,36},{36... | collective-permute-start | bytes 2555912 | tf_op jit(solution)/shard_map/ppermute | solution.py:316
  89.4 38.0 %copy-start = (f32[1,512,896]{2,1,0:T(8,128)S(1)}, f32[1,512,896]{2,1,0:T(8,128)}, u32[]{:S(2)}) copy-start(f32[1,512,896]{2,1,0:T(8,128)} %param.6) | copy-start | bytes 5505028
  89.5 38.0 %copy-start.2 = (bf16[1,512,896]{2,1,0:T(8,128)(2,1)S(1)}, bf16[1,512,896]{2,1,0:T(8,128)(2,1)}, u32[]{:S(2)}) copy-start(bf16[1,512,896]{2,1,0:T(8,128)(2,1)} %param.5) | copy-start | bytes 2752516
  89.5 37.9 %collective-permute-start.11 = (bf16[1152,512]{1,0:T(8,128)(2,1)S(1)}, bf16[1152,512]{1,0:T(8,128)(2,1)S(1)}, u32[]{:S(2)}, u32[]{:S(2)}) collective-permute-start(bf16[1152,512]{1,0:T(8,128)(2,1)S(1)} %rows.1.right_in.right0), channel_id=1, source_target_pairs={{0,1},{1,0},{2,3},{3,2},{4,5},{5,4},{6,7},{7,6},{8,9},{9,8},{10,11... | collective-permute-start | bytes 3538952 | tf_op jit(solution)/shard_map/ppermute | solution.py:316
  111.2 16.2 %collective-permute-start.10 = (bf16[384,512]{1,0:T(8,128)(2,1)S(1)}, bf16[384,512]{1,0:T(8,128)(2,1)S(1)}, u32[]{:S(2)}, u32[]{:S(2)}) collective-permute-start(bf16[384,512]{1,0:T(8,128)(2,1)S(1)} %get-tuple-element.45.w0), channel_id=1, source_target_pairs={{0,1},{1,0},{2,3},{3,2},{4,5},{5,4},{6,7},{7,6},{8,9},{9,8},{10,11... | collective-permute-start | bytes 1179656 | tf_op jit(solution)/shard_map/ppermute | solution.py:316

commit v8 on v7

--- a/solution.py
+++ b/solution.py
@@ -222,17 +222,18 @@
     packed(out, g, r)
 
 
-def line_kernel(place, own, one, two, three, out):
+def line_kernel(place, own, one, two, three, weight, out, half):
+    late, wide = weight.shape[0] - EARLY, weight.shape[1] - N
     for k, got in enumerate((own, one, two, three)):
-        out[place[0] ^ k] = got[...]
-
-
-def rows_kernel(place, own, got, weight, right):
-    late = weight.shape[0] - EARLY
-    wide = weight.shape[1] - N
-    right[8 * RR : 8 * RR + late, :] = weight[EARLY:, :N]
-    right[8 * RR + late :, :wide] = weight[EARLY:, N:]
-    right[8 * RR + late :, wide:] = jnp.zeros((late, N - wide), B)
+        y = place[0] ^ k
+        out[y] = got[...]
+        half[pl.ds(pl.multiple_of(y * RR, 16), RR), :] = got[:RR, :]
+    half[4 * RR : 4 * RR + late, :] = weight[EARLY:, :N]
+    half[4 * RR + late :, :wide] = weight[EARLY:, N:]
+    half[4 * RR + late :, wide:] = jnp.zeros((late, N - wide), B)
+
+
+def rows_kernel(place, own, got, right):
     for y in range(4):
         for c, part in ((place[1], own), (1 - place[1], got)):
             right[pl.ds(pl.multiple_of((2 * y + c) * RR, 16), RR), :] = part[y, :RR, :]
@@ -256,15 +257,14 @@
     w16[256:, :256] = wh[:128, :256]
     w16[256:, 256:] = wh[128:256, :256]
     ortho[...] = (dot(left[...], wh, NT) + dot(left[...], wl, NT)).astype(B)
-    raw = right_in[: 8 * RR, :]
-    r = dot(raw, wh, NT) + dot(raw, wl, NT)
+    r = dot(right_in[...], wh, NT) + dot(right_in[...], wl, NT)
     right[...] = r
     squares[...] = jnp.sum(r * r, axis=0, keepdims=True)
 
 
 def last_kernel(
-    place, sums, momentum, gradient, ortho, right, left0, w0, right0, weight0, left1, w1, right1, weight1,
-    out_weight, out_moment, out_basis, out_rollout, weight, moment, basis, w, sems,
+    place, sums, momentum, gradient, ortho, right, left0, w0, raw0, weight0, left1, w1, half1, half2, weight1,
+    out_weight, out_moment, out_basis, out_rollout, weight, moment, basis, w, raw1, sems,
 ):
     scales = []
     for side in range(2):
@@ -281,21 +281,24 @@
     moment[...] = blend - 0.05 * dot(ortho[...], right[...].astype(B), NT)
     copies.append(pltpu.make_async_copy(moment, out_moment, sems.at[1]))
     copies[-1].start()
-    for half, refs in enumerate(((left0, w0, right0, weight0), (left1, w1, right1, weight1))):
+    for y in range(4):
+        for c, part in ((place[1], half1), (1 - place[1], half2)):
+            raw1[pl.ds(pl.multiple_of((2 * y + c) * RR, 16), RR), :] = part[y * RR : (y + 1) * RR, :]
+    for half, refs in enumerate(((left0, w0, raw0, weight0), (left1, w1, raw1, weight1))):
         left, packed_w, raw, old = refs
         w[256:, :] = packed_w[:256, :]
         w[:128, :256] = packed_w[256:, :256]
         w[128:256, :256] = packed_w[256:, 256:]
         w[:256, 256:] = jnp.zeros((256, 256), B)
         o = (dot(left[...], w[...], NT) * scale[half]).astype(B)
-        r = dot(raw[: 8 * RR, :], w[...], NT).astype(B)
+        r = dot(raw[...], w[...], NT).astype(B)
         update = 0.3 * dot(o, r, NT)
         if half == 0:
             weight[half] = (old[...].astype(F) - update).astype(B)
         else:
             late, wide = update.shape[0] - EARLY, update.shape[1] - N
             weight[half, :EARLY] = (old[...].astype(F) - update[:EARLY]).astype(B)
-            low, high = raw[8 * RR : 8 * RR + late, :], raw[8 * RR + late :, :wide]
+            low, high = half1[4 * RR : 4 * RR + late, :], half1[4 * RR + late :, :wide]
             weight[half, EARLY:, :N] = (low.astype(F) - update[EARLY:, :N]).astype(B)
             weight[half, EARLY:, N:] = (high.astype(F) - update[EARLY:, N:]).astype(B)
         side = place[2] if half == 0 else 1 - place[2]
@@ -344,14 +347,14 @@
     )(place, keep_g, keep_r, got)
     arrived = [swap(x, "y", k + 1) for k, x in enumerate(outs)]
     (piece,) = call(sum_kernel, [((RR + GR, N), B)], name="sum")(own_g, own_r, *arrived)
-    (line,) = call(line_kernel, [((4, RR + GR, N), B)], smem=1, name="line")(
-        place, piece, *[swap(piece, "y", k) for k in (1, 2, 3)]
+    late = 2 * (weights.shape[1] - EARLY)
+    line, half = call(line_kernel, [((4, RR + GR, N), B), ((4 * RR + late, N), B)], smem=1, name="line")(
+        place, piece, *[swap(piece, "y", k) for k in (1, 2, 3)], weights[0]
     )
-    line, left_o, weight_o = lax.optimization_barrier((line, left_o, weight_o))
+    line, half, left_o, weight_o = lax.optimization_barrier((line, half, left_o, weight_o))
     other_core = swap(line, "c")
-    late = 2 * (weights.shape[1] - EARLY)
-    (raw,) = call(rows_kernel, [((8 * RR + late, N), B)], smem=1, name="rows")(place, line, other_core, weights[0])
-    raw_o = swap(raw, "r")
+    half_o = swap(half, "r")
+    (raw,) = call(rows_kernel, [((8 * RR, N), B)], smem=1, name="rows")(place, line, other_core)
 
     w16, ortho, right, squares = call(
         solve_kernel,
@@ -360,18 +363,23 @@
         smem=1,
         name="solve",
     )(place, line, other_core, left, raw)
+    w16, half_o = lax.optimization_barrier((w16, half_o))
     w16_o = swap(w16, "r")
+    half_oc = swap(half_o, "c")
     sums = exchange(jnp.broadcast_to(squares[None], (32, 1, N)), ("x", "z", "r"))
     wide, tall = momentum.shape, right.shape
     weight_new, moment_new, basis_new, rollout = call(
         last_kernel,
         [(wide, B), (wide, F), (tall, F), ((2, *wide), B)],
-        [pltpu.VMEM((2, *wide), B), pltpu.VMEM(wide, F), pltpu.VMEM(tall, F), pltpu.VMEM((N, N), B), pltpu.SemaphoreType.DMA((5,))],
+        [pltpu.VMEM((2, *wide), B), pltpu.VMEM(wide, F), pltpu.VMEM(tall, F), pltpu.VMEM((N, N), B)]
+        + [pltpu.VMEM((8 * RR, N), B), pltpu.SemaphoreType.DMA((5,))],
         smem=1,
         name="last",
         mib=24,
         out_spec=pl.BlockSpec(memory_space=pl.ANY),
-    )(place, sums, momentum, gradient, ortho, right, left, w16, raw, weights[0], left_o, w16_o, raw_o, weight_o)
+    )(
+        place, sums, momentum, gradient, ortho, right, left, w16, raw, weights[0], left_o, w16_o, half_o, half_oc, weight_o
+    )
     return weight_new[None], moment_new[None], basis_new[None], rollout
 
 

time: 134 us -> 133 us (level)
  waiting for transfers between devices: 23 us -> 21 us
  starting transfers between devices: 18.6 us -> 20.1 us
    ppermute x12 -> x13, waiting for transfers between devices: 23 us -> 21 us  [swap(): lax.ppermute(x, axis, [(i, i ^ bit) for i in range(lax.axis_size(axis))])]
    ppermute x12 -> x13, starting transfers between devices: 18.6 us -> 20.1 us  [swap(): lax.ppermute(x, axis, [(i, i ^ bit) for i in range(lax.axis_size(axis))])]
  transfers between devices with their start and end apart: 12 -> 13, of which waited for: 5 -> 4; matrix products, arithmetic and copies ran while one was open for 0% -> 0% of each run, Pallas kernels for 15% -> 16%
where the time goes in v8:
time: 133 us; the launch traced here: 132 us
  blocking collectives  57 us (43%)
  Pallas kernels  33 us (25%)
  waiting for transfers between devices  21 us (16%)
  starting transfers between devices  20.1 us (15%)
    all_to_all x3, blocking collectives, exchange(): return lax.all_to_all(x, axis, 0, 0, tiled=True)  57 us
    pallas_call x8, Pallas kernels, run(): pl.pallas_call(kernel, out_shape=[jax.ShapeDtypeStruct(s, d) for s, d in...  29.1 us
    ppermute x13, waiting for transfers between devices, swap(): lax.ppermute(x, axis, [(i, i ^ bit) for i in range(lax.axis_size(axis))])  21 us
    ppermute x13, starting transfers between devices, swap(): lax.ppermute(x, axis, [(i, i ^ bit) for i in range(lax.axis_size(axis))])  20.1 us
    pallas_call x1, Pallas kernels, front(): pl.pallas_call(front_kernel, out_shape=[jax.ShapeDtypeStruct((rows, N), B...  3.87 us
  transfers between devices with their start and end apart: 13, of which 4 were waited for; matrix products, arithmetic and copies ran while one was open for 0% of the time, Pallas kernels for 16%

profile of v8, /device:TPU:1, one launch (start us, length us, event | category | flops | bytes accessed | tf_op | source)
XLA Modules:
  0.0 132.3 jit_solution(3368954474976270034)
XLA Ops:
  0.6 0.1 pad_add_fusion.place
  0.7 3.9 %front.1 = (bf16[512,512]{1,0:T(8,128)(2,1)}, bf16[512,896]{1,0:T(8,128)(2,1)}) custom-call(f32[512,896]{1,0:T(8,128)} %bitcast.19, bf16[512,896]{1,0:T(8,128)(2,1)} %bitcast.23, f32[896,512]{1,0:T(8,128)} %bitcast.26), custom_call_target="tpu_custom_call" | custom-call | tf_op jit(solution)/shard_map/front/pallas_call | solution.py:151
  4.6 0.0 copy-start.3
  4.6 23.9 %all_to_all.15.pieces = bf16[16,32,512]{2,1,0:T(8,128)(2,1)S(1)} all-to-all(bf16[16,32,512]{2,1,0:T(8,128)(2,1)} %bitcast.27), channel_id=1, replica_groups=mesh['y'=4,'c'=2,'x'=2,'z'=8,'r'=2] {'x','z'}, dimensions={0} | all-to-all | bytes 1048576 | tf_op jit(solution)/shard_map/all_to_all | solution.py:315
  28.5 0.1 spread.1
  28.6 18.8 %all_to_all.16 = bf16[16,32,512]{2,1,0:T(8,128)(2,1)S(1)} all-to-all(bf16[16,32,512]{2,1,0:T(8,128)(2,1)S(1)} %spread.1), channel_id=1, replica_groups=mesh['y'=4,'c'=2,'x'=2,'z'=8,'r'=2] {'x','z'}, dimensions={0} | all-to-all | bytes 1048576 | tf_op jit(solution)/shard_map/all_to_all | solution.py:315
  47.5 1.6 %pieces.1 = (f32[4,96,256]{2,1,0:T(8,128)S(1)}, f32[4,112,512]{2,1,0:T(8,128)S(1)}, bf16[4,208,512]{2,1,0:T(8,128)(2,1)S(1)}) custom-call(s32[3]{0:T(128)S(1)} %pad_add_fusion.place, bf16[512,512]{1,0:T(8,128)(2,1)S(1)} %bitcast.15, bf16[512,896]{1,0:T(8,128)(2,1)S(1)} %copy-done.3), custom_call_target="tpu_custom_call" | custom-call | tf_op jit(solution)/shard_map/pieces/pallas_call | solution.py:26
  49.0 3.2 %collective-permute-start = (bf16[4,208,512]{2,1,0:T(8,128)(2,1)S(1)}, bf16[4,208,512]{2,1,0:T(8,128)(2,1)S(1)}, u32[]{:S(2)}, u32[]{:S(2)}) collective-permute-start(bf16[4,208,512]{2,1,0:T(8,128)(2,1)S(1)} %get-tuple-element.39), channel_id=1, source_target_pairs={{0,32},{32,0},{1,33},{33,1},{2,34},{34,2},{3,35},{35,3},{4,36},{36... | collective-permute-start | bytes 2555912 | tf_op jit(solution)/shard_map/ppermute | solution.py:319
  52.2 0.1 slice_bitcast_fusion
  52.3 2.5 %collective-permute-start.8 = (bf16[384,896]{1,0:T(8,128)(2,1)S(1)}, bf16[384,896]{1,0:T(8,128)(2,1)S(1)}, u32[]{:S(2)}, u32[]{:S(2)}) collective-permute-start(bf16[384,896]{1,0:T(8,128)(2,1)S(1)} %slice_bitcast_fusion), channel_id=1, source_target_pairs={{0,1},{1,0},{2,3},{3,2},{4,5},{5,4},{6,7},{7,6},{8,9},{9,8},{10,11... | collective-permute-start | bytes 2064392 | tf_op jit(solution)/shard_map/ppermute | solution.py:319
  54.8 0.5 collective-permute-start.7
  55.4 0.7 join.1
  56.1 1.4 %collective-permute-start.1 = (bf16[208,512]{1,0:T(8,128)(2,1)S(1)}, bf16[208,512]{1,0:T(8,128)(2,1)S(1)}, u32[]{:S(2)}, u32[]{:S(2)}) collective-permute-start(bf16[208,512]{1,0:T(8,128)(2,1)S(1)} %get-tuple-element.42), channel_id=1, source_target_pairs={{0,64},{64,0},{128,192},{192,128},{1,65},{65,1},{129,193},{193,129... | collective-permute-start | bytes 638984 | tf_op jit(solution)/shard_map/ppermute | solution.py:319
  57.5 2.6 %collective-permute-start.2 = (bf16[208,512]{1,0:T(8,128)(2,1)S(1)}, bf16[208,512]{1,0:T(8,128)(2,1)S(1)}, u32[]{:S(2)}, u32[]{:S(2)}) collective-permute-start(bf16[208,512]{1,0:T(8,128)(2,1)S(1)} %get-tuple-element.43), channel_id=1, source_target_pairs={{0,128},{64,192},{128,0},{192,64},{1,129},{65,193},{129,1},{193,65... | collective-permute-start | bytes 638984 | tf_op jit(solution)/shard_map/ppermute | solution.py:319
  60.1 2.3 %collective-permute-done.1.one = bf16[208,512]{1,0:T(8,128)(2,1)S(1)} collective-permute-done((bf16[208,512]{1,0:T(8,128)(2,1)S(1)}, bf16[208,512]{1,0:T(8,128)(2,1)S(1)}, u32[]{:S(2)}, u32[]{:S(2)}) %collective-permute-start.1) | collective-permute-done | bytes 213024 | tf_op jit(solution)/shard_map/ppermute | solution.py:319
  62.4 7.0 %collective-permute-done.2.two = bf16[208,512]{1,0:T(8,128)(2,1)S(1)} collective-permute-done((bf16[208,512]{1,0:T(8,128)(2,1)S(1)}, bf16[208,512]{1,0:T(8,128)(2,1)S(1)}, u32[]{:S(2)}, u32[]{:S(2)}) %collective-permute-start.2) | collective-permute-done | bytes 213024 | tf_op jit(solution)/shard_map/ppermute | solution.py:319
  69.4 2.4 %collective-permute-done.3.three = bf16[208,512]{1,0:T(8,128)(2,1)S(1)} collective-permute-done((bf16[208,512]{1,0:T(8,128)(2,1)S(1)}, bf16[208,512]{1,0:T(8,128)(2,1)S(1)}, u32[]{:S(2)}, u32[]{:S(2)}) %collective-permute-start.3) | collective-permute-done | bytes 213024 | tf_op jit(solution)/shard_map/ppermute | solution.py:319
  71.8 0.1 sum.1.own
  71.9 0.1 collective-permute-start.6
  72.1 0.1 collective-permute-start.5
  72.1 3.1 %collective-permute-start.4 = (bf16[208,512]{1,0:T(8,128)(2,1)S(1)}, bf16[208,512]{1,0:T(8,128)(2,1)S(1)}, u32[]{:S(2)}, u32[]{:S(2)}) collective-permute-start(bf16[208,512]{1,0:T(8,128)(2,1)S(1)} %sum.1.own), channel_id=1, source_target_pairs={{0,64},{64,0},{128,192},{192,128},{1,65},{65,1},{129,193},{193,129... | collective-permute-start | bytes 638984 | tf_op jit(solution)/shard_map/ppermute | solution.py:319
  75.3 9.2 %collective-permute-done.6.three = bf16[208,512]{1,0:T(8,128)(2,1)S(1)} collective-permute-done((bf16[208,512]{1,0:T(8,128)(2,1)S(1)}, bf16[208,512]{1,0:T(8,128)(2,1)S(1)}, u32[]{:S(2)}, u32[]{:S(2)}) %collective-permute-start.6) | collective-permute-done | bytes 213024 | tf_op jit(solution)/shard_map/ppermute | solution.py:319
  84.5 0.7 line.1
  85.2 1.7 %collective-permute-start.9 = (bf16[4,208,512]{2,1,0:T(8,128)(2,1)S(1)}, bf16[4,208,512]{2,1,0:T(8,128)(2,1)S(1)}, u32[]{:S(2)}, u32[]{:S(2)}) collective-permute-start(bf16[4,208,512]{2,1,0:T(8,128)(2,1)S(1)} %get-tuple-element.48.own), channel_id=1, source_target_pairs={{0,32},{32,0},{1,33},{33,1},{2,34},{34,2},{3,35},{35,3},{4,36},{36... | collective-permute-start | bytes 2555912 | tf_op jit(solution)/shard_map/ppermute | solution.py:319
  86.9 2.5 %collective-permute-start.10 = (bf16[704,512]{1,0:T(8,128)(2,1)S(1)}, bf16[704,512]{1,0:T(8,128)(2,1)S(1)}, u32[]{:S(2)}, u32[]{:S(2)}) collective-permute-start(bf16[704,512]{1,0:T(8,128)(2,1)S(1)} %get-tuple-element.53), channel_id=1, source_target_pairs={{0,1},{1,0},{2,3},{3,2},{4,5},{5,4},{6,7},{7,6},{8,9},{9,8},{10,11... | collective-permute-start | bytes 2162696 | tf_op jit(solution)/shard_map/ppermute | solution.py:319
  89.3 0.6 rows.1.right_in.raw0
  89.9 0.0 copy-start.2
  89.9 19.0 %solve.1 = (bf16[384,512]{1,0:T(8,128)(2,1)S(1)}, bf16[512,512]{1,0:T(8,128)(2,1)S(1)}, f32[896,512]{1,0:T(8,128)S(1)}, f32[1,512]{1,0:T(1,128)S(1)}) custom-call(s32[3]{0:T(128)S(1)} %pad_add_fusion.place, bf16[4,208,512]{2,1,0:T(8,128)(2,1)S(1)} %get-tuple-element.48.own, bf16[4,208,512]{2,1,0:T(8,128)(2,1)S(1)} %collective-permute-done.9.got, ...), custom_call_target="tpu_custom_call" | custom-call | tf_op jit(solution)/shard_map/solve/pallas_call | solution.py:26
  109.0 0.6 collective-permute-start.12
  109.6 1.8 %collective-permute-start.11 = (bf16[384,512]{1,0:T(8,128)(2,1)S(1)}, bf16[384,512]{1,0:T(8,128)(2,1)S(1)}, u32[]{:S(2)}, u32[]{:S(2)}) collective-permute-start(bf16[384,512]{1,0:T(8,128)(2,1)S(1)} %get-tuple-element.54.w0), channel_id=1, source_target_pairs={{0,1},{1,0},{2,3},{3,2},{4,5},{5,4},{6,7},{7,6},{8,9},{9,8},{10,11... | collective-permute-start | bytes 1179656 | tf_op jit(solution)/shard_map/ppermute | solution.py:319
  111.5 14.2 %all_to_all.17.sums = f32[32,1,512]{2,1,0:T(1,128)S(1)} all-to-all(f32[32,1,512]{2,1,0:T(1,128)S(1)} %broadcast_in_dim.18), channel_id=1, replica_groups=mesh['y'=4,'c'=2,'x'=2,'z'=8,'r'=2] {'x','z','r'}, dimensions={0} | all-to-all | bytes 131072 | tf_op jit(solution)/shard_map/all_to_all | solution.py:315
  125.7 6.4 %last.1 = (bf16[512,896]{1,0:T(8,128)(2,1)}, f32[512,896]{1,0:T(8,128)}, f32[896,512]{1,0:T(8,128)}, bf16[2,512,896]{2,1,0:T(8,128)(2,1)}) custom-call(s32[3]{0:T(128)S(1)} %pad_add_fusion.place, f32[32,1,512]{2,1,0:T(1,128)S(1)} %all_to_all.17.sums, f32[512,896]{1,0:T(8,128)S(1)} %bitcast.20, bf16[512,896]{1,0:T(8,128)(2,1)S(1)} %bitcast.24, ...), custom_call_target="tpu_custom_call" | custom-call | tf_op jit(solution)/shard_map/last/pallas_call | solution.py:26
  (17 shorter events, 0.1 us)
Async XLA Ops:
  4.6 42.9 %copy-start.3 = (bf16[512,896]{1,0:T(8,128)(2,1)S(1)}, bf16[512,896]{1,0:T(8,128)(2,1)}, u32[]{:S(2)}) copy-start(bf16[512,896]{1,0:T(8,128)(2,1)} %get-tuple-element.36.blend_ref) | copy-start | bytes 2752516
  28.5 23.7 %copy-start.1 = (bf16[1,512,896]{2,1,0:T(8,128)(2,1)S(1)}, bf16[1,512,896]{2,1,0:T(8,128)(2,1)}, u32[]{:S(2)}) copy-start(bf16[1,512,896]{2,1,0:T(8,128)(2,1)} %param.4) | copy-start | bytes 2752516
  49.0 6.3 %collective-permute-start = (bf16[4,208,512]{2,1,0:T(8,128)(2,1)S(1)}, bf16[4,208,512]{2,1,0:T(8,128)(2,1)S(1)}, u32[]{:S(2)}, u32[]{:S(2)}) collective-permute-start(bf16[4,208,512]{2,1,0:T(8,128)(2,1)S(1)} %get-tuple-element.39), channel_id=1, source_target_pairs={{0,32},{32,0},{1,33},{33,1},{2,34},{34,2},{3,35},{35,3},{4,36},{36... | collective-permute-start | bytes 2555912 | tf_op jit(solution)/shard_map/ppermute | solution.py:319
  52.3 32.9 %collective-permute-start.8 = (bf16[384,896]{1,0:T(8,128)(2,1)S(1)}, bf16[384,896]{1,0:T(8,128)(2,1)S(1)}, u32[]{:S(2)}, u32[]{:S(2)}) collective-permute-start(bf16[384,896]{1,0:T(8,128)(2,1)S(1)} %slice_bitcast_fusion), channel_id=1, source_target_pairs={{0,1},{1,0},{2,3},{3,2},{4,5},{5,4},{6,7},{7,6},{8,9},{9,8},{10,11... | collective-permute-start | bytes 2064392 | tf_op jit(solution)/shard_map/ppermute | solution.py:319
  54.8 30.3 %collective-permute-start.7 = (bf16[512,512]{1,0:T(8,128)(2,1)S(1)}, bf16[512,512]{1,0:T(8,128)(2,1)S(1)}, u32[]{:S(2)}, u32[]{:S(2)}) collective-permute-start(bf16[512,512]{1,0:T(8,128)(2,1)S(1)} %bitcast.16), channel_id=1, source_target_pairs={{0,1},{1,0},{2,3},{3,2},{4,5},{5,4},{6,7},{7,6},{8,9},{9,8},{10,11... | collective-permute-start | bytes 1572872 | tf_op jit(solution)/shard_map/ppermute | solution.py:319
  56.1 6.3 %collective-permute-start.1 = (bf16[208,512]{1,0:T(8,128)(2,1)S(1)}, bf16[208,512]{1,0:T(8,128)(2,1)S(1)}, u32[]{:S(2)}, u32[]{:S(2)}) collective-permute-start(bf16[208,512]{1,0:T(8,128)(2,1)S(1)} %get-tuple-element.42), channel_id=1, source_target_pairs={{0,64},{64,0},{128,192},{192,128},{1,65},{65,1},{129,193},{193,129... | collective-permute-start | bytes 638984 | tf_op jit(solution)/shard_map/ppermute | solution.py:319
  57.5 12.0 %collective-permute-start.2 = (bf16[208,512]{1,0:T(8,128)(2,1)S(1)}, bf16[208,512]{1,0:T(8,128)(2,1)S(1)}, u32[]{:S(2)}, u32[]{:S(2)}) collective-permute-start(bf16[208,512]{1,0:T(8,128)(2,1)S(1)} %get-tuple-element.43), channel_id=1, source_target_pairs={{0,128},{64,192},{128,0},{192,64},{1,129},{65,193},{129,1},{193,65... | collective-permute-start | bytes 638984 | tf_op jit(solution)/shard_map/ppermute | solution.py:319
  60.1 11.8 %collective-permute-start.3 = (bf16[208,512]{1,0:T(8,128)(2,1)S(1)}, bf16[208,512]{1,0:T(8,128)(2,1)S(1)}, u32[]{:S(2)}, u32[]{:S(2)}) collective-permute-start(bf16[208,512]{1,0:T(8,128)(2,1)S(1)} %get-tuple-element.44), channel_id=1, source_target_pairs={{0,192},{64,128},{128,64},{192,0},{1,193},{65,129},{129,65},{193,1... | collective-permute-start | bytes 638984 | tf_op jit(solution)/shard_map/ppermute | solution.py:319
  71.9 12.6 %collective-permute-start.6 = (bf16[208,512]{1,0:T(8,128)(2,1)S(1)}, bf16[208,512]{1,0:T(8,128)(2,1)S(1)}, u32[]{:S(2)}, u32[]{:S(2)}) collective-permute-start(bf16[208,512]{1,0:T(8,128)(2,1)S(1)} %sum.1.own), channel_id=1, source_target_pairs={{0,192},{64,128},{128,64},{192,0},{1,193},{65,129},{129,65},{193,1... | collective-permute-start | bytes 638984 | tf_op jit(solution)/shard_map/ppermute | solution.py:319
  72.1 12.4 %collective-permute-start.5 = (bf16[208,512]{1,0:T(8,128)(2,1)S(1)}, bf16[208,512]{1,0:T(8,128)(2,1)S(1)}, u32[]{:S(2)}, u32[]{:S(2)}) collective-permute-start(bf16[208,512]{1,0:T(8,128)(2,1)S(1)} %sum.1.own), channel_id=1, source_target_pairs={{0,128},{64,192},{128,0},{192,64},{1,129},{65,193},{129,1},{193,65... | collective-permute-start | bytes 638984 | tf_op jit(solution)/shard_map/ppermute | solution.py:319
  72.1 12.4 %collective-permute-start.4 = (bf16[208,512]{1,0:T(8,128)(2,1)S(1)}, bf16[208,512]{1,0:T(8,128)(2,1)S(1)}, u32[]{:S(2)}, u32[]{:S(2)}) collective-permute-start(bf16[208,512]{1,0:T(8,128)(2,1)S(1)} %sum.1.own), channel_id=1, source_target_pairs={{0,64},{64,0},{128,192},{192,128},{1,65},{65,1},{129,193},{193,129... | collective-permute-start | bytes 638984 | tf_op jit(solution)/shard_map/ppermute | solution.py:319
  85.2 4.1 %collective-permute-start.9 = (bf16[4,208,512]{2,1,0:T(8,128)(2,1)S(1)}, bf16[4,208,512]{2,1,0:T(8,128)(2,1)S(1)}, u32[]{:S(2)}, u32[]{:S(2)}) collective-permute-start(bf16[4,208,512]{2,1,0:T(8,128)(2,1)S(1)} %get-tuple-element.48.own), channel_id=1, source_target_pairs={{0,32},{32,0},{1,33},{33,1},{2,34},{34,2},{3,35},{35,3},{4,36},{36... | collective-permute-start | bytes 2555912 | tf_op jit(solution)/shard_map/ppermute | solution.py:319
  86.9 22.1 %collective-permute-start.10 = (bf16[704,512]{1,0:T(8,128)(2,1)S(1)}, bf16[704,512]{1,0:T(8,128)(2,1)S(1)}, u32[]{:S(2)}, u32[]{:S(2)}) collective-permute-start(bf16[704,512]{1,0:T(8,128)(2,1)S(1)} %get-tuple-element.53), channel_id=1, source_target_pairs={{0,1},{1,0},{2,3},{3,2},{4,5},{5,4},{6,7},{7,6},{8,9},{9,8},{10,11... | collective-permute-start | bytes 2162696 | tf_op jit(solution)/shard_map/ppermute | solution.py:319
  89.9 35.8 %copy-start = (f32[1,512,896]{2,1,0:T(8,128)S(1)}, f32[1,512,896]{2,1,0:T(8,128)}, u32[]{:S(2)}) copy-start(f32[1,512,896]{2,1,0:T(8,128)} %param.6) | copy-start | bytes 5505028
  89.9 35.8 %copy-start.2 = (bf16[1,512,896]{2,1,0:T(8,128)(2,1)S(1)}, bf16[1,512,896]{2,1,0:T(8,128)(2,1)}, u32[]{:S(2)}) copy-start(bf16[1,512,896]{2,1,0:T(8,128)(2,1)} %param.5) | copy-start | bytes 2752516
  109.0 16.7 %collective-permute-start.12 = (bf16[704,512]{1,0:T(8,128)(2,1)S(1)}, bf16[704,512]{1,0:T(8,128)(2,1)S(1)}, u32[]{:S(2)}, u32[]{:S(2)}) collective-permute-start(bf16[704,512]{1,0:T(8,128)(2,1)S(1)} %collective-permute-done.10.half1), channel_id=1, source_target_pairs={{0,32},{32,0},{1,33},{33,1},{2,34},{34,2},{3,35},{35,3},{4,36},{36... | collective-permute-start | bytes 2162696 | tf_op jit(solution)/shard_map/ppermute | solution.py:319
  109.6 16.1 %collective-permute-start.11 = (bf16[384,512]{1,0:T(8,128)(2,1)S(1)}, bf16[384,512]{1,0:T(8,128)(2,1)S(1)}, u32[]{:S(2)}, u32[]{:S(2)}) collective-permute-start(bf16[384,512]{1,0:T(8,128)(2,1)S(1)} %get-tuple-element.54.w0), channel_id=1, source_target_pairs={{0,1},{1,0},{2,3},{3,2},{4,5},{5,4},{6,7},{7,6},{8,9},{9,8},{10,11... | collective-permute-start | bytes 1179656 | tf_op jit(solution)/shard_map/ppermute | solution.py:319

commit v9 on v8

--- a/solution.py
+++ b/solution.py
@@ -14,7 +14,7 @@
 N = 512
 NB = 128
 GRP = 8
-GR = 96
+GR = 80
 RR = 112
 EARLY = 384
 VMEM = pl.BlockSpec(memory_space=pltpu.VMEM)
@@ -179,8 +179,11 @@
         c = place[1] if mine else 1 - place[1]
         wide = left_ref[:, pl.ds(pl.multiple_of(c * 256, 256), 256)]
         narrow = left_ref[:, pl.ds(pl.multiple_of(c * 128, 128), 128)]
-        part[:256, :] = dot(wide, wide, TN)
-        part[256:, :] = dot(narrow, left_ref[:, 256:], TN)
+        part[:128, :] = dot(wide[:, :128], wide, TN)
+        corner = dot(wide[:, 128:], wide[:, 128:], TN)
+        part[128:192, :128] = corner[:64, :]
+        part[128:192, 128:] = corner[64:, :]
+        part[192:, :] = dot(narrow, left_ref[:, 256:], TN)
         for y in range(4):
             g = part[y * GR : (y + 1) * GR, :]
             r = right_scr[pl.ds(pl.multiple_of((2 * y + c) * RR, 16), RR), :]
@@ -240,17 +243,18 @@
 
 
 def solve_kernel(place, own, got, left, right_in, w16, ortho, right, squares, a, w):
-    for y in range(4):
-        first = y * GR
-        square = max(0, min(GR, 256 - first))
-        for c, part in ((place[1], own), (1 - place[1], got)):
-            g = gram_of(part.at[y])
-            if square:
-                rows = pl.ds(pl.multiple_of(c * 256 + first, 32), square)
-                a[rows, pl.ds(pl.multiple_of(c * 256, 256), 256)] = g[:square, :]
-            if square < GR:
-                rows = pl.ds(pl.multiple_of(c * 128 + first + square - 256, 32), GR - square)
-                a[rows, 256:] = g[square:, :]
+    for c, part in ((place[1], own), (1 - place[1], got)):
+        at = lambda first, count: pl.ds(pl.multiple_of(first, 16), count)
+        square = pl.ds(pl.multiple_of(c * 256, 256), 256)
+        corner = pl.ds(pl.multiple_of(c * 256 + 128, 128), 128)
+        g = [gram_of(part.at[y]) for y in range(4)]
+        a[at(c * 256, 80), square] = g[0]
+        a[at(c * 256 + 80, 48), square] = g[1][:48, :]
+        for first, rows in ((128, g[1][48:, :]), (160, g[2][:32, :])):
+            a[at(c * 256 + first, 32), corner] = rows[:, :128]
+            a[at(c * 256 + first + 64, 32), corner] = rows[:, 128:]
+        a[at(c * 128, 48), 256:] = g[2][32:, :]
+        a[at(c * 128 + 48, 80), 256:] = g[3]
     inverse_factor(a, w)
     wh, wl = halves(w[...])
     w16[:256, :] = wh[256:, :]
@@ -331,7 +335,7 @@
     keep_g, keep_r, send = call(
         pieces_kernel,
         [((4, GR, 256), F), ((4, RR, N), F), ((4, RR + GR, N), B)],
-        [pltpu.VMEM((8 * RR, N), F), pltpu.VMEM((384, 256), F)],
+        [pltpu.VMEM((8 * RR, N), F), pltpu.VMEM((4 * GR, 256), F)],
         smem=1,
         name="pieces",
     )(place, left, blend16)

time: 133 us -> 131 us (0.985)
  no operation moved by 1% of the time
where the time goes in v9:
time: 131 us
  blocking collectives  57.1 us (44%)
  Pallas kernels  32.9 us (25%)
  starting transfers between devices  20.1 us (15%)
  waiting for transfers between devices  19.8 us (15%)
    all_to_all x3, blocking collectives, exchange(): return lax.all_to_all(x, axis, 0, 0, tiled=True)  57.1 us
    pallas_call x8, Pallas kernels, run(): pl.pallas_call(kernel, out_shape=[jax.ShapeDtypeStruct(s, d) for s, d in...  29 us
    ppermute x13, starting transfers between devices, swap(): lax.ppermute(x, axis, [(i, i ^ bit) for i in range(lax.axis_size(axis))])  20.1 us
    ppermute x13, waiting for transfers between devices, swap(): lax.ppermute(x, axis, [(i, i ^ bit) for i in range(lax.axis_size(axis))])  19.8 us
    pallas_call x1, Pallas kernels, front(): pl.pallas_call(front_kernel, out_shape=[jax.ShapeDtypeStruct((rows, N), B...  3.87 us
  transfers between devices with their start and end apart: 13, of which 4 were waited for; matrix products, arithmetic and copies ran while one was open for 0% of the time, Pallas kernels for 16%

profile of v9, /device:TPU:1, one launch (start us, length us, event | category | flops | bytes accessed | tf_op | source)
XLA Modules:
  0.0 131.0 jit_solution(4766154032294992257)
XLA Ops:
  0.6 0.1 pad_add_fusion.place
  0.7 3.9 %front.1 = (bf16[512,512]{1,0:T(8,128)(2,1)}, bf16[512,896]{1,0:T(8,128)(2,1)}) custom-call(f32[512,896]{1,0:T(8,128)} %bitcast.19, bf16[512,896]{1,0:T(8,128)(2,1)} %bitcast.23, f32[896,512]{1,0:T(8,128)} %bitcast.26), custom_call_target="tpu_custom_call" | custom-call | tf_op jit(solution)/shard_map/front/pallas_call | solution.py:151
  4.6 0.0 copy-start.3
  4.6 23.9 %all_to_all.15.pieces = bf16[16,32,512]{2,1,0:T(8,128)(2,1)S(1)} all-to-all(bf16[16,32,512]{2,1,0:T(8,128)(2,1)} %bitcast.27), channel_id=1, replica_groups=mesh['y'=4,'c'=2,'x'=2,'z'=8,'r'=2] {'x','z'}, dimensions={0} | all-to-all | bytes 1048576 | tf_op jit(solution)/shard_map/all_to_all | solution.py:319
  28.5 0.1 spread.1
  28.6 18.8 %all_to_all.16 = bf16[16,32,512]{2,1,0:T(8,128)(2,1)S(1)} all-to-all(bf16[16,32,512]{2,1,0:T(8,128)(2,1)S(1)} %spread.1), channel_id=1, replica_groups=mesh['y'=4,'c'=2,'x'=2,'z'=8,'r'=2] {'x','z'}, dimensions={0} | all-to-all | bytes 1048576 | tf_op jit(solution)/shard_map/all_to_all | solution.py:319
  47.5 1.6 %pieces.1 = (f32[4,80,256]{2,1,0:T(8,128)S(1)}, f32[4,112,512]{2,1,0:T(8,128)S(1)}, bf16[4,192,512]{2,1,0:T(8,128)(2,1)S(1)}) custom-call(s32[3]{0:T(128)S(1)} %pad_add_fusion.place, bf16[512,512]{1,0:T(8,128)(2,1)S(1)} %bitcast.15, bf16[512,896]{1,0:T(8,128)(2,1)S(1)} %copy-done.3), custom_call_target="tpu_custom_call" | custom-call | tf_op jit(solution)/shard_map/pieces/pallas_call | solution.py:26
  49.0 3.2 %collective-permute-start = (bf16[4,192,512]{2,1,0:T(8,128)(2,1)S(1)}, bf16[4,192,512]{2,1,0:T(8,128)(2,1)S(1)}, u32[]{:S(2)}, u32[]{:S(2)}) collective-permute-start(bf16[4,192,512]{2,1,0:T(8,128)(2,1)S(1)} %get-tuple-element.39), channel_id=1, source_target_pairs={{0,32},{32,0},{1,33},{33,1},{2,34},{34,2},{3,35},{35,3},{4,36},{36... | collective-permute-start | bytes 2359304 | tf_op jit(solution)/shard_map/ppermute | solution.py:323
  52.2 0.1 slice_bitcast_fusion
  52.3 2.5 %collective-permute-start.8 = (bf16[384,896]{1,0:T(8,128)(2,1)S(1)}, bf16[384,896]{1,0:T(8,128)(2,1)S(1)}, u32[]{:S(2)}, u32[]{:S(2)}) collective-permute-start(bf16[384,896]{1,0:T(8,128)(2,1)S(1)} %slice_bitcast_fusion), channel_id=1, source_target_pairs={{0,1},{1,0},{2,3},{3,2},{4,5},{5,4},{6,7},{7,6},{8,9},{9,8},{10,11... | collective-permute-start | bytes 2064392 | tf_op jit(solution)/shard_map/ppermute | solution.py:323
  54.8 0.5 collective-permute-start.7
  55.4 0.7 join.1
  56.1 1.4 %collective-permute-start.1 = (bf16[192,512]{1,0:T(8,128)(2,1)S(1)}, bf16[192,512]{1,0:T(8,128)(2,1)S(1)}, u32[]{:S(2)}, u32[]{:S(2)}) collective-permute-start(bf16[192,512]{1,0:T(8,128)(2,1)S(1)} %get-tuple-element.42), channel_id=1, source_target_pairs={{0,64},{64,0},{128,192},{192,128},{1,65},{65,1},{129,193},{193,129... | collective-permute-start | bytes 589832 | tf_op jit(solution)/shard_map/ppermute | solution.py:323
  57.4 2.6 %collective-permute-start.2 = (bf16[192,512]{1,0:T(8,128)(2,1)S(1)}, bf16[192,512]{1,0:T(8,128)(2,1)S(1)}, u32[]{:S(2)}, u32[]{:S(2)}) collective-permute-start(bf16[192,512]{1,0:T(8,128)(2,1)S(1)} %get-tuple-element.43), channel_id=1, source_target_pairs={{0,128},{64,192},{128,0},{192,64},{1,129},{65,193},{129,1},{193,65... | collective-permute-start | bytes 589832 | tf_op jit(solution)/shard_map/ppermute | solution.py:323
  60.1 2.0 %collective-permute-done.1.one = bf16[192,512]{1,0:T(8,128)(2,1)S(1)} collective-permute-done((bf16[192,512]{1,0:T(8,128)(2,1)S(1)}, bf16[192,512]{1,0:T(8,128)(2,1)S(1)}, u32[]{:S(2)}, u32[]{:S(2)}) %collective-permute-start.1) | collective-permute-done | bytes 196640 | tf_op jit(solution)/shard_map/ppermute | solution.py:323
  62.0 6.7 %collective-permute-done.2.two = bf16[192,512]{1,0:T(8,128)(2,1)S(1)} collective-permute-done((bf16[192,512]{1,0:T(8,128)(2,1)S(1)}, bf16[192,512]{1,0:T(8,128)(2,1)S(1)}, u32[]{:S(2)}, u32[]{:S(2)}) %collective-permute-start.2) | collective-permute-done | bytes 196640 | tf_op jit(solution)/shard_map/ppermute | solution.py:323
  68.7 2.6 %collective-permute-done.3.three = bf16[192,512]{1,0:T(8,128)(2,1)S(1)} collective-permute-done((bf16[192,512]{1,0:T(8,128)(2,1)S(1)}, bf16[192,512]{1,0:T(8,128)(2,1)S(1)}, u32[]{:S(2)}, u32[]{:S(2)}) %collective-permute-start.3) | collective-permute-done | bytes 196640 | tf_op jit(solution)/shard_map/ppermute | solution.py:323
  71.3 0.1 sum.1.own
  71.4 0.1 collective-permute-start.6
  71.5 0.1 collective-permute-start.5
  71.6 3.1 %collective-permute-start.4 = (bf16[192,512]{1,0:T(8,128)(2,1)S(1)}, bf16[192,512]{1,0:T(8,128)(2,1)S(1)}, u32[]{:S(2)}, u32[]{:S(2)}) collective-permute-start(bf16[192,512]{1,0:T(8,128)(2,1)S(1)} %sum.1.own), channel_id=1, source_target_pairs={{0,64},{64,0},{128,192},{192,128},{1,65},{65,1},{129,193},{193,129... | collective-permute-start | bytes 589832 | tf_op jit(solution)/shard_map/ppermute | solution.py:323
  74.7 8.5 %collective-permute-done.6.three = bf16[192,512]{1,0:T(8,128)(2,1)S(1)} collective-permute-done((bf16[192,512]{1,0:T(8,128)(2,1)S(1)}, bf16[192,512]{1,0:T(8,128)(2,1)S(1)}, u32[]{:S(2)}, u32[]{:S(2)}) %collective-permute-start.6) | collective-permute-done | bytes 196640 | tf_op jit(solution)/shard_map/ppermute | solution.py:323
  83.3 0.6 line.1
  83.9 1.7 %collective-permute-start.9 = (bf16[4,192,512]{2,1,0:T(8,128)(2,1)S(1)}, bf16[4,192,512]{2,1,0:T(8,128)(2,1)S(1)}, u32[]{:S(2)}, u32[]{:S(2)}) collective-permute-start(bf16[4,192,512]{2,1,0:T(8,128)(2,1)S(1)} %get-tuple-element.48.own), channel_id=1, source_target_pairs={{0,32},{32,0},{1,33},{33,1},{2,34},{34,2},{3,35},{35,3},{4,36},{36... | collective-permute-start | bytes 2359304 | tf_op jit(solution)/shard_map/ppermute | solution.py:323
  85.6 2.5 %collective-permute-start.10 = (bf16[704,512]{1,0:T(8,128)(2,1)S(1)}, bf16[704,512]{1,0:T(8,128)(2,1)S(1)}, u32[]{:S(2)}, u32[]{:S(2)}) collective-permute-start(bf16[704,512]{1,0:T(8,128)(2,1)S(1)} %get-tuple-element.53), channel_id=1, source_target_pairs={{0,1},{1,0},{2,3},{3,2},{4,5},{5,4},{6,7},{7,6},{8,9},{9,8},{10,11... | collective-permute-start | bytes 2162696 | tf_op jit(solution)/shard_map/ppermute | solution.py:323
  88.1 0.6 rows.1.right_in.raw0
  88.7 0.0 copy-start
  88.7 19.0 %solve.1 = (bf16[384,512]{1,0:T(8,128)(2,1)S(1)}, bf16[512,512]{1,0:T(8,128)(2,1)S(1)}, f32[896,512]{1,0:T(8,128)S(1)}, f32[1,512]{1,0:T(1,128)S(1)}) custom-call(s32[3]{0:T(128)S(1)} %pad_add_fusion.place, bf16[4,192,512]{2,1,0:T(8,128)(2,1)S(1)} %get-tuple-element.48.own, bf16[4,192,512]{2,1,0:T(8,128)(2,1)S(1)} %collective-permute-done.9.got, ...), custom_call_target="tpu_custom_call" | custom-call | tf_op jit(solution)/shard_map/solve/pallas_call | solution.py:26
  107.7 0.6 collective-permute-start.12
  108.3 1.7 %collective-permute-start.11 = (bf16[384,512]{1,0:T(8,128)(2,1)S(1)}, bf16[384,512]{1,0:T(8,128)(2,1)S(1)}, u32[]{:S(2)}, u32[]{:S(2)}) collective-permute-start(bf16[384,512]{1,0:T(8,128)(2,1)S(1)} %get-tuple-element.54.w0), channel_id=1, source_target_pairs={{0,1},{1,0},{2,3},{3,2},{4,5},{5,4},{6,7},{7,6},{8,9},{9,8},{10,11... | collective-permute-start | bytes 1179656 | tf_op jit(solution)/shard_map/ppermute | solution.py:323
  110.1 14.3 %all_to_all.17.sums = f32[32,1,512]{2,1,0:T(1,128)S(1)} all-to-all(f32[32,1,512]{2,1,0:T(1,128)S(1)} %broadcast_in_dim.18), channel_id=1, replica_groups=mesh['y'=4,'c'=2,'x'=2,'z'=8,'r'=2] {'x','z','r'}, dimensions={0} | all-to-all | bytes 131072 | tf_op jit(solution)/shard_map/all_to_all | solution.py:319
  124.4 6.4 %last.1 = (bf16[512,896]{1,0:T(8,128)(2,1)}, f32[512,896]{1,0:T(8,128)}, f32[896,512]{1,0:T(8,128)}, bf16[2,512,896]{2,1,0:T(8,128)(2,1)}) custom-call(s32[3]{0:T(128)S(1)} %pad_add_fusion.place, f32[32,1,512]{2,1,0:T(1,128)S(1)} %all_to_all.17.sums, f32[512,896]{1,0:T(8,128)S(1)} %bitcast.20, bf16[512,896]{1,0:T(8,128)(2,1)S(1)} %bitcast.24, ...), custom_call_target="tpu_custom_call" | custom-call | tf_op jit(solution)/shard_map/last/pallas_call | solution.py:26
  (17 shorter events, 0.1 us)
Async XLA Ops:
  4.6 42.9 %copy-start.3 = (bf16[512,896]{1,0:T(8,128)(2,1)S(1)}, bf16[512,896]{1,0:T(8,128)(2,1)}, u32[]{:S(2)}) copy-start(bf16[512,896]{1,0:T(8,128)(2,1)} %get-tuple-element.36.blend_ref) | copy-start | bytes 2752516
  28.5 23.7 %copy-start.1 = (bf16[1,512,896]{2,1,0:T(8,128)(2,1)S(1)}, bf16[1,512,896]{2,1,0:T(8,128)(2,1)}, u32[]{:S(2)}) copy-start(bf16[1,512,896]{2,1,0:T(8,128)(2,1)} %param.4) | copy-start | bytes 2752516
  49.0 6.3 %collective-permute-start = (bf16[4,192,512]{2,1,0:T(8,128)(2,1)S(1)}, bf16[4,192,512]{2,1,0:T(8,128)(2,1)S(1)}, u32[]{:S(2)}, u32[]{:S(2)}) collective-permute-start(bf16[4,192,512]{2,1,0:T(8,128)(2,1)S(1)} %get-tuple-element.39), channel_id=1, source_target_pairs={{0,32},{32,0},{1,33},{33,1},{2,34},{34,2},{3,35},{35,3},{4,36},{36... | collective-permute-start | bytes 2359304 | tf_op jit(solution)/shard_map/ppermute | solution.py:323
  52.3 31.6 %collective-permute-start.8 = (bf16[384,896]{1,0:T(8,128)(2,1)S(1)}, bf16[384,896]{1,0:T(8,128)(2,1)S(1)}, u32[]{:S(2)}, u32[]{:S(2)}) collective-permute-start(bf16[384,896]{1,0:T(8,128)(2,1)S(1)} %slice_bitcast_fusion), channel_id=1, source_target_pairs={{0,1},{1,0},{2,3},{3,2},{4,5},{5,4},{6,7},{7,6},{8,9},{9,8},{10,11... | collective-permute-start | bytes 2064392 | tf_op jit(solution)/shard_map/ppermute | solution.py:323
  54.8 29.1 %collective-permute-start.7 = (bf16[512,512]{1,0:T(8,128)(2,1)S(1)}, bf16[512,512]{1,0:T(8,128)(2,1)S(1)}, u32[]{:S(2)}, u32[]{:S(2)}) collective-permute-start(bf16[512,512]{1,0:T(8,128)(2,1)S(1)} %bitcast.16), channel_id=1, source_target_pairs={{0,1},{1,0},{2,3},{3,2},{4,5},{5,4},{6,7},{7,6},{8,9},{9,8},{10,11... | collective-permute-start | bytes 1572872 | tf_op jit(solution)/shard_map/ppermute | solution.py:323
  56.1 6.0 %collective-permute-start.1 = (bf16[192,512]{1,0:T(8,128)(2,1)S(1)}, bf16[192,512]{1,0:T(8,128)(2,1)S(1)}, u32[]{:S(2)}, u32[]{:S(2)}) collective-permute-start(bf16[192,512]{1,0:T(8,128)(2,1)S(1)} %get-tuple-element.42), channel_id=1, source_target_pairs={{0,64},{64,0},{128,192},{192,128},{1,65},{65,1},{129,193},{193,129... | collective-permute-start | bytes 589832 | tf_op jit(solution)/shard_map/ppermute | solution.py:323
  57.4 11.3 %collective-permute-start.2 = (bf16[192,512]{1,0:T(8,128)(2,1)S(1)}, bf16[192,512]{1,0:T(8,128)(2,1)S(1)}, u32[]{:S(2)}, u32[]{:S(2)}) collective-permute-start(bf16[192,512]{1,0:T(8,128)(2,1)S(1)} %get-tuple-element.43), channel_id=1, source_target_pairs={{0,128},{64,192},{128,0},{192,64},{1,129},{65,193},{129,1},{193,65... | collective-permute-start | bytes 589832 | tf_op jit(solution)/shard_map/ppermute | solution.py:323
  60.0 11.2 %collective-permute-start.3 = (bf16[192,512]{1,0:T(8,128)(2,1)S(1)}, bf16[192,512]{1,0:T(8,128)(2,1)S(1)}, u32[]{:S(2)}, u32[]{:S(2)}) collective-permute-start(bf16[192,512]{1,0:T(8,128)(2,1)S(1)} %get-tuple-element.44), channel_id=1, source_target_pairs={{0,192},{64,128},{128,64},{192,0},{1,193},{65,129},{129,65},{193,1... | collective-permute-start | bytes 589832 | tf_op jit(solution)/shard_map/ppermute | solution.py:323
  71.4 11.9 %collective-permute-start.6 = (bf16[192,512]{1,0:T(8,128)(2,1)S(1)}, bf16[192,512]{1,0:T(8,128)(2,1)S(1)}, u32[]{:S(2)}, u32[]{:S(2)}) collective-permute-start(bf16[192,512]{1,0:T(8,128)(2,1)S(1)} %sum.1.own), channel_id=1, source_target_pairs={{0,192},{64,128},{128,64},{192,0},{1,193},{65,129},{129,65},{193,1... | collective-permute-start | bytes 589832 | tf_op jit(solution)/shard_map/ppermute | solution.py:323
  71.5 11.7 %collective-permute-start.5 = (bf16[192,512]{1,0:T(8,128)(2,1)S(1)}, bf16[192,512]{1,0:T(8,128)(2,1)S(1)}, u32[]{:S(2)}, u32[]{:S(2)}) collective-permute-start(bf16[192,512]{1,0:T(8,128)(2,1)S(1)} %sum.1.own), channel_id=1, source_target_pairs={{0,128},{64,192},{128,0},{192,64},{1,129},{65,193},{129,1},{193,65... | collective-permute-start | bytes 589832 | tf_op jit(solution)/shard_map/ppermute | solution.py:323
  71.6 11.7 %collective-permute-start.4 = (bf16[192,512]{1,0:T(8,128)(2,1)S(1)}, bf16[192,512]{1,0:T(8,128)(2,1)S(1)}, u32[]{:S(2)}, u32[]{:S(2)}) collective-permute-start(bf16[192,512]{1,0:T(8,128)(2,1)S(1)} %sum.1.own), channel_id=1, source_target_pairs={{0,64},{64,0},{128,192},{192,128},{1,65},{65,1},{129,193},{193,129... | collective-permute-start | bytes 589832 | tf_op jit(solution)/shard_map/ppermute | solution.py:323
  83.9 4.1 %collective-permute-start.9 = (bf16[4,192,512]{2,1,0:T(8,128)(2,1)S(1)}, bf16[4,192,512]{2,1,0:T(8,128)(2,1)S(1)}, u32[]{:S(2)}, u32[]{:S(2)}) collective-permute-start(bf16[4,192,512]{2,1,0:T(8,128)(2,1)S(1)} %get-tuple-element.48.own), channel_id=1, source_target_pairs={{0,32},{32,0},{1,33},{33,1},{2,34},{34,2},{3,35},{35,3},{4,36},{36... | collective-permute-start | bytes 2359304 | tf_op jit(solution)/shard_map/ppermute | solution.py:323
  85.6 22.1 %collective-permute-start.10 = (bf16[704,512]{1,0:T(8,128)(2,1)S(1)}, bf16[704,512]{1,0:T(8,128)(2,1)S(1)}, u32[]{:S(2)}, u32[]{:S(2)}) collective-permute-start(bf16[704,512]{1,0:T(8,128)(2,1)S(1)} %get-tuple-element.53), channel_id=1, source_target_pairs={{0,1},{1,0},{2,3},{3,2},{4,5},{5,4},{6,7},{7,6},{8,9},{9,8},{10,11... | collective-permute-start | bytes 2162696 | tf_op jit(solution)/shard_map/ppermute | solution.py:323
  88.7 35.8 %copy-start = (f32[1,512,896]{2,1,0:T(8,128)S(1)}, f32[1,512,896]{2,1,0:T(8,128)}, u32[]{:S(2)}) copy-start(f32[1,512,896]{2,1,0:T(8,128)} %param.6) | copy-start | bytes 5505028
  88.7 35.8 %copy-start.2 = (bf16[1,512,896]{2,1,0:T(8,128)(2,1)S(1)}, bf16[1,512,896]{2,1,0:T(8,128)(2,1)}, u32[]{:S(2)}) copy-start(bf16[1,512,896]{2,1,0:T(8,128)(2,1)} %param.5) | copy-start | bytes 2752516
  107.7 16.8 %collective-permute-start.12 = (bf16[704,512]{1,0:T(8,128)(2,1)S(1)}, bf16[704,512]{1,0:T(8,128)(2,1)S(1)}, u32[]{:S(2)}, u32[]{:S(2)}) collective-permute-start(bf16[704,512]{1,0:T(8,128)(2,1)S(1)} %collective-permute-done.10.half1), channel_id=1, source_target_pairs={{0,32},{32,0},{1,33},{33,1},{2,34},{34,2},{3,35},{35,3},{4,36},{36... | collective-permute-start | bytes 2162696 | tf_op jit(solution)/shard_map/ppermute | solution.py:323
  108.3 16.1 %collective-permute-start.11 = (bf16[384,512]{1,0:T(8,128)(2,1)S(1)}, bf16[384,512]{1,0:T(8,128)(2,1)S(1)}, u32[]{:S(2)}, u32[]{:S(2)}) collective-permute-start(bf16[384,512]{1,0:T(8,128)(2,1)S(1)} %get-tuple-element.54.w0), channel_id=1, source_target_pairs={{0,1},{1,0},{2,3},{3,2},{4,5},{5,4},{6,7},{7,6},{8,9},{9,8},{10,11... | collective-permute-start | bytes 1179656 | tf_op jit(solution)/shard_map/ppermute | solution.py:323

commit v10 on v9

--- a/solution.py
+++ b/solution.py
@@ -16,7 +16,7 @@
 GRP = 8
 GR = 80
 RR = 112
-EARLY = 384
+EARLY = 320
 VMEM = pl.BlockSpec(memory_space=pltpu.VMEM)
 SMEM = pl.BlockSpec(memory_space=pltpu.SMEM)
 

time: 131 us -> 133 us (1.015)
  waiting for transfers between devices: 19.8 us -> 21.7 us
    ppermute x13, waiting for transfers between devices: 19.8 us -> 21.7 us  [swap(): lax.ppermute(x, axis, [(i, i ^ bit) for i in range(lax.axis_size(axis))])]
  transfers between devices with their start and end apart: 13 -> 13, of which waited for: 4 -> 5; matrix products, arithmetic and copies ran while one was open for 0% -> 0% of each run, Pallas kernels for 16% -> 16%
where the time goes in v10:
time: 133 us
  blocking collectives  58.3 us (44%)
  Pallas kernels  32.9 us (25%)
  waiting for transfers between devices  21.7 us (16%)
  starting transfers between devices  18.9 us (14%)
    all_to_all x3, blocking collectives, exchange(): return lax.all_to_all(x, axis, 0, 0, tiled=True)  58.3 us
    pallas_call x8, Pallas kernels, run(): pl.pallas_call(kernel, out_shape=[jax.ShapeDtypeStruct(s, d) for s, d in...  29 us
    ppermute x13, waiting for transfers between devices, swap(): lax.ppermute(x, axis, [(i, i ^ bit) for i in range(lax.axis_size(axis))])  21.7 us
    ppermute x13, starting transfers between devices, swap(): lax.ppermute(x, axis, [(i, i ^ bit) for i in range(lax.axis_size(axis))])  18.9 us
    pallas_call x1, Pallas kernels, front(): pl.pallas_call(front_kernel, out_shape=[jax.ShapeDtypeStruct((rows, N), B...  3.87 us
  transfers between devices with their start and end apart: 13, of which 5 were waited for; matrix products, arithmetic and copies ran while one was open for 0% of the time, Pallas kernels for 16%

profile of v10, /device:TPU:1, one launch (start us, length us, event | category | flops | bytes accessed | tf_op | source)
XLA Modules:
  0.0 133.0 jit_solution(11056426116982821351)
XLA Ops:
  0.6 0.1 pad_add_fusion.place
  0.7 3.9 %front.1 = (bf16[512,512]{1,0:T(8,128)(2,1)}, bf16[512,896]{1,0:T(8,128)(2,1)}) custom-call(f32[512,896]{1,0:T(8,128)} %bitcast.19, bf16[512,896]{1,0:T(8,128)(2,1)} %bitcast.23, f32[896,512]{1,0:T(8,128)} %bitcast.26), custom_call_target="tpu_custom_call" | custom-call | tf_op jit(solution)/shard_map/front/pallas_call | solution.py:151
  4.6 0.0 copy-start.3
  4.6 23.9 %all_to_all.15.pieces = bf16[16,32,512]{2,1,0:T(8,128)(2,1)S(1)} all-to-all(bf16[16,32,512]{2,1,0:T(8,128)(2,1)} %bitcast.27), channel_id=1, replica_groups=mesh['y'=4,'c'=2,'x'=2,'z'=8,'r'=2] {'x','z'}, dimensions={0} | all-to-all | bytes 1048576 | tf_op jit(solution)/shard_map/all_to_all | solution.py:319
  28.5 0.1 spread.1
  28.6 18.8 %all_to_all.16 = bf16[16,32,512]{2,1,0:T(8,128)(2,1)S(1)} all-to-all(bf16[16,32,512]{2,1,0:T(8,128)(2,1)S(1)} %spread.1), channel_id=1, replica_groups=mesh['y'=4,'c'=2,'x'=2,'z'=8,'r'=2] {'x','z'}, dimensions={0} | all-to-all | bytes 1048576 | tf_op jit(solution)/shard_map/all_to_all | solution.py:319
  47.5 1.6 %pieces.1 = (f32[4,80,256]{2,1,0:T(8,128)S(1)}, f32[4,112,512]{2,1,0:T(8,128)S(1)}, bf16[4,192,512]{2,1,0:T(8,128)(2,1)S(1)}) custom-call(s32[3]{0:T(128)S(1)} %pad_add_fusion.place, bf16[512,512]{1,0:T(8,128)(2,1)S(1)} %bitcast.15, bf16[512,896]{1,0:T(8,128)(2,1)S(1)} %copy-done.3), custom_call_target="tpu_custom_call" | custom-call | tf_op jit(solution)/shard_map/pieces/pallas_call | solution.py:26
  49.0 3.2 %collective-permute-start = (bf16[4,192,512]{2,1,0:T(8,128)(2,1)S(1)}, bf16[4,192,512]{2,1,0:T(8,128)(2,1)S(1)}, u32[]{:S(2)}, u32[]{:S(2)}) collective-permute-start(bf16[4,192,512]{2,1,0:T(8,128)(2,1)S(1)} %get-tuple-element.39), channel_id=1, source_target_pairs={{0,32},{32,0},{1,33},{33,1},{2,34},{34,2},{3,35},{35,3},{4,36},{36... | collective-permute-start | bytes 2359304 | tf_op jit(solution)/shard_map/ppermute | solution.py:323
  52.3 2.5 %collective-permute-start.8 = (bf16[320,896]{1,0:T(8,128)(2,1)S(1)}, bf16[320,896]{1,0:T(8,128)(2,1)S(1)}, u32[]{:S(2)}, u32[]{:S(2)}) collective-permute-start(bf16[320,896]{1,0:T(8,128)(2,1)S(1)} %slice_bitcast_fusion), channel_id=1, source_target_pairs={{0,1},{1,0},{2,3},{3,2},{4,5},{5,4},{6,7},{7,6},{8,9},{9,8},{10,11... | collective-permute-start | bytes 1720328 | tf_op jit(solution)/shard_map/ppermute | solution.py:323
  54.8 0.5 collective-permute-start.7
  55.3 0.7 join.1
  56.0 1.4 %collective-permute-start.1 = (bf16[192,512]{1,0:T(8,128)(2,1)S(1)}, bf16[192,512]{1,0:T(8,128)(2,1)S(1)}, u32[]{:S(2)}, u32[]{:S(2)}) collective-permute-start(bf16[192,512]{1,0:T(8,128)(2,1)S(1)} %get-tuple-element.42), channel_id=1, source_target_pairs={{0,64},{64,0},{128,192},{192,128},{1,65},{65,1},{129,193},{193,129... | collective-permute-start | bytes 589832 | tf_op jit(solution)/shard_map/ppermute | solution.py:323
  57.4 2.6 %collective-permute-start.2 = (bf16[192,512]{1,0:T(8,128)(2,1)S(1)}, bf16[192,512]{1,0:T(8,128)(2,1)S(1)}, u32[]{:S(2)}, u32[]{:S(2)}) collective-permute-start(bf16[192,512]{1,0:T(8,128)(2,1)S(1)} %get-tuple-element.43), channel_id=1, source_target_pairs={{0,128},{64,192},{128,0},{192,64},{1,129},{65,193},{129,1},{193,65... | collective-permute-start | bytes 589832 | tf_op jit(solution)/shard_map/ppermute | solution.py:323
  60.0 2.0 %collective-permute-done.1.one = bf16[192,512]{1,0:T(8,128)(2,1)S(1)} collective-permute-done((bf16[192,512]{1,0:T(8,128)(2,1)S(1)}, bf16[192,512]{1,0:T(8,128)(2,1)S(1)}, u32[]{:S(2)}, u32[]{:S(2)}) %collective-permute-start.1) | collective-permute-done | bytes 196640 | tf_op jit(solution)/shard_map/ppermute | solution.py:323
  62.0 6.7 %collective-permute-done.2.two = bf16[192,512]{1,0:T(8,128)(2,1)S(1)} collective-permute-done((bf16[192,512]{1,0:T(8,128)(2,1)S(1)}, bf16[192,512]{1,0:T(8,128)(2,1)S(1)}, u32[]{:S(2)}, u32[]{:S(2)}) %collective-permute-start.2) | collective-permute-done | bytes 196640 | tf_op jit(solution)/shard_map/ppermute | solution.py:323
  68.7 2.6 %collective-permute-done.3.three = bf16[192,512]{1,0:T(8,128)(2,1)S(1)} collective-permute-done((bf16[192,512]{1,0:T(8,128)(2,1)S(1)}, bf16[192,512]{1,0:T(8,128)(2,1)S(1)}, u32[]{:S(2)}, u32[]{:S(2)}) %collective-permute-start.3) | collective-permute-done | bytes 196640 | tf_op jit(solution)/shard_map/ppermute | solution.py:323
  71.3 0.1 sum.1.own
  71.4 0.1 collective-permute-start.6
  71.5 0.1 collective-permute-start.5
  71.6 3.1 %collective-permute-start.4 = (bf16[192,512]{1,0:T(8,128)(2,1)S(1)}, bf16[192,512]{1,0:T(8,128)(2,1)S(1)}, u32[]{:S(2)}, u32[]{:S(2)}) collective-permute-start(bf16[192,512]{1,0:T(8,128)(2,1)S(1)} %sum.1.own), channel_id=1, source_target_pairs={{0,64},{64,0},{128,192},{192,128},{1,65},{65,1},{129,193},{193,129... | collective-permute-start | bytes 589832 | tf_op jit(solution)/shard_map/ppermute | solution.py:323
  74.7 8.5 %collective-permute-done.6.three = bf16[192,512]{1,0:T(8,128)(2,1)S(1)} collective-permute-done((bf16[192,512]{1,0:T(8,128)(2,1)S(1)}, bf16[192,512]{1,0:T(8,128)(2,1)S(1)}, u32[]{:S(2)}, u32[]{:S(2)}) %collective-permute-start.6) | collective-permute-done | bytes 196640 | tf_op jit(solution)/shard_map/ppermute | solution.py:323
  83.3 0.7 line.1
  83.9 2.5 %collective-permute-start.10 = (bf16[832,512]{1,0:T(8,128)(2,1)S(1)}, bf16[832,512]{1,0:T(8,128)(2,1)S(1)}, u32[]{:S(2)}, u32[]{:S(2)}) collective-permute-start(bf16[832,512]{1,0:T(8,128)(2,1)S(1)} %get-tuple-element.53), channel_id=1, source_target_pairs={{0,1},{1,0},{2,3},{3,2},{4,5},{5,4},{6,7},{7,6},{8,9},{9,8},{10,11... | collective-permute-start | bytes 2555912 | tf_op jit(solution)/shard_map/ppermute | solution.py:323
  86.5 1.8 %collective-permute-start.9 = (bf16[4,192,512]{2,1,0:T(8,128)(2,1)S(1)}, bf16[4,192,512]{2,1,0:T(8,128)(2,1)S(1)}, u32[]{:S(2)}, u32[]{:S(2)}) collective-permute-start(bf16[4,192,512]{2,1,0:T(8,128)(2,1)S(1)} %get-tuple-element.48.own), channel_id=1, source_target_pairs={{0,32},{32,0},{1,33},{33,1},{2,34},{34,2},{3,35},{35,3},{4,36},{36... | collective-permute-start | bytes 2359304 | tf_op jit(solution)/shard_map/ppermute | solution.py:323
  88.3 1.9 %collective-permute-done.9.got = bf16[4,192,512]{2,1,0:T(8,128)(2,1)S(1)} collective-permute-done((bf16[4,192,512]{2,1,0:T(8,128)(2,1)S(1)}, bf16[4,192,512]{2,1,0:T(8,128)(2,1)S(1)}, u32[]{:S(2)}, u32[]{:S(2)}) %collective-permute-start.9) | collective-permute-done | bytes 786464 | tf_op jit(solution)/shard_map/ppermute | solution.py:323
  90.2 0.6 rows.1.right_in.raw0
  90.9 0.0 copy-start
  90.9 19.0 %solve.1 = (bf16[384,512]{1,0:T(8,128)(2,1)S(1)}, bf16[512,512]{1,0:T(8,128)(2,1)S(1)}, f32[896,512]{1,0:T(8,128)S(1)}, f32[1,512]{1,0:T(1,128)S(1)}) custom-call(s32[3]{0:T(128)S(1)} %pad_add_fusion.place, bf16[4,192,512]{2,1,0:T(8,128)(2,1)S(1)} %get-tuple-element.48.own, bf16[4,192,512]{2,1,0:T(8,128)(2,1)S(1)} %collective-permute-done.9.got, ...), custom_call_target="tpu_custom_call" | custom-call | tf_op jit(solution)/shard_map/solve/pallas_call | solution.py:26
  109.9 0.5 collective-permute-start.12
  110.3 0.5 collective-permute-start.11
  110.9 15.6 %all_to_all.17.sums = f32[32,1,512]{2,1,0:T(1,128)S(1)} all-to-all(f32[32,1,512]{2,1,0:T(1,128)S(1)} %broadcast_in_dim.18), channel_id=1, replica_groups=mesh['y'=4,'c'=2,'x'=2,'z'=8,'r'=2] {'x','z','r'}, dimensions={0} | all-to-all | bytes 131072 | tf_op jit(solution)/shard_map/all_to_all | solution.py:319
  126.5 6.4 %last.1 = (bf16[512,896]{1,0:T(8,128)(2,1)}, f32[512,896]{1,0:T(8,128)}, f32[896,512]{1,0:T(8,128)}, bf16[2,512,896]{2,1,0:T(8,128)(2,1)}) custom-call(s32[3]{0:T(128)S(1)} %pad_add_fusion.place, f32[32,1,512]{2,1,0:T(1,128)S(1)} %all_to_all.17.sums, f32[512,896]{1,0:T(8,128)S(1)} %bitcast.20, bf16[512,896]{1,0:T(8,128)(2,1)S(1)} %bitcast.24, ...), custom_call_target="tpu_custom_call" | custom-call | tf_op jit(solution)/shard_map/last/pallas_call | solution.py:26
  (17 shorter events, 0.1 us)
Async XLA Ops:
  4.6 42.9 %copy-start.3 = (bf16[512,896]{1,0:T(8,128)(2,1)S(1)}, bf16[512,896]{1,0:T(8,128)(2,1)}, u32[]{:S(2)}) copy-start(bf16[512,896]{1,0:T(8,128)(2,1)} %get-tuple-element.36.blend_ref) | copy-start | bytes 2752516
  28.5 23.7 %copy-start.1 = (bf16[1,512,896]{2,1,0:T(8,128)(2,1)S(1)}, bf16[1,512,896]{2,1,0:T(8,128)(2,1)}, u32[]{:S(2)}) copy-start(bf16[1,512,896]{2,1,0:T(8,128)(2,1)} %param.4) | copy-start | bytes 2752516
  49.0 6.3 %collective-permute-start = (bf16[4,192,512]{2,1,0:T(8,128)(2,1)S(1)}, bf16[4,192,512]{2,1,0:T(8,128)(2,1)S(1)}, u32[]{:S(2)}, u32[]{:S(2)}) collective-permute-start(bf16[4,192,512]{2,1,0:T(8,128)(2,1)S(1)} %get-tuple-element.39), channel_id=1, source_target_pairs={{0,32},{32,0},{1,33},{33,1},{2,34},{34,2},{3,35},{35,3},{4,36},{36... | collective-permute-start | bytes 2359304 | tf_op jit(solution)/shard_map/ppermute | solution.py:323
  52.3 31.6 %collective-permute-start.8 = (bf16[320,896]{1,0:T(8,128)(2,1)S(1)}, bf16[320,896]{1,0:T(8,128)(2,1)S(1)}, u32[]{:S(2)}, u32[]{:S(2)}) collective-permute-start(bf16[320,896]{1,0:T(8,128)(2,1)S(1)} %slice_bitcast_fusion), channel_id=1, source_target_pairs={{0,1},{1,0},{2,3},{3,2},{4,5},{5,4},{6,7},{7,6},{8,9},{9,8},{10,11... | collective-permute-start | bytes 1720328 | tf_op jit(solution)/shard_map/ppermute | solution.py:323
  54.8 29.1 %collective-permute-start.7 = (bf16[512,512]{1,0:T(8,128)(2,1)S(1)}, bf16[512,512]{1,0:T(8,128)(2,1)S(1)}, u32[]{:S(2)}, u32[]{:S(2)}) collective-permute-start(bf16[512,512]{1,0:T(8,128)(2,1)S(1)} %bitcast.16), channel_id=1, source_target_pairs={{0,1},{1,0},{2,3},{3,2},{4,5},{5,4},{6,7},{7,6},{8,9},{9,8},{10,11... | collective-permute-start | bytes 1572872 | tf_op jit(solution)/shard_map/ppermute | solution.py:323
  56.0 6.0 %collective-permute-start.1 = (bf16[192,512]{1,0:T(8,128)(2,1)S(1)}, bf16[192,512]{1,0:T(8,128)(2,1)S(1)}, u32[]{:S(2)}, u32[]{:S(2)}) collective-permute-start(bf16[192,512]{1,0:T(8,128)(2,1)S(1)} %get-tuple-element.42), channel_id=1, source_target_pairs={{0,64},{64,0},{128,192},{192,128},{1,65},{65,1},{129,193},{193,129... | collective-permute-start | bytes 589832 | tf_op jit(solution)/shard_map/ppermute | solution.py:323
  57.4 11.3 %collective-permute-start.2 = (bf16[192,512]{1,0:T(8,128)(2,1)S(1)}, bf16[192,512]{1,0:T(8,128)(2,1)S(1)}, u32[]{:S(2)}, u32[]{:S(2)}) collective-permute-start(bf16[192,512]{1,0:T(8,128)(2,1)S(1)} %get-tuple-element.43), channel_id=1, source_target_pairs={{0,128},{64,192},{128,0},{192,64},{1,129},{65,193},{129,1},{193,65... | collective-permute-start | bytes 589832 | tf_op jit(solution)/shard_map/ppermute | solution.py:323
  60.0 11.2 %collective-permute-start.3 = (bf16[192,512]{1,0:T(8,128)(2,1)S(1)}, bf16[192,512]{1,0:T(8,128)(2,1)S(1)}, u32[]{:S(2)}, u32[]{:S(2)}) collective-permute-start(bf16[192,512]{1,0:T(8,128)(2,1)S(1)} %get-tuple-element.44), channel_id=1, source_target_pairs={{0,192},{64,128},{128,64},{192,0},{1,193},{65,129},{129,65},{193,1... | collective-permute-start | bytes 589832 | tf_op jit(solution)/shard_map/ppermute | solution.py:323
  71.4 11.9 %collective-permute-start.6 = (bf16[192,512]{1,0:T(8,128)(2,1)S(1)}, bf16[192,512]{1,0:T(8,128)(2,1)S(1)}, u32[]{:S(2)}, u32[]{:S(2)}) collective-permute-start(bf16[192,512]{1,0:T(8,128)(2,1)S(1)} %sum.1.own), channel_id=1, source_target_pairs={{0,192},{64,128},{128,64},{192,0},{1,193},{65,129},{129,65},{193,1... | collective-permute-start | bytes 589832 | tf_op jit(solution)/shard_map/ppermute | solution.py:323
  71.5 11.7 %collective-permute-start.5 = (bf16[192,512]{1,0:T(8,128)(2,1)S(1)}, bf16[192,512]{1,0:T(8,128)(2,1)S(1)}, u32[]{:S(2)}, u32[]{:S(2)}) collective-permute-start(bf16[192,512]{1,0:T(8,128)(2,1)S(1)} %sum.1.own), channel_id=1, source_target_pairs={{0,128},{64,192},{128,0},{192,64},{1,129},{65,193},{129,1},{193,65... | collective-permute-start | bytes 589832 | tf_op jit(solution)/shard_map/ppermute | solution.py:323
  71.6 11.7 %collective-permute-start.4 = (bf16[192,512]{1,0:T(8,128)(2,1)S(1)}, bf16[192,512]{1,0:T(8,128)(2,1)S(1)}, u32[]{:S(2)}, u32[]{:S(2)}) collective-permute-start(bf16[192,512]{1,0:T(8,128)(2,1)S(1)} %sum.1.own), channel_id=1, source_target_pairs={{0,64},{64,0},{128,192},{192,128},{1,65},{65,1},{129,193},{193,129... | collective-permute-start | bytes 589832 | tf_op jit(solution)/shard_map/ppermute | solution.py:323
  83.9 25.9 %collective-permute-start.10 = (bf16[832,512]{1,0:T(8,128)(2,1)S(1)}, bf16[832,512]{1,0:T(8,128)(2,1)S(1)}, u32[]{:S(2)}, u32[]{:S(2)}) collective-permute-start(bf16[832,512]{1,0:T(8,128)(2,1)S(1)} %get-tuple-element.53), channel_id=1, source_target_pairs={{0,1},{1,0},{2,3},{3,2},{4,5},{5,4},{6,7},{7,6},{8,9},{9,8},{10,11... | collective-permute-start | bytes 2555912 | tf_op jit(solution)/shard_map/ppermute | solution.py:323
  86.5 3.8 %collective-permute-start.9 = (bf16[4,192,512]{2,1,0:T(8,128)(2,1)S(1)}, bf16[4,192,512]{2,1,0:T(8,128)(2,1)S(1)}, u32[]{:S(2)}, u32[]{:S(2)}) collective-permute-start(bf16[4,192,512]{2,1,0:T(8,128)(2,1)S(1)} %get-tuple-element.48.own), channel_id=1, source_target_pairs={{0,32},{32,0},{1,33},{33,1},{2,34},{34,2},{3,35},{35,3},{4,36},{36... | collective-permute-start | bytes 2359304 | tf_op jit(solution)/shard_map/ppermute | solution.py:323
  90.9 35.6 %copy-start = (f32[1,512,896]{2,1,0:T(8,128)S(1)}, f32[1,512,896]{2,1,0:T(8,128)}, u32[]{:S(2)}) copy-start(f32[1,512,896]{2,1,0:T(8,128)} %param.6) | copy-start | bytes 5505028
  90.9 35.6 %copy-start.2 = (bf16[1,512,896]{2,1,0:T(8,128)(2,1)S(1)}, bf16[1,512,896]{2,1,0:T(8,128)(2,1)}, u32[]{:S(2)}) copy-start(bf16[1,512,896]{2,1,0:T(8,128)(2,1)} %param.5) | copy-start | bytes 2752516
  109.9 16.6 %collective-permute-start.12 = (bf16[832,512]{1,0:T(8,128)(2,1)S(1)}, bf16[832,512]{1,0:T(8,128)(2,1)S(1)}, u32[]{:S(2)}, u32[]{:S(2)}) collective-permute-start(bf16[832,512]{1,0:T(8,128)(2,1)S(1)} %collective-permute-done.10.half1), channel_id=1, source_target_pairs={{0,32},{32,0},{1,33},{33,1},{2,34},{34,2},{3,35},{35,3},{4,36},{36... | collective-permute-start | bytes 2555912 | tf_op jit(solution)/shard_map/ppermute | solution.py:323
  110.3 16.1 %collective-permute-start.11 = (bf16[384,512]{1,0:T(8,128)(2,1)S(1)}, bf16[384,512]{1,0:T(8,128)(2,1)S(1)}, u32[]{:S(2)}, u32[]{:S(2)}) collective-permute-start(bf16[384,512]{1,0:T(8,128)(2,1)S(1)} %get-tuple-element.54.w0), channel_id=1, source_target_pairs={{0,1},{1,0},{2,3},{3,2},{4,5},{5,4},{6,7},{7,6},{8,9},{9,8},{10,11... | collective-permute-start | bytes 1179656 | tf_op jit(solution)/shard_map/ppermute | solution.py:323
